TPU v7x, 32 devices: a whole 2x2x4 slice. The times are simulated.
32 devices in a mesh: dp: 16 (over z, x, core), seq: 2 (over y).
Axes of the slice: x: 2, y: 2, z: 4, core: 2. Of those that a mesh axis runs over, the one named last changes fastest.
Arguments:
- tokens: bfloat16 [32, 1024, 768], P('dp', 'seq'), may hold values from -6 to 6
- segments: int32 [32, 1024], P('dp', 'seq'), may hold values from 0 to 7, as said below
- cotangent: bfloat16 [32, 1024, 768], P('dp', 'seq'), may hold values from -21 to 21
- gain_attn: float32 [768], replicated, may hold values from 0.25 to 1.75
- w_qkv: bfloat16 [768, 2304], replicated, may hold values from -0.21875 to 0.21875
- w_out: bfloat16 [768, 768], replicated, may hold values from -2.5 to 2.5
- gain_ffn: float32 [768], replicated, may hold values from 0.25 to 1.75
- w_up: bfloat16 [768, 3072], replicated, may hold values from -0.21875 to 0.21875
- w_down: bfloat16 [3072, 768], replicated, may hold values from -0.109375 to 0.109375
Outputs:
- outputs: bfloat16 [32, 1024, 768], P('dp', 'seq')
- grad_tokens: bfloat16 [32, 1024, 768], P('dp', 'seq')
- grad_w_qkv: float32 [768, 2304], P(('dp', 'seq'))
- grad_w_out: float32 [768, 768], P(('dp', 'seq'))
- grad_w_up: float32 [768, 3072], P(('dp', 'seq'))
- grad_w_down: float32 [3072, 768], P(('dp', 'seq'))
- grad_gain_attn: float32 [768], P(('dp', 'seq'))
- grad_gain_ffn: float32 [768], P(('dp', 'seq'))
Inputs may be any that keep to these rules, and one draw needn't show every extreme that they name: `segments`: within each window the ids never fall, start at 0 at its first position and end at 7 at its last.
All inputs are finite; a program needn't handle non-finite values.
Results may differ from a plain program's by a relative error of at most 0.012.
Values may be sent and summed in bfloat16 or wider, within the bound.
No kernel may reach another device: no remote copies, remote signals or barrier semaphores. Data moves between devices by JAX's collectives and lax.ppermute only.
A program may use at most 384 MiB of HBM per device.

v0:
```python
import jax
import jax.numpy as jnp
from jax import lax
from jax.sharding import PartitionSpec as P

HEADS = 24
HEAD_DIM = 32


epsilon = 1e-05
masked_score = -1e30


def shifted(block, axis, distance):
    devices = range(lax.axis_size(axis))
    route = [(i - distance, i) for i in devices if i - distance in devices]
    return lax.ppermute(block, axis, route)


def norm_gain(values, gain_vector):
    row_mean = jnp.mean(values, axis=-1, keepdims=True)
    centred = values - row_mean
    variance = jnp.mean(centred * centred, axis=-1, keepdims=True)
    return centred * lax.rsqrt(variance + epsilon) * gain_vector


def block_scores(queries, keys_all, allowed):
    scores = jnp.einsum(
        "qhd,khd->hqk", queries, keys_all, preferred_element_type=jnp.float32
    ) * HEAD_DIM ** (-0.5)
    return jnp.where(allowed[None], scores, masked_score)


def attend(packed):
    queries, keys_all, values_all, allowed = packed
    scores = block_scores(queries, keys_all, allowed)
    row_max = jnp.max(scores, axis=-1, keepdims=True)
    exponent = jnp.exp(scores - row_max)
    row_total = jnp.sum(exponent, axis=-1, keepdims=True)
    soft_weights = (exponent / row_total).astype(jnp.bfloat16)
    mixture = jnp.einsum(
        "hqk,khd->qhd", soft_weights, values_all, preferred_element_type=jnp.float32
    )
    return (mixture.astype(jnp.bfloat16), row_max + jnp.log(row_total))


def attend_back(packed):
    queries, keys_all, values_all, allowed, log_total, upstream = packed
    scores = block_scores(queries, keys_all, allowed)
    likely = jnp.exp(scores - log_total)
    soft_weights = likely.astype(jnp.bfloat16)
    grad_values = jnp.einsum(
        "hqk,qhd->khd", soft_weights, upstream, preferred_element_type=jnp.float32
    )
    grad_likely = jnp.einsum(
        "qhd,khd->hqk", upstream, values_all, preferred_element_type=jnp.float32
    )
    inner_sum = jnp.sum(likely * grad_likely, axis=-1, keepdims=True)
    grad_scores = (likely * (grad_likely - inner_sum)).astype(jnp.bfloat16)
    grad_queries = jnp.einsum(
        "hqk,khd->qhd", grad_scores, keys_all, preferred_element_type=jnp.float32
    ) * HEAD_DIM ** (-0.5)
    grad_keys = jnp.einsum(
        "hqk,qhd->khd", grad_scores, queries, preferred_element_type=jnp.float32
    ) * HEAD_DIM ** (-0.5)
    return (grad_queries, grad_keys, grad_values)


def body(tokens, segments, cotangent, gain_attn, w_qkv, w_out, gain_ffn, w_up, w_down):
    windows, local_rows, model_width = tokens.shape
    row_count = windows * local_rows
    seq_index = lax.axis_index("seq")
    inputs = tokens.reshape(row_count, model_width).astype(jnp.float32)
    normed_one, norm_one_pull = jax.vjp(norm_gain, inputs, gain_attn)
    low_one = normed_one.astype(jnp.bfloat16)
    project = jnp.dot(low_one, w_qkv, preferred_element_type=jnp.float32).astype(jnp.bfloat16)
    queries = project[:, :model_width].reshape(windows, local_rows, HEADS, HEAD_DIM)
    key_value = project[:, model_width:].reshape(windows, local_rows, 2 * model_width)
    remote_kv, remote_ids = shifted((key_value, segments), "seq", 1)
    joined_kv = jnp.concatenate([remote_kv, key_value], axis=1)
    joined_ids = jnp.concatenate([remote_ids, segments], axis=1)
    keys_all = joined_kv[..., :model_width].reshape(windows, 2 * local_rows, HEADS, HEAD_DIM)
    values_all = joined_kv[..., model_width:].reshape(windows, 2 * local_rows, HEADS, HEAD_DIM)
    query_place = seq_index * local_rows + jnp.arange(local_rows)
    key_place = (seq_index - 1) * local_rows + jnp.arange(2 * local_rows)
    present = jnp.arange(2 * local_rows) >= jnp.where(seq_index > 0, 0, local_rows)
    allowed = ((key_place[None, :] <= query_place[:, None]) & present[None, :])[None] & (
        segments[:, :, None] == joined_ids[:, None, :]
    )
    mixture, log_total = lax.map(attend, (queries, keys_all, values_all, allowed))
    mixture = mixture.reshape(row_count, model_width)
    middle = inputs + jnp.dot(mixture, w_out, preferred_element_type=jnp.float32)
    normed_two, norm_two_pull = jax.vjp(norm_gain, middle, gain_ffn)
    low_two = normed_two.astype(jnp.bfloat16)
    up_proj = jnp.dot(low_two, w_up, preferred_element_type=jnp.float32)
    activated, gelu_pull = jax.vjp(jax.nn.gelu, up_proj)
    low_three = activated.astype(jnp.bfloat16)
    outputs = middle + jnp.dot(low_three, w_down, preferred_element_type=jnp.float32)
    upstream = cotangent.reshape(row_count, model_width)
    grad_w_down = jnp.dot(low_three.T, upstream, preferred_element_type=jnp.float32)
    grad_active = jnp.dot(upstream, w_down.T, preferred_element_type=jnp.float32)
    grad_up = gelu_pull(grad_active)[0].astype(jnp.bfloat16)
    grad_w_up = jnp.dot(low_two.T, grad_up, preferred_element_type=jnp.float32)
    grad_norm_two = jnp.dot(grad_up, w_up.T, preferred_element_type=jnp.float32)
    grad_middle_norm, grad_gain_ffn = norm_two_pull(grad_norm_two)
    grad_middle = upstream.astype(jnp.float32) + grad_middle_norm
    grad_branch = grad_middle.astype(jnp.bfloat16)
    grad_w_out = jnp.dot(mixture.T, grad_branch, preferred_element_type=jnp.float32)
    grad_mixture = jnp.dot(grad_branch, w_out.T, preferred_element_type=jnp.float32).astype(
        jnp.bfloat16
    )
    grad_mixture = grad_mixture.reshape(windows, local_rows, HEADS, HEAD_DIM)
    grad_queries, grad_keys, grad_values = lax.map(
        attend_back, (queries, keys_all, values_all, allowed, log_total, grad_mixture)
    )
    grad_kv = jnp.concatenate(
        [
            grad_keys.reshape(windows, 2 * local_rows, model_width),
            grad_values.reshape(windows, 2 * local_rows, model_width),
        ],
        axis=2,
    )
    returned = shifted(grad_kv[:, :local_rows].astype(jnp.bfloat16), "seq", -1).astype(jnp.float32)
    own_kv = grad_kv[:, local_rows:] + returned
    grad_project = jnp.concatenate(
        [grad_queries.reshape(row_count, model_width), own_kv.reshape(row_count, 2 * model_width)],
        axis=1,
    ).astype(jnp.bfloat16)
    grad_w_qkv = jnp.dot(low_one.T, grad_project, preferred_element_type=jnp.float32)
    grad_norm_one = jnp.dot(grad_project, w_qkv.T, preferred_element_type=jnp.float32)
    grad_input_norm, grad_gain_attn = norm_one_pull(grad_norm_one)
    grad_inputs = grad_middle + grad_input_norm
    summed = (
        lax.psum_scatter(grad_w_qkv, ("dp", "seq"), scatter_dimension=0, tiled=True),
        lax.psum_scatter(grad_w_out, ("dp", "seq"), scatter_dimension=0, tiled=True),
        lax.psum_scatter(grad_w_up, ("dp", "seq"), scatter_dimension=0, tiled=True),
        lax.psum_scatter(grad_w_down, ("dp", "seq"), scatter_dimension=0, tiled=True),
        lax.psum_scatter(grad_gain_attn, ("dp", "seq"), scatter_dimension=0, tiled=True),
        lax.psum_scatter(grad_gain_ffn, ("dp", "seq"), scatter_dimension=0, tiled=True),
    )
    return (
        outputs.reshape(windows, local_rows, model_width).astype(jnp.bfloat16),
        grad_inputs.reshape(windows, local_rows, model_width).astype(jnp.bfloat16),
        summed[0],
        summed[1],
        summed[2],
        summed[3],
        summed[4],
        summed[5],
    )


def solution(mesh):
    placed = (
        P("dp", "seq", None),
        P("dp", "seq"),
        P("dp", "seq", None),
        P(),
        P(),
        P(),
        P(),
        P(),
        P(),
    )
    return jax.shard_map(
        body,
        mesh=mesh,
        in_specs=placed,
        out_specs=(
            P("dp", "seq", None),
            P("dp", "seq", None),
            P(("dp", "seq"), None),
            P(("dp", "seq"), None),
            P(("dp", "seq"), None),
            P(("dp", "seq"), None),
            P(("dp", "seq")),
            P(("dp", "seq")),
        ),
        check_vma=False,
    )
```

profile of v0, /device:TPU:0, one launch (start us, length us, event | category | flops | bytes accessed | tf_op | source)
XLA Modules:
  0.0 873.5 jit_solution(6227400594382644741)
XLA Ops:
  41.5 51.1 %collective-permute-done.1 = s32[2,512]{1,0:T(2,128)S(1)} collective-permute-done((s32[2,512]{1,0:T(2,128)S(1)}, s32[2,512]{1,0:T(2,128)S(1)}, u32[]{:S(2)}, u32[]{:S(2)}) %collective-permute-start.1) | collective-permute-done | bytes 4128 | tf_op jit(solution)/shard_map/ppermute | solution.py:17
  108.6 138.6 %while.26 = (s32[]{:T(128)}, bf16[2,512,24,32]{1,3,2,0:T(8,128)(2,1)}, f32[2,24,512,1]{2,1,3,0:T(8,128)}, bf16[2,1024,24,32]{1,3,2,0:T(8,128)(2,1)}, pred[2,512,...) while((s32[]{:T(128)}, ...), condition=%wide.region_5.6_spmd, body=%wide.region_2.5_spmd.sunk | while | flops 1761988608 | bytes 186976560 | solution.py:90
  110.4 22.7 %fusion.125 = (f32[24,512]{1,0:T(8,128)}, f32[24,512,1024]{2,1,0:T(8,128)}) fusion(pred[512,1024]{1,0:T(8,128)(4,1)} %dynamic-slice_bitcast_fusion.6, bf16[2,1024,24,32]{1,3,2,0:T(8,128)(2,1)} %get-tuple-element.362, s32[]{:T(128)S(6)} %copy.68, bf16[2,512,24,32]{1,3,2,0:T(8,128)(2,1)} %get-tuple-element.361), kind=kOutput, calls=%fused_computation.3.clone.1 | convolution fusion | flops 843042816 | bytes 53265408 | tf_op jit(solution)/shard_map/while/body/eval_jaxpr/qhd,khd->hqk/dot_general | solution.py:28
  133.1 22.8 %fusion.126 = f32[24,512]{1,0:T(8,128)S(1)} fusion(f32[24,512,1024]{2,1,0:T(8,128)} %get-tuple-element.326, f32[24,512]{1,0:T(8,128)} %get-tuple-element.327, pred[512,1024]{1,0:T(8,128)(4,1)} %dynamic-slice_bitcast_fusion.6), kind=kLoop, calls=%fused_computation.4.clone.1 | loop fusion | flops 50319360 | bytes 50954240 | tf_op jit(solution)/shard_map/while/body/eval_jaxpr/reduce_sum | solution.py:39
  156.0 19.9 %fusion.127 = bf16[2,512,24,32]{1,3,2,0:T(8,128)(2,1)S(1)} fusion(bf16[2,512,24,32]{1,3,2,0:T(8,128)(2,1)S(1)} %copy-done.18, s32[]{:T(128)S(6)} %copy.68, f32[24,512,1024]{2,1,0:T(8,128)} %get-tuple-element.326, f32[24,512]{1,0:T(8,128)S(1)} %fusion.126, f32[24,512]{1,0:T(8,128)S(1)} %copy-done.10, pred[512,1024]{1,0:T(8,128)(4,1)S(1)} %copy-done.1, ...), kind=kOutput, calls=%fused_computation.14.clone.1 | convolution fusion | flops 868614144 | bytes 53314560 | tf_op jit(solution)/shard_map/while/body/eval_jaxpr/hqk,khd->qhd/dot_general | solution.py:41
  179.6 22.7 %fusion.125 = (f32[24,512]{1,0:T(8,128)}, f32[24,512,1024]{2,1,0:T(8,128)}) fusion(pred[512,1024]{1,0:T(8,128)(4,1)} %dynamic-slice_bitcast_fusion.6, bf16[2,1024,24,32]{1,3,2,0:T(8,128)(2,1)} %get-tuple-element.362, s32[]{:T(128)S(6)} %copy.68, bf16[2,512,24,32]{1,3,2,0:T(8,128)(2,1)} %get-tuple-element.361), kind=kOutput, calls=%fused_computation.3.clone.1 | convolution fusion | flops 843042816 | bytes 53265408 | tf_op jit(solution)/shard_map/while/body/eval_jaxpr/qhd,khd->hqk/dot_general | solution.py:28
  202.2 22.8 %fusion.126 = f32[24,512]{1,0:T(8,128)S(1)} fusion(f32[24,512,1024]{2,1,0:T(8,128)} %get-tuple-element.326, f32[24,512]{1,0:T(8,128)} %get-tuple-element.327, pred[512,1024]{1,0:T(8,128)(4,1)} %dynamic-slice_bitcast_fusion.6), kind=kLoop, calls=%fused_computation.4.clone.1 | loop fusion | flops 50319360 | bytes 50954240 | tf_op jit(solution)/shard_map/while/body/eval_jaxpr/reduce_sum | solution.py:39
  225.1 19.9 %fusion.127 = bf16[2,512,24,32]{1,3,2,0:T(8,128)(2,1)S(1)} fusion(bf16[2,512,24,32]{1,3,2,0:T(8,128)(2,1)S(1)} %copy-done.18, s32[]{:T(128)S(6)} %copy.68, f32[24,512,1024]{2,1,0:T(8,128)} %get-tuple-element.326, f32[24,512]{1,0:T(8,128)S(1)} %fusion.126, f32[24,512]{1,0:T(8,128)S(1)} %copy-done.10, pred[512,1024]{1,0:T(8,128)(4,1)S(1)} %copy-done.1, ...), kind=kOutput, calls=%fused_computation.14.clone.1 | convolution fusion | flops 868614144 | bytes 53314560 | tf_op jit(solution)/shard_map/while/body/eval_jaxpr/hqk,khd->qhd/dot_general | solution.py:41
  261.6 14.4 %fusion.61 = bf16[1024,3072]{1,0:T(8,128)(2,1)S(1)} fusion(f32[1024,3072]{1,0:T(8,128)} %fusion.86, bf16[1024,768]{1,0:T(8,128)(2,1)S(1)} %bitcast.192, bf16[3072,768]{1,0:T(8,128)(2,1)} %param.21), kind=kOutput, calls=%fused_computation.65 | convolution fusion | flops 4894752768 | bytes 25165824 | tf_op jit(solution)/shard_map/dot_general | solution.py:101
  331.8 315.4 %while.27 = (s32[]{:T(128)}, bf16[2,512,24,32]{1,3,2,0:T(8,128)(2,1)}, f32[2,1024,24,32]{1,3,2,0:T(8,128)}, f32[2,1024,24,32]{1,3,2,0:T(8,128)}, bf16[2,1024,24,...) while((s32[]{:T(128)}, ...), condition=%wide.region_12.13_spmd, body=%wide.region_10.12_spmd.sunk | while | flops 4216442880 | bytes 396186752 | solution.py:113
  335.5 21.4 %fusion.136 = f32[24,512,1024]{2,1,0:T(8,128)} fusion(bf16[2,1024,24,32]{1,3,2,0:T(8,128)(2,1)} %get-tuple-element.390, s32[]{:T(128)S(6)} %copy.78, bf16[2,512,24,32]{1,3,2,0:T(8,128)(2,1)} %get-tuple-element.392), kind=kOutput, calls=%fused_computation.36.clone.1 | convolution fusion | flops 805306368 | bytes 52691968 | tf_op jit(solution)/shard_map/while/body/eval_jaxpr/qhd,khd->hqk/dot_general | solution.py:28
  356.9 22.0 %bitcast_dynamic-update-slice_fusion.11 = f32[2,1024,24,32]{1,3,2,0:T(8,128)} fusion(f32[2,1024,24,32]{1,3,2,0:T(8,128)} %get-tuple-element.378, s32[]{:T(128)S(6)} %copy.78, f32[24,512,1024]{2,1,0:T(8,128)} %fusion.136, f32[24,512]{1,0:T(8,128)} %dynamic-slice_bitcast_fusion.7, pred[512,1024]{1,0:T(8,128)(4,1)} %dynamic-slice_bitcast_fusion.8, ...), kind=kOutput, calls=%fused_computation.28.clone.1 | convolution fusion | flops 855638016 | bytes 54838272 | tf_op jit(solution)/shard_map/while/body/eval_jaxpr/hqk,qhd->khd/dot_general | solution.py:52
  378.9 37.8 %multiply_reduce_fusion.5 = (f32[24,512]{1,0:T(8,128)}, f32[24,512,1024]{2,1,0:T(8,128)}) fusion(f32[24,512,1024]{2,1,0:T(8,128)} %fusion.136, f32[24,512]{1,0:T(8,128)} %dynamic-slice_bitcast_fusion.7, pred[512,1024]{1,0:T(8,128)(4,1)} %dynamic-slice_bitcast_fusion.8, bf16[2,1024,24,32]{1,3,2,0:T(8,128)(2,1)} %get-tuple-element.395, s32[]{:T(128)S(6)} %copy.78, ...), kind=kOutput, calls=%fused_computation.23.clone.1 | convolution fusion | flops 868208640 | bytes 103646208 | tf_op jit(solution)/shard_map/while/body/eval_jaxpr/qhd,khd->hqk/dot_general | solution.py:55
  416.7 44.3 %multiply_convert_fusion.8 = bf16[24,512,1024]{2,1,0:T(8,128)(2,1)} fusion(f32[24,512,1024]{2,1,0:T(8,128)} %get-tuple-element.338, f32[24,512,1024]{2,1,0:T(8,128)} %fusion.136, f32[24,512]{1,0:T(8,128)} %get-tuple-element.339, f32[24,512]{1,0:T(8,128)} %dynamic-slice_bitcast_fusion.7, pred[512,1024]{1,0:T(8,128)(4,1)} %dynamic-slice_bitcast_fusion.8), kind=kLoop, calls=%fused_computation.22.clone.1 | loop fusion | flops 75497472 | bytes 126451712 | tf_op jit(solution)/shard_map/while/body/eval_jaxpr/convert_element_type | solution.py:59
  474.6 15.1 %bitcast_dynamic-update-slice_fusion.10 = f32[2,1024,24,32]{1,3,2,0:T(8,128)} fusion(f32[2,1024,24,32]{1,3,2,0:T(8,128)} %get-tuple-element.377, s32[]{:T(128)S(6)} %copy.78, bf16[24,512,1024]{2,1,0:T(8,128)(2,1)} %multiply_convert_fusion.8, bf16[2,512,24,32]{1,3,2,0:T(8,128)(2,1)} %get-tuple-element.392), kind=kOutput, calls=%fused_computation.29.clone.1 | convolution fusion | flops 806092800 | bytes 29099008 | tf_op jit(solution)/shard_map/while/body/eval_jaxpr/hqk,qhd->khd/dot_general | solution.py:63
  493.0 21.6 %fusion.136 = f32[24,512,1024]{2,1,0:T(8,128)} fusion(bf16[2,1024,24,32]{1,3,2,0:T(8,128)(2,1)} %get-tuple-element.390, s32[]{:T(128)S(6)} %copy.78, bf16[2,512,24,32]{1,3,2,0:T(8,128)(2,1)} %get-tuple-element.392), kind=kOutput, calls=%fused_computation.36.clone.1 | convolution fusion | flops 805306368 | bytes 52691968 | tf_op jit(solution)/shard_map/while/body/eval_jaxpr/qhd,khd->hqk/dot_general | solution.py:28
  514.6 22.0 %bitcast_dynamic-update-slice_fusion.11 = f32[2,1024,24,32]{1,3,2,0:T(8,128)} fusion(f32[2,1024,24,32]{1,3,2,0:T(8,128)} %get-tuple-element.378, s32[]{:T(128)S(6)} %copy.78, f32[24,512,1024]{2,1,0:T(8,128)} %fusion.136, f32[24,512]{1,0:T(8,128)} %dynamic-slice_bitcast_fusion.7, pred[512,1024]{1,0:T(8,128)(4,1)} %dynamic-slice_bitcast_fusion.8, ...), kind=kOutput, calls=%fused_computation.28.clone.1 | convolution fusion | flops 855638016 | bytes 54838272 | tf_op jit(solution)/shard_map/while/body/eval_jaxpr/hqk,qhd->khd/dot_general | solution.py:52
  536.6 38.1 %multiply_reduce_fusion.5 = (f32[24,512]{1,0:T(8,128)}, f32[24,512,1024]{2,1,0:T(8,128)}) fusion(f32[24,512,1024]{2,1,0:T(8,128)} %fusion.136, f32[24,512]{1,0:T(8,128)} %dynamic-slice_bitcast_fusion.7, pred[512,1024]{1,0:T(8,128)(4,1)} %dynamic-slice_bitcast_fusion.8, bf16[2,1024,24,32]{1,3,2,0:T(8,128)(2,1)} %get-tuple-element.395, s32[]{:T(128)S(6)} %copy.78, ...), kind=kOutput, calls=%fused_computation.23.clone.1 | convolution fusion | flops 868208640 | bytes 103646208 | tf_op jit(solution)/shard_map/while/body/eval_jaxpr/qhd,khd->hqk/dot_general | solution.py:55
  574.6 43.4 %multiply_convert_fusion.8 = bf16[24,512,1024]{2,1,0:T(8,128)(2,1)} fusion(f32[24,512,1024]{2,1,0:T(8,128)} %get-tuple-element.338, f32[24,512,1024]{2,1,0:T(8,128)} %fusion.136, f32[24,512]{1,0:T(8,128)} %get-tuple-element.339, f32[24,512]{1,0:T(8,128)} %dynamic-slice_bitcast_fusion.7, pred[512,1024]{1,0:T(8,128)(4,1)} %dynamic-slice_bitcast_fusion.8), kind=kLoop, calls=%fused_computation.22.clone.1 | loop fusion | flops 75497472 | bytes 126451712 | tf_op jit(solution)/shard_map/while/body/eval_jaxpr/convert_element_type | solution.py:59
  618.1 13.9 %bitcast_dynamic-update-slice_fusion.9 = bf16[2,512,24,32]{1,3,2,0:T(8,128)(2,1)} fusion(bf16[2,512,24,32]{1,3,2,0:T(8,128)(2,1)} %get-tuple-element.376, s32[]{:T(128)S(6)} %copy.78, bf16[24,512,1024]{2,1,0:T(8,128)(2,1)} %multiply_convert_fusion.8, bf16[2,1024,24,32]{1,3,2,0:T(8,128)(2,1)} %get-tuple-element.390), kind=kOutput, calls=%fused_computation.31.clone.1 | convolution fusion | flops 805699584 | bytes 28312576 | tf_op jit(solution)/shard_map/while/body/eval_jaxpr/hqk,khd->qhd/dot_general | solution.py:60
  632.0 15.0 %bitcast_dynamic-update-slice_fusion.10 = f32[2,1024,24,32]{1,3,2,0:T(8,128)} fusion(f32[2,1024,24,32]{1,3,2,0:T(8,128)} %get-tuple-element.377, s32[]{:T(128)S(6)} %copy.78, bf16[24,512,1024]{2,1,0:T(8,128)(2,1)} %multiply_convert_fusion.8, bf16[2,512,24,32]{1,3,2,0:T(8,128)(2,1)} %get-tuple-element.392), kind=kOutput, calls=%fused_computation.29.clone.1 | convolution fusion | flops 806092800 | bytes 29099008 | tf_op jit(solution)/shard_map/while/body/eval_jaxpr/hqk,qhd->khd/dot_general | solution.py:63
  659.4 66.9 %collective-permute-done.2 = bf16[2,512,1536]{1,2,0:T(8,128)(2,1)} collective-permute-done((bf16[2,512,1536]{1,2,0:T(8,128)(2,1)}, bf16[2,512,1536]{1,2,0:T(8,128)(2,1)}, u32[]{:S(2)}, u32[]{:S(2)}) %collective-permute-start.2) | collective-permute-done | bytes 3145760 | tf_op jit(solution)/shard_map/ppermute | solution.py:17
  765.8 39.8 %all-reduce.2 = (f32[768]{0:T(1024)}, f32[768]{0:T(1024)}) all-reduce(f32[768]{0:T(1024)} %get-tuple-element.175, f32[768]{0:T(1024)} %get-tuple-element.173), channel_id=6, replica_groups=mesh['dp'=16,'seq'=2] {'dp','seq'}, use_global_device_ids=true, to_apply=%region_20.21.clone | all-reduce | flops 1536 | bytes 12288
  814.2 52.7 %reduce-scatter.5.cloned.1.call-done = f32[24,2304]{1,0:T(8,128)} async-done(((f32[768,2304]{1,0:T(8,128)}), f32[24,2304]{1,0:T(8,128)}) %reduce-scatter.5.cloned.1.call-update) | async-done | bytes 221200 | tf_op jit(solution)/shard_map/reduce_scatter | solution.py:134
  (177 shorter events, 207.7 us)
Async XLA Ops:
  7.2 806.9 %reduce-scatter.7.cloned.1.call-start = ((), (), s32[]{:S(2)}) async-start(), calls=%async_computation.5 | async-start | bytes 2433024 | tf_op jit(solution)/shard_map/reduce_scatter | solution.py:135
  20.1 74.4 %collective-permute-start = (bf16[2,512,1536]{2,1,0:T(8,128)(2,1)}, bf16[2,512,1536]{2,1,0:T(8,128)(2,1)}, u32[]{:S(2)}, u32[]{:S(2)}) collective-permute-start(bf16[2,512,1536]{2,1,0:T(8,128)(2,1)} %bitcast.20), channel_id=1, source_target_pairs={{0,1},{2,3},{4,5},{6,7},{8,9},{10,11},{12,13},{14,15},{16,17},{18,... | collective-permute-start | bytes 9437192 | tf_op jit(solution)/shard_map/ppermute | solution.py:17
  26.7 65.9 %collective-permute-start.1 = (s32[2,512]{1,0:T(2,128)S(1)}, s32[2,512]{1,0:T(2,128)S(1)}, u32[]{:S(2)}, u32[]{:S(2)}) collective-permute-start(s32[2,512]{1,0:T(2,128)S(1)} %copy-done.34), channel_id=1, source_target_pairs={{0,1},{2,3},{4,5},{6,7},{8,9},{10,11},{12,13},{14,15},{16,17},{18,... | collective-permute-start | bytes 12296 | tf_op jit(solution)/shard_map/ppermute | solution.py:17
  38.6 54.1 %copy-start.15 = (pred[512,1024]{1,0:T(8,128)(4,1)S(1)}, pred[512,1024]{1,0:T(8,128)(4,1)}, u32[]{:S(2)}) copy-start(pred[512,1024]{1,0:T(8,128)(4,1)} %compare_and_fusion.1) | copy-start | bytes 1572868
  133.1 22.8 %copy-start.1 = (pred[512,1024]{1,0:T(8,128)(4,1)S(1)}, pred[512,1024]{1,0:T(8,128)(4,1)}, u32[]{:S(2)}) copy-start(pred[512,1024]{1,0:T(8,128)(4,1)} %dynamic-slice_bitcast_fusion.6) | copy-start | bytes 1572868 | tf_op jit(solution)/shard_map/while
  133.1 22.8 %copy-start.5 = (bf16[2,1024,24,32]{1,3,2,0:T(8,128)(2,1)S(1)}, bf16[2,1024,24,32]{1,3,2,0:T(8,128)(2,1)}, u32[]{:S(2)}) copy-start(bf16[2,1024,24,32]{1,3,2,0:T(8,128)(2,1)} %get-tuple-element.359) | copy-start | bytes 9437188 | tf_op jit(solution)/shard_map/while
  133.1 22.8 %copy-start.10 = (f32[24,512]{1,0:T(8,128)S(1)}, f32[24,512]{1,0:T(8,128)}, u32[]{:S(2)}) copy-start(f32[24,512]{1,0:T(8,128)} %get-tuple-element.327) | copy-start | bytes 147460 | tf_op jit(solution)/shard_map/while
  133.1 22.8 %copy-start.18 = (bf16[2,512,24,32]{1,3,2,0:T(8,128)(2,1)S(1)}, bf16[2,512,24,32]{1,3,2,0:T(8,128)(2,1)}, u32[]{:S(2)}) copy-start(bf16[2,512,24,32]{1,3,2,0:T(8,128)(2,1)} %get-tuple-element.349) | copy-start | bytes 4718596 | tf_op jit(solution)/shard_map/while
  156.0 19.9 %copy-start.22 = (f32[2,24,512,1]{2,1,3,0:T(8,128)S(1)}, f32[2,24,512,1]{2,1,3,0:T(8,128)}, u32[]{:S(2)}) copy-start(f32[2,24,512,1]{2,1,3,0:T(8,128)} %get-tuple-element.350) | copy-start | bytes 294916 | tf_op jit(solution)/shard_map/while
  202.2 22.8 %copy-start.1 = (pred[512,1024]{1,0:T(8,128)(4,1)S(1)}, pred[512,1024]{1,0:T(8,128)(4,1)}, u32[]{:S(2)}) copy-start(pred[512,1024]{1,0:T(8,128)(4,1)} %dynamic-slice_bitcast_fusion.6) | copy-start | bytes 1572868 | tf_op jit(solution)/shard_map/while
  202.2 22.8 %copy-start.5 = (bf16[2,1024,24,32]{1,3,2,0:T(8,128)(2,1)S(1)}, bf16[2,1024,24,32]{1,3,2,0:T(8,128)(2,1)}, u32[]{:S(2)}) copy-start(bf16[2,1024,24,32]{1,3,2,0:T(8,128)(2,1)} %get-tuple-element.359) | copy-start | bytes 9437188 | tf_op jit(solution)/shard_map/while
  202.2 22.8 %copy-start.10 = (f32[24,512]{1,0:T(8,128)S(1)}, f32[24,512]{1,0:T(8,128)}, u32[]{:S(2)}) copy-start(f32[24,512]{1,0:T(8,128)} %get-tuple-element.327) | copy-start | bytes 147460 | tf_op jit(solution)/shard_map/while
  202.2 22.8 %copy-start.18 = (bf16[2,512,24,32]{1,3,2,0:T(8,128)(2,1)S(1)}, bf16[2,512,24,32]{1,3,2,0:T(8,128)(2,1)}, u32[]{:S(2)}) copy-start(bf16[2,512,24,32]{1,3,2,0:T(8,128)(2,1)} %get-tuple-element.349) | copy-start | bytes 4718596 | tf_op jit(solution)/shard_map/while
  225.1 19.9 %copy-start.22 = (f32[2,24,512,1]{2,1,3,0:T(8,128)S(1)}, f32[2,24,512,1]{2,1,3,0:T(8,128)}, u32[]{:S(2)}) copy-start(f32[2,24,512,1]{2,1,3,0:T(8,128)} %get-tuple-element.350) | copy-start | bytes 294916 | tf_op jit(solution)/shard_map/while
  252.5 34.3 %copy-start.6 = (f32[1024,768]{1,0:T(8,128)}, f32[1024,768]{1,0:T(8,128)S(1)}, u32[]{:S(2)}) copy-start(f32[1024,768]{1,0:T(8,128)S(1)} %get-tuple-element.224) | copy-start | bytes 9437188
  294.0 520.1 %reduce-scatter.11.cloned.1.call-start = ((), (), s32[]{:S(2)}) async-start(), calls=%async_computation.7 | async-start | bytes 9732096 | tf_op jit(solution)/shard_map/reduce_scatter | solution.py:137
  307.0 507.2 %reduce-scatter.9.cloned.1.call-start = ((), (), s32[]{:S(2)}) async-start(), calls=%async_computation.6 | async-start | bytes 9732096 | tf_op jit(solution)/shard_map/reduce_scatter | solution.py:136
  331.7 535.1 %reduce-scatter.5.cloned.1.call-start = ((), (), s32[]{:S(2)}) async-start(), calls=%async_computation.4 | async-start | bytes 7299072 | tf_op jit(solution)/shard_map/reduce_scatter | solution.py:134
  652.3 74.0 %collective-permute-start.2 = (bf16[2,512,1536]{1,2,0:T(8,128)(2,1)}, bf16[2,512,1536]{1,2,0:T(8,128)(2,1)}, u32[]{:S(2)}, u32[]{:S(2)}) collective-permute-start(bf16[2,512,1536]{1,2,0:T(8,128)(2,1)} %fusion.65), channel_id=1, source_target_pairs={{1,0},{3,2},{5,4},{7,6},{9,8},{11,10},{13,12},{15,14},{17,16},{19,... | collective-permute-start | bytes 9437192 | tf_op jit(solution)/shard_map/ppermute | solution.py:17
  746.1 13.2 %copy-start.4 = (bf16[2,512,768]{2,1,0:T(8,128)(2,1)S(1)}, bf16[2,512,768]{2,1,0:T(8,128)(2,1)}, u32[]{:S(2)}) copy-start(bf16[2,512,768]{2,1,0:T(8,128)(2,1)} %param.13) | copy-start | bytes 4718596
  746.1 13.2 %copy-start.14 = (bf16[2,512,1536]{2,1,0:T(8,128)(2,1)S(1)}, bf16[2,512,1536]{2,1,0:T(8,128)(2,1)}, u32[]{:S(2)}) copy-start(bf16[2,512,1536]{2,1,0:T(8,128)(2,1)} %copy.54) | copy-start | bytes 9437188
  746.1 13.2 %copy-start.17 = (bf16[1024,768]{1,0:T(8,128)(2,1)S(1)}, bf16[1024,768]{1,0:T(8,128)(2,1)}, u32[]{:S(2)}) copy-start(bf16[1024,768]{1,0:T(8,128)(2,1)} %copy.55) | copy-start | bytes 4718596
  746.1 13.2 %copy-start.26 = (f32[1,4,2,128]{3,1,2,0:T(4,128)S(1)}, f32[1,4,2,128]{3,1,2,0:T(4,128)}, u32[]{:S(2)}) copy-start(f32[1,4,2,128]{3,1,2,0:T(4,128)} %copy-done.25) | copy-start | bytes 12292
  746.2 13.2 %copy-start.30 = (f32[768]{0:T(1024)S(1)}, f32[768]{0:T(1024)}, u32[]{:S(2)}) copy-start(f32[768]{0:T(1024)} %param.16) | copy-start | bytes 9220
  (28 other events, 96.8 us)
Sparse Core Ops, SparseCore 0:
  294.2 101.1 reduce-scatter.6
  402.8 134.5 reduce-scatter.10
  543.9 136.1 reduce-scatter.8
  746.2 120.5 reduce-scatter.4
where the time goes:
time: 878 us; the launch traced here: 874 us
  matrix products  402 us (46%)
  waiting for transfers between devices  171 us (19%)
  other arithmetic  167 us (19%)
  local copies, waits for them, and re-layouts  68.4 us (8%)
  blocking collectives  39.8 us (5%)
  between operations  14.5 us (2%)
  starting transfers between devices  9.55 us (1%)
    ppermute x3, waiting for transfers between devices, shifted(): return lax.ppermute(block, axis, route)  118 us
    dot_general x4, matrix products, block_scores(): jnp.einsum('qhd,khd->hqk', queries, keys_all, preferred_element_type=jnp....  88.4 us
    convert_element_type x2, other arithmetic, attend_back(): grad_scores = (likely * (grad_likely - inner_sum)).astype(jnp.bfloat16)  87.8 us
    dot_general x2, matrix products, attend_back(): jnp.einsum('qhd,khd->hqk', upstream, values_all, preferred_element_type=j...  75.8 us
    reduce_scatter x1, waiting for transfers between devices, body(): lax.psum_scatter(grad_w_qkv, ('dp', 'seq'), scatter_dimension=0, tiled=True)  52.7 us
    reduce_sum x2, other arithmetic, attend(): row_total = jnp.sum(exponent, axis=-1, keepdims=True)  45.6 us
    dot_general x2, matrix products, attend_back(): jnp.einsum('hqk,qhd->khd', soft_weights, upstream, preferred_element_type...  43.9 us
    dot_general x2, matrix products, attend(): jnp.einsum('hqk,khd->qhd', soft_weights, values_all, preferred_element_ty...  39.8 us
  transfers between devices with their start and end apart: 7, of which 3 were waited for; matrix products, arithmetic and copies ran while one was open for 49% of the time, Pallas kernels for 0%

commit v1 on v0

v1 whole, which is shorter than its diff:
```python
import functools

import jax
import jax.numpy as jnp
from jax import lax
from jax.experimental import pallas as pl
from jax.experimental.pallas import tpu as pltpu
from jax.sharding import PartitionSpec as P

HEAD_DIM = 32
GROUP = 8
LANES = GROUP * HEAD_DIM
GRAIN = 128
masked_score = -1e30
SCALE = HEAD_DIM ** (-0.5)
SCALE2 = SCALE * 1.4426950408889634
NT = (((1,), (1,)), ((), ()))
NN = (((1,), (0,)), ((), ()))


def mm(a, b, dims=NN):
    return lax.dot_general(a, b, dims, preferred_element_type=jnp.float32)


def attend_kernel(first, seg_ref, q_ref, k_ref, v_ref, o_ref, lse_ref, bias, total, *, bq, unroll):
    i, g = pl.program_id(0), pl.program_id(1)
    length = k_ref.shape[0]
    start = first[i]
    lane = lax.div(lax.broadcasted_iota(jnp.int32, (1, LANES), 1), HEAD_DIM)
    lane_head = lax.broadcasted_iota(jnp.int32, (1, 128), 1)

    def span(width):
        begin = pl.multiple_of(start * GRAIN, GRAIN)

        @pl.when(g == 0)
        def _():
            seg_q = jnp.transpose(jnp.broadcast_to(seg_ref[0:1, pl.ds(pl.multiple_of(i * bq, bq), bq)], (128, bq)))[:, 0:1]
            place_q = i * bq + lax.broadcasted_iota(jnp.int32, (bq, width), 0)
            place_k = begin + lax.broadcasted_iota(jnp.int32, (bq, width), 1)
            allowed = (place_k <= place_q) & (seg_q == seg_ref[0:1, pl.ds(begin, width)])
            bias[:, :width] = jnp.where(allowed, 0.0, masked_score)

        total[...] = jnp.zeros_like(total)

        def head(h, logs):
            query = jnp.where(lane == h, q_ref[...], jnp.zeros((), jnp.bfloat16))
            s = mm(query, k_ref[pl.ds(begin, width), :], NT) * SCALE2 + bias[:, :width]
            top = jnp.max(s, axis=-1, keepdims=True)
            e = jnp.exp2(s - top)
            row = jnp.sum(e, axis=-1, keepdims=True)
            out = mm(e.astype(jnp.bfloat16), v_ref[pl.ds(begin, width), :])
            total[...] = jnp.where(lane == h, out / row, total[...])
            return jnp.where(lane_head == h, top + jnp.log2(row), logs)

        logs = lax.fori_loop(0, GROUP, head, jnp.zeros((bq, 128), jnp.float32), unroll=unroll)
        o_ref[...] = total[...].astype(o_ref.dtype)
        lse_ref[...] = jnp.transpose(logs)[:GROUP]

    blocks = (i + 1) * (bq // GRAIN) - start
    for count in range(bq // GRAIN, length // GRAIN + 1):
        pl.when(blocks == count)(functools.partial(span, count * GRAIN))


def attend(first, seg, proj, bq=256, unroll=2):
    length, width = proj.shape
    groups = width // 3 // LANES
    grid_spec = pltpu.PrefetchScalarGridSpec(
        num_scalar_prefetch=1,
        grid=(length // bq, groups),
        in_specs=[
            pl.BlockSpec((1, length), lambda i, g, *_: (0, 0)),
            pl.BlockSpec((bq, LANES), lambda i, g, *_: (i, g)),
            pl.BlockSpec((length, LANES), lambda i, g, *_: (0, groups + g)),
            pl.BlockSpec((length, LANES), lambda i, g, *_: (0, 2 * groups + g)),
        ],
        out_specs=[
            pl.BlockSpec((bq, LANES), lambda i, g, *_: (i, g)),
            pl.BlockSpec((GROUP, bq), lambda i, g, *_: (g, i)),
        ],
        scratch_shapes=[pltpu.VMEM((bq, length), jnp.float32), pltpu.VMEM((bq, LANES), jnp.float32)],
    )
    return pl.pallas_call(
        functools.partial(attend_kernel, bq=bq, unroll=unroll),
        grid_spec=grid_spec,
        out_shape=[
            jax.ShapeDtypeStruct((length, width // 3), jnp.bfloat16),
            jax.ShapeDtypeStruct((groups * GROUP, length), jnp.float32),
        ],
        compiler_params=pltpu.CompilerParams(vmem_limit_bytes=48 << 20),
        name="attend",
    )(first, seg, proj, proj, proj)


def attend_back_kernel(last, seg_ref, q_ref, k_ref, v_ref, up_ref, o_ref, lse_ref, gq_ref, gk_ref, gv_ref,
                       bias, inner, logs, key_t, gq_t, gk, gv, *, bk, unroll):
    g, j = pl.program_id(0), pl.program_id(1)
    length = q_ref.shape[0]
    lane = lax.div(lax.broadcasted_iota(jnp.int32, (1, LANES), 1), HEAD_DIM)

    @pl.when(j == 0)
    def _():
        gq_t[...] = jnp.zeros_like(gq_t)
        pick = (lax.div(lax.broadcasted_iota(jnp.int32, (GROUP, LANES), 1), HEAD_DIM)
                == lax.broadcasted_iota(jnp.int32, (GROUP, LANES), 0)).astype(jnp.float32)
        product = up_ref[...].astype(jnp.float32) * o_ref[...].astype(jnp.float32)
        totals = lax.dot_general(pick, product, NT, precision=lax.Precision.HIGHEST,
                                 preferred_element_type=jnp.float32)
        for h in range(GROUP):
            inner[h] = totals[h:h + 1]
            logs[h] = lse_ref[h:h + 1]

    key_t[...] = jnp.transpose(k_ref[...])

    def span(width):
        begin = pl.multiple_of(j * bk, bk)
        here = pl.ds(begin, width)
        seg_k = jnp.transpose(jnp.broadcast_to(seg_ref[0:1, pl.ds(begin, bk)], (128, bk)))[:, 0:1]
        place_k = lax.broadcasted_iota(jnp.int32, (bk, width), 0)
        place_q = lax.broadcasted_iota(jnp.int32, (bk, width), 1)
        allowed = (place_k <= place_q) & (seg_k == seg_ref[0:1, here])
        bias[:, :width] = jnp.where(allowed, 0.0, masked_score)

        def head(h, carry):
            zero = jnp.zeros((), jnp.bfloat16)
            key = jnp.where(lane == h, k_ref[...], zero)
            value = jnp.where(lane == h, v_ref[...], zero)
            s = mm(key, q_ref[here, :], NT) * SCALE2 + (bias[:, :width] - logs[h, :, here])
            p = jnp.exp2(s)
            dp = mm(value, up_ref[here, :], NT)
            ds = (p * (dp - inner[h, :, here])).astype(jnp.bfloat16)
            gv[...] = jnp.where(lane == h, mm(p.astype(jnp.bfloat16), up_ref[here, :]), gv[...])
            gk[...] = jnp.where(lane == h, mm(ds, q_ref[here, :]), gk[...])
            rows = pl.ds(pl.multiple_of(h * HEAD_DIM, HEAD_DIM), HEAD_DIM)
            gq_t[rows, here] += mm(key_t[rows, :], ds)
            return carry

        lax.fori_loop(0, GROUP, head, 0, unroll=unroll)

    blocks = last[j] - j * (bk // GRAIN)
    for count in range(bk // GRAIN, length // GRAIN + 1):
        pl.when(blocks == count)(functools.partial(span, count * GRAIN))

    gk_ref[...] = (gk[...] * SCALE).astype(gk_ref.dtype)
    gv_ref[...] = gv[...].astype(gv_ref.dtype)

    @pl.when(j == pl.num_programs(1) - 1)
    def _():
        gq_ref[...] = jnp.transpose((gq_t[...] * SCALE).astype(gq_ref.dtype))


def attend_back(last, seg, proj, up, o, lse, bk=256, unroll=2):
    length, width = proj.shape
    groups = width // 3 // LANES
    whole = lambda at: pl.BlockSpec((length, LANES), lambda g, j, *_: (0, at(g)))
    block = lambda at: pl.BlockSpec((bk, LANES), lambda g, j, *_: (j, at(g)))
    grid_spec = pltpu.PrefetchScalarGridSpec(
        num_scalar_prefetch=1,
        grid=(groups, length // bk),
        in_specs=[
            pl.BlockSpec((1, length), lambda g, j, *_: (0, 0)),
            whole(lambda g: g),
            block(lambda g: groups + g),
            block(lambda g: 2 * groups + g),
            whole(lambda g: g),
            whole(lambda g: g),
            pl.BlockSpec((GROUP, length), lambda g, j, *_: (g, 0)),
        ],
        out_specs=[whole(lambda g: g), block(lambda g: g), block(lambda g: g)],
        scratch_shapes=[
            pltpu.VMEM((bk, length), jnp.float32),
            pltpu.VMEM((GROUP, 1, length), jnp.float32),
            pltpu.VMEM((GROUP, 1, length), jnp.float32),
            pltpu.VMEM((LANES, bk), jnp.bfloat16),
            pltpu.VMEM((LANES, length), jnp.float32),
            pltpu.VMEM((bk, LANES), jnp.float32),
            pltpu.VMEM((bk, LANES), jnp.float32),
        ],
    )
    out = jax.ShapeDtypeStruct((length, width // 3), jnp.bfloat16)
    return pl.pallas_call(
        functools.partial(attend_back_kernel, bk=bk, unroll=unroll),
        grid_spec=grid_spec,
        out_shape=[out, out, out],
        compiler_params=pltpu.CompilerParams(vmem_limit_bytes=48 << 20),
        name="attend_back",
    )(last, seg, proj, proj, proj, up, o, lse)


def bounds(seg, bq, bk):
    length = seg.shape[1]
    row = seg[0]
    first = jnp.sum(row[None, :] < row[::bq][:, None], axis=1) // GRAIN
    last = (jnp.sum(row[None, :] <= row[bk - 1::bk][:, None], axis=1) + GRAIN - 1) // GRAIN
    return first.astype(jnp.int32), last.astype(jnp.int32)

epsilon = 1e-05


def norm_gain(values, gain_vector):
    row_mean = jnp.mean(values, axis=-1, keepdims=True)
    centred = values - row_mean
    variance = jnp.mean(centred * centred, axis=-1, keepdims=True)
    return centred * lax.rsqrt(variance + epsilon) * gain_vector


def swapped(block):
    return lax.ppermute(block, "seq", [(0, 1), (1, 0)])


def gather_window(block):
    place = lax.axis_index("seq")
    kept = lax.dynamic_index_in_dim(block, place, 0, keepdims=False)
    other = swapped(lax.dynamic_index_in_dim(block, 1 - place, 0, keepdims=False))
    return jnp.where(place == 0, jnp.concatenate([kept, other]), jnp.concatenate([other, kept]))


def spread_window(rows):
    place = lax.axis_index("seq")
    halves = rows.reshape(2, rows.shape[0] // 2, rows.shape[1])
    kept = lax.dynamic_index_in_dim(halves, place, 0, keepdims=False)
    other = swapped(lax.dynamic_index_in_dim(halves, 1 - place, 0, keepdims=False))
    return jnp.where(place == 0, jnp.stack([kept, other]), jnp.stack([other, kept]))


def body(tokens, segments, cotangent, gain_attn, w_qkv, w_out, gain_ffn, w_up, w_down):
    bf16 = jnp.bfloat16
    inputs = gather_window(tokens).astype(jnp.float32)
    seg = gather_window(segments)[None]
    upstream = gather_window(cotangent)
    first, last = bounds(seg, 256, 256)
    normed_one, norm_one_pull = jax.vjp(norm_gain, inputs, gain_attn)
    low_one = normed_one.astype(bf16)
    proj = mm(low_one, w_qkv).astype(bf16)
    mixture, lse = attend(first, seg, proj, bq=256, unroll=8)
    middle = inputs + mm(mixture, w_out)
    normed_two, norm_two_pull = jax.vjp(norm_gain, middle, gain_ffn)
    low_two = normed_two.astype(bf16)
    up_proj = mm(low_two, w_up)
    activated, gelu_pull = jax.vjp(jax.nn.gelu, up_proj)
    low_three = activated.astype(bf16)
    outputs = (middle + mm(low_three, w_down)).astype(bf16)
    grad_w_down = mm(low_three.T, upstream)
    grad_active = mm(upstream, w_down.T)
    grad_up = gelu_pull(grad_active)[0].astype(bf16)
    grad_w_up = mm(low_two.T, grad_up)
    grad_norm_two = mm(grad_up, w_up.T)
    grad_middle_norm, grad_gain_ffn = norm_two_pull(grad_norm_two)
    grad_middle = upstream.astype(jnp.float32) + grad_middle_norm
    grad_branch = grad_middle.astype(bf16)
    grad_w_out = mm(mixture.T, grad_branch)
    grad_mixture = mm(grad_branch, w_out.T).astype(bf16)
    grad_project = jnp.concatenate(
        attend_back(last, seg, proj, grad_mixture, mixture, lse, bk=256, unroll=4), axis=1
    )
    grad_w_qkv = mm(low_one.T, grad_project)
    grad_norm_one = mm(grad_project, w_qkv.T)
    grad_input_norm, grad_gain_attn = norm_one_pull(grad_norm_one)
    grad_inputs = (grad_middle + grad_input_norm).astype(bf16)
    summed = [
        lax.psum_scatter(grad, ("dp", "seq"), scatter_dimension=0, tiled=True)
        for grad in (grad_w_qkv, grad_w_out, grad_w_up, grad_w_down, grad_gain_attn, grad_gain_ffn)
    ]
    return (spread_window(outputs), spread_window(grad_inputs), *summed)


def solution(mesh):
    placed = (
        P("dp", "seq", None),
        P("dp", "seq"),
        P("dp", "seq", None),
        P(),
        P(),
        P(),
        P(),
        P(),
        P(),
    )
    return jax.shard_map(
        body,
        mesh=mesh,
        in_specs=placed,
        out_specs=(
            P("dp", "seq", None),
            P("dp", "seq", None),
            P(("dp", "seq"), None),
            P(("dp", "seq"), None),
            P(("dp", "seq"), None),
            P(("dp", "seq"), None),
            P(("dp", "seq")),
            P(("dp", "seq")),
        ),
        check_vma=False,
    )
```

time: 878 us -> 657 us (0.75)
  matrix products: 402 us -> 109 us
  waiting for transfers between devices: 171 us -> 329 us
  other arithmetic: 167 us -> 29.1 us
  Pallas kernels: 0 us -> 100 us
  local copies, waits for them, and re-layouts: 68.4 us -> 13.9 us
  blocking collectives: 39.8 us -> 54.9 us
    dot_general x26 -> x12, matrix products: 402 us -> 109 us  [mm(): return lax.dot_general(a, b, dims, preferred_element_type=jnp.float32)]
    reduce_scatter x4, waiting for transfers between devices: 52.7 us -> 314 us  [body(): lax.psum_scatter(grad, ('dp', 'seq'), scatter_dimension=0, tiled=True)]
    ppermute x3 -> x5, waiting for transfers between devices: 118 us -> 15.3 us  [swapped(): return lax.ppermute(block, 'seq', [(0, 1), (1, 0)])]
    pallas_call x0 -> x2, Pallas kernels: none -> 100 us  [the longest x1 57.5 us: attend_back(): pl.pallas_call(functools.partial(attend_back_kernel, bk=bk, unroll=unroll...]
    convert_element_type x5 -> x2, other arithmetic: 94.1 us -> 8.2 us  [the longest x1 5.07 us: body(): grad_inputs = (grad_middle + grad_input_norm).astype(bf16)]
    reduce_sum x2 -> x1, other arithmetic: 45.6 us -> 1.37 us  [bounds(): jnp.sum(row[None, :] <= row[bk - 1::bk][:, None], axis=1) + GRAIN - 1]
    slice x5 -> x2, local copies, waits for them, and re-layouts: 16.6 us -> 1.19 us  [the longest x1 0.59 us: bounds(): row[bk - 1::bk][:, None]]
    unnamed x1, blocking collectives: 39.8 us -> 54.9 us
  transfers between devices with their start and end apart: 7 -> 9, of which waited for: 3 -> 4; matrix products, arithmetic and copies ran while one was open for 49% -> 17% of each run, Pallas kernels for 0% -> 15%
where the time goes in v1:
time: 657 us; the launch traced here: 659 us
  waiting for transfers between devices  329 us (50%)
  matrix products  109 us (17%)
  Pallas kernels  100 us (15%)
  blocking collectives  54.9 us (8%)
  other arithmetic  29.1 us (4%)
  between operations  14.5 us (2%)
  local copies, waits for them, and re-layouts  13.9 us (2%)
  starting transfers between devices  7.54 us (1%)
    reduce_scatter x4, waiting for transfers between devices, body(): lax.psum_scatter(grad, ('dp', 'seq'), scatter_dimension=0, tiled=True)  314 us
    dot_general x12, matrix products, mm(): return lax.dot_general(a, b, dims, preferred_element_type=jnp.float32)  109 us
    pallas_call x1, Pallas kernels, attend_back(): pl.pallas_call(functools.partial(attend_back_kernel, bk=bk, unroll=unroll...  57.5 us
    unnamed x1, blocking collectives  54.9 us
    pallas_call x1, Pallas kernels, attend(): pl.pallas_call(functools.partial(attend_kernel, bq=bq, unroll=unroll), gr...  42.7 us
    ppermute x5, waiting for transfers between devices, swapped(): return lax.ppermute(block, 'seq', [(0, 1), (1, 0)])  15.3 us
  transfers between devices with their start and end apart: 9, of which 4 were waited for; matrix products, arithmetic and copies ran while one was open for 17% of the time, Pallas kernels for 15%

profile of v1, /device:TPU:0, one launch (start us, length us, event | category | flops | bytes accessed | tf_op | source)
XLA Modules:
  0.0 658.6 jit_solution(17604138879303901681)
XLA Ops:
  10.0 3.0 collective-permute-start
  16.4 15.3 %collective-permute-done.1 = s32[512]{0:T(512)S(1)} collective-permute-done((s32[512]{0:T(512)S(1)}, s32[512]{0:T(512)S(1)}, u32[]{:S(2)}, u32[]{:S(2)}) %collective-permute-start.1) | collective-permute-done | bytes 2080 | tf_op jit(solution)/shard_map/ppermute | solution.py:207
  41.4 7.7 %convolution_convert_fusion.q_ref.k_ref.v_ref = bf16[1024,2304]{1,0:T(8,128)(2,1)} fusion(bf16[768,2304]{1,0:T(8,128)(2,1)S(1)} %copy-done, f32[768]{0:T(1024)S(1)} %copy-done.26, f32[1024]{0:T(1024)S(1)} %fusion.18, f32[1024]{0:T(1024)S(1)} %broadcast_multiply_fusion.1, bf16[512,768]{1,0:T(8,128)(2,1)} %collective-permute-done, ...), kind=kOutput, calls=%fused_computation.10 | convolution fusion | flops 3637248000 | bytes 9841665 | tf_op jit(solution)/shard_map/dot_general | solution.py:22
  49.2 42.7 %attend.1 = (bf16[1024,768]{1,0:T(8,128)(2,1)S(1)}, f32[24,1024]{1,0:T(8,128)S(1)}) custom-call(s32[4]{0:T(128)S(1)} %and_select_fusion.1.first, s32[1,1024]{1,0:T(1,128)S(1)} %broadcast_select_fusion.seg_ref, bf16[1024,2304]{1,0:T(8,128)(2,1)} %convolution_convert_fusion.q_ref.k_ref.v_ref, bf16[1024,2304]{1,0:T(8,128)(2,1)} %convolution_convert_fusion.q_ref.k_ref.v_ref, ...), custom_call_target="tpu_custom_call" | custom-call | tf_op jit(solution)/shard_map/attend/pallas_call | solution.py:82
  91.9 3.5 fusion.28
  96.2 8.2 %fusion.25 = f32[1024,3072]{1,0:T(8,128)} fusion(bf16[768,3072]{1,0:T(8,128)(2,1)S(1)} %bitcast.41, f32[1024,768]{1,0:T(8,128)S(1)} %get-tuple-element.39, f32[768]{0:T(1024)S(1)} %copy-done.16, f32[1024]{0:T(1024)S(1)} %fusion.19, f32[1024]{0:T(1024)S(1)} %broadcast_multiply_fusion), kind=kOutput, calls=%fused_computation.77 | convolution fusion | flops 4834983936 | bytes 20458496 | tf_op jit(solution)/shard_map/dot_general | solution.py:22
  104.4 18.4 %fusion.6 = bf16[1024,3072]{1,0:T(8,128)(2,1)} fusion(f32[1024,3072]{1,0:T(8,128)} %fusion.25, bf16[3072,768]{1,0:T(8,128)(2,1)} %param.17, bf16[512,768]{1,0:T(8,128)(2,1)} %collective-permute-done.3, bf16[512,768]{1,0:T(8,128)(2,1)S(1)} %copy-done.10, pred[]{:T(512)S(6)} %eq.2), kind=kOutput, calls=%fused_computation.8 | convolution fusion | flops 4901830656 | bytes 25165824 | tf_op jit(solution)/shard_map/dot_general | solution.py:22
  122.9 9.7 %multiply_reduce_fusion = (f32[768]{0:T(1024)}, f32[1024]{0:T(1024)S(1)}, f32[1024,768]{1,0:T(8,128)S(1)}) fusion(f32[1024,768]{1,0:T(8,128)S(1)} %get-tuple-element.39, f32[1024]{0:T(1024)S(1)} %fusion.19, f32[1024]{0:T(1024)S(1)} %broadcast_multiply_fusion, f32[768]{0:T(1024)S(1)} %copy-done.16, bf16[1024,3072]{1,0:T(8,128)(2,1)} %fusion.6, ...), kind=kOutput, calls=%fused_computation.26 | convolution fusion | flops 4837341184 | bytes 17319936 | tf_op jit(solution)/shard_map/dot_general | solution.py:22
  134.1 3.1 fusion.17
  138.4 2.8 fusion.29
  142.0 4.3 convolution_convert_fusion.1.up_ref
  146.3 57.5 %attend_back.1 = (bf16[1024,768]{1,0:T(8,128)(2,1)S(1)}, bf16[1024,768]{1,0:T(8,128)(2,1)S(1)}, bf16[1024,768]{1,0:T(8,128)(2,1)S(1)}) custom-call(s32[4]{0:T(128)S(1)} %and_select_fusion.last, s32[1,1024]{1,0:T(1,128)S(1)} %broadcast_select_fusion.seg_ref, bf16[1024,2304]{1,0:T(8,128)(2,1)} %convolution_convert_fusion.q_ref.k_ref.v_ref, ...), custom_call_target="tpu_custom_call" | custom-call | tf_op jit(solution)/shard_map/attend_back/pallas_call | solution.py:180
  206.3 8.6 %fusion.20 = f32[768,2304]{1,0:T(8,128)} fusion(bf16[1024,2304]{1,0:T(8,128)(2,1)S(1)} %constant_dynamic-update-slice_fusion, f32[768]{0:T(1024)S(1)} %copy-done.27, f32[1024]{0:T(1024)S(1)} %copy-done.20, f32[1024]{0:T(1024)S(1)} %copy-done.18, bf16[512,768]{1,0:T(8,128)(2,1)} %collective-permute-done, bf16[512,768]{1,0:T(8,128)(2,1)S(1)} %copy-done.8, ...), kind=kOutput, calls=%fused_computation.74 | convolution fusion | flops 3634888704 | bytes 13380609 | tf_op jit(solution)/shard_map/dot_general | solution.py:22
  215.1 15.9 %fusion.26 = f32[3072,768]{1,0:T(8,128)} fusion(bf16[512,768]{1,0:T(8,128)(2,1)} %collective-permute-done.3, bf16[512,768]{1,0:T(8,128)(2,1)} %get-tuple-element.30, pred[]{:T(512)S(6)} %eq.2, f32[1024,3072]{1,0:T(8,128)} %fusion.25), kind=kOutput, calls=%fused_computation.78 | convolution fusion | flops 4867227648 | bytes 23592960 | tf_op jit(solution)/shard_map/dot_general | solution.py:22
  231.0 10.9 %fusion.24 = f32[768,3072]{1,0:T(8,128)} fusion(bf16[1024,3072]{1,0:T(8,128)(2,1)} %fusion.6, f32[1024,768]{1,0:T(8,128)} %copy-done.4, f32[768]{0:T(1024)S(1)} %copy-done.16, f32[1024]{0:T(1024)S(1)} %fusion.19, f32[1024]{0:T(1024)S(1)} %broadcast_multiply_fusion), kind=kOutput, calls=%fused_computation.76 | convolution fusion | flops 4834983936 | bytes 18885632 | tf_op jit(solution)/shard_map/dot_general | solution.py:22
  241.9 12.1 %add_convert_fusion.1 = bf16[1024,768]{1,0:T(8,128)(2,1)S(1)} fusion(f32[1024,768]{1,0:T(8,128)} %copy-done.4, bf16[3072,768]{1,0:T(8,128)(2,1)} %param.17, f32[1024,3072]{1,0:T(8,128)} %fusion.25), kind=kOutput, calls=%fused_computation.30 | convolution fusion | flops 4861722624 | bytes 22020096 | tf_op jit(solution)/shard_map/dot_general | solution.py:22
  257.4 7.2 %fusion.16 = (f32[1024]{0:T(1024)S(1)}, f32[1024,768]{1,0:T(8,128)S(1)}) fusion(f32[768]{0:T(1024)S(1)} %copy-done.28, f32[1024]{0:T(1024)S(1)} %copy-done.18, bf16[512,768]{1,0:T(8,128)(2,1)S(1)} %copy-done.9, bf16[512,768]{1,0:T(8,128)(2,1)} %collective-permute-done, pred[]{:T(512)S(6)} %eq.2, bf16[1024,2304]{1,0:T(8,128)(2,1)} %copy-done.15, ...), kind=kOutput, calls=%fused_computation.25 | convolution fusion | flops 3634887680 | bytes 12987393 | tf_op jit(solution)/shard_map/dot_general | solution.py:22
  264.6 4.4 fusion.14
  269.1 5.1 add_convert_fusion
  275.8 54.9 %all-reduce.2 = (f32[768]{0:T(1024)S(1)}, f32[768]{0:T(1024)S(1)}) all-reduce(f32[768]{0:T(1024)S(1)} %get-tuple-element.20, f32[768]{0:T(1024)S(1)} %copy-done.31), channel_id=6, replica_groups=mesh['dp'=16,'seq'=2] {'dp','seq'}, use_global_device_ids=true, to_apply=%region_15.16.clone | all-reduce | flops 1536 | bytes 12288
  331.8 3.6 maximum_select_fusion.1
  338.3 30.3 %reduce-scatter.5.cloned.1.call-done = f32[24,2304]{1,0:T(8,128)} async-done(((f32[768,2304]{1,0:T(8,128)}), f32[24,2304]{1,0:T(8,128)}) %reduce-scatter.5.cloned.1.call-update) | async-done | bytes 221200 | tf_op jit(solution)/shard_map/reduce_scatter | solution.py:260
  368.6 141.3 %reduce-scatter.11.cloned.1.call-done = f32[96,768]{1,0:T(8,128)} async-done(((f32[3072,768]{1,0:T(8,128)}), f32[96,768]{1,0:T(8,128)}) %reduce-scatter.11.cloned.1.call-update) | async-done | bytes 294928 | tf_op jit(solution)/shard_map/reduce_scatter | solution.py:260
  509.9 142.0 %reduce-scatter.9.cloned.1.call-done = f32[24,3072]{1,0:T(8,128)} async-done(((f32[768,3072]{1,0:T(8,128)}), f32[24,3072]{1,0:T(8,128)}) %reduce-scatter.9.cloned.1.call-update) | async-done | bytes 294928 | tf_op jit(solution)/shard_map/reduce_scatter | solution.py:260
  (118 shorter events, 31.5 us)
Async XLA Ops:
  7.2 34.3 %copy-start = (bf16[768,2304]{1,0:T(8,128)(2,1)S(1)}, bf16[768,2304]{1,0:T(8,128)(2,1)}, u32[]{:S(2)}) copy-start(bf16[768,2304]{1,0:T(8,128)(2,1)} %param.13) | copy-start | bytes 10616836
  7.2 5.8 copy-start.30
  7.2 331.1 %reduce-scatter.7.cloned.1.call-start = ((), (), s32[]{:S(2)}) async-start(), calls=%async_computation.5 | async-start | bytes 2433024 | tf_op jit(solution)/shard_map/reduce_scatter | solution.py:260
  7.2 5.9 copy-start.13
  10.0 25.0 %collective-permute-start = (bf16[512,768]{1,0:T(8,128)(2,1)}, bf16[512,768]{1,0:T(8,128)(2,1)}, u32[]{:S(2)}, u32[]{:S(2)}) collective-permute-start(bf16[512,768]{1,0:T(8,128)(2,1)} %get-tuple-element.34), channel_id=1, source_target_pairs={{0,1},{1,0},{2,3},{3,2},{4,5},{5,4},{6,7},{7,6},{8,9},{9,8},{10,11... | collective-permute-start | bytes 2359304 | tf_op jit(solution)/shard_map/ppermute | solution.py:207
  13.0 28.4 %copy-start.26 = (f32[768]{0:T(1024)S(1)}, f32[768]{0:T(1024)}, u32[]{:S(2)}) copy-start(f32[768]{0:T(1024)} %param.12) | copy-start | bytes 9220
  13.0 18.7 %collective-permute-start.1 = (s32[512]{0:T(512)S(1)}, s32[512]{0:T(512)S(1)}, u32[]{:S(2)}, u32[]{:S(2)}) collective-permute-start(s32[512]{0:T(512)S(1)} %bitcast.39), channel_id=1, source_target_pairs={{0,1},{1,0},{2,3},{3,2},{4,5},{5,4},{6,7},{7,6},{8,9},{9,8},{10,11... | collective-permute-start | bytes 6152 | tf_op jit(solution)/shard_map/ppermute | solution.py:207
  14.4 90.1 %collective-permute-start.3 = (bf16[512,768]{1,0:T(8,128)(2,1)}, bf16[512,768]{1,0:T(8,128)(2,1)}, u32[]{:S(2)}, u32[]{:S(2)}) collective-permute-start(bf16[512,768]{1,0:T(8,128)(2,1)} %get-tuple-element.31), channel_id=1, source_target_pairs={{0,1},{1,0},{2,3},{3,2},{4,5},{5,4},{6,7},{7,6},{8,9},{9,8},{10,11... | collective-permute-start | bytes 2359304 | tf_op jit(solution)/shard_map/ppermute | solution.py:207
  32.9 8.6 %copy-start.7 = (bf16[512,768]{1,0:T(8,128)(2,1)S(1)}, bf16[512,768]{1,0:T(8,128)(2,1)}, u32[]{:S(2)}) copy-start(bf16[512,768]{1,0:T(8,128)(2,1)} %get-tuple-element.35) | copy-start | bytes 2359300
  49.2 42.7 %copy-start.32 = (bf16[768,768]{1,0:T(8,128)(2,1)S(1)}, bf16[768,768]{1,0:T(8,128)(2,1)}, u32[]{:S(2)}) copy-start(bf16[768,768]{1,0:T(8,128)(2,1)} %param.14) | copy-start | bytes 3538948
  91.9 45.4 %copy-start.1 = (bf16[1024,768]{1,0:T(8,128)(2,1)}, bf16[1024,768]{1,0:T(8,128)(2,1)S(1)}, u32[]{:S(2)}) copy-start(bf16[1024,768]{1,0:T(8,128)(2,1)S(1)} %get-tuple-element.13.o_ref) | copy-start | bytes 4718596
  95.5 37.1 %copy-start.4 = (f32[1024,768]{1,0:T(8,128)}, f32[1024,768]{1,0:T(8,128)S(1)}, u32[]{:S(2)}) copy-start(f32[1024,768]{1,0:T(8,128)S(1)} %get-tuple-element.39) | copy-start | bytes 9437188
  96.2 8.3 %copy-start.10 = (bf16[512,768]{1,0:T(8,128)(2,1)S(1)}, bf16[512,768]{1,0:T(8,128)(2,1)}, u32[]{:S(2)}) copy-start(bf16[512,768]{1,0:T(8,128)(2,1)} %get-tuple-element.30) | copy-start | bytes 2359300
  141.3 227.3 %reduce-scatter.5.cloned.1.call-start = ((), (), s32[]{:S(2)}) async-start(), calls=%async_computation.4 | async-start | bytes 7299072 | tf_op jit(solution)/shard_map/reduce_scatter | solution.py:260
  215.0 294.9 %reduce-scatter.11.cloned.1.call-start = ((), (), s32[]{:S(2)}) async-start(), calls=%async_computation.7 | async-start | bytes 9732096 | tf_op jit(solution)/shard_map/reduce_scatter | solution.py:260
  231.0 420.9 %reduce-scatter.9.cloned.1.call-start = ((), (), s32[]{:S(2)}) async-start(), calls=%async_computation.6 | async-start | bytes 9732096 | tf_op jit(solution)/shard_map/reduce_scatter | solution.py:260
  255.3 9.3 %copy-start.23 = (f32[1024]{0:T(1024)S(1)}, f32[1024]{0:T(1024)}, u32[]{:S(2)}) copy-start(f32[1024]{0:T(1024)} %copy-done.22) | copy-start | bytes 12292
  255.3 9.3 %copy-start.21 = (f32[1024]{0:T(1024)S(1)}, f32[1024]{0:T(1024)}, u32[]{:S(2)}) copy-start(f32[1024]{0:T(1024)} %copy-done.19) | copy-start | bytes 12292
  255.3 76.5 %collective-permute-start.2 = (bf16[512,768]{1,0:T(8,128)(2,1)}, bf16[512,768]{1,0:T(8,128)(2,1)}, u32[]{:S(2)}, u32[]{:S(2)}) collective-permute-start(bf16[512,768]{1,0:T(8,128)(2,1)} %get-tuple-element.33), channel_id=1, source_target_pairs={{0,1},{1,0},{2,3},{3,2},{4,5},{5,4},{6,7},{7,6},{8,9},{9,8},{10,11... | collective-permute-start | bytes 2359304 | tf_op jit(solution)/shard_map/ppermute | solution.py:207
  264.5 4.5 copy-start.6
  264.6 4.5 copy-start.11
  264.6 4.5 copy-start.25
  275.5 60.0 %collective-permute-start.4 = (bf16[512,768]{1,0:T(8,128)(2,1)}, bf16[512,768]{1,0:T(8,128)(2,1)}, u32[]{:S(2)}, u32[]{:S(2)}) collective-permute-start(bf16[512,768]{1,0:T(8,128)(2,1)} %get-tuple-element.29), channel_id=1, source_target_pairs={{0,1},{1,0},{2,3},{3,2},{4,5},{5,4},{6,7},{7,6},{8,9},{9,8},{10,11... | collective-permute-start | bytes 2359304 | tf_op jit(solution)/shard_map/ppermute | solution.py:207
  330.6 4.8 copy-start.12
  (20 other events, 49.5 us)
Sparse Core Ops, SparseCore 0:
  141.4 101.8 reduce-scatter.6
  250.5 118.0 reduce-scatter.4
  375.0 134.8 reduce-scatter.10
  517.2 134.5 reduce-scatter.8

commit v2 on v1

v2 whole, which is shorter than its diff:
```python
import functools

import jax
import jax.numpy as jnp
from jax import lax
from jax.experimental import pallas as pl
from jax.experimental.pallas import tpu as pltpu
from jax.sharding import PartitionSpec as P

HEAD_DIM = 32
GROUP = 8
LANES = GROUP * HEAD_DIM
SMALL = 128
PART = 3 * SMALL
GRAIN = 128
masked_score = -1e30
epsilon = 1e-05
SCALE = HEAD_DIM ** (-0.5)
SCALE2 = SCALE * 1.4426950408889634
NT = (((1,), (1,)), ((), ()))
NN = (((1,), (0,)), ((), ()))


def mm(a, b, dims=NN):
    return lax.dot_general(a, b, dims, preferred_element_type=jnp.float32)


def attend_kernel(first, seg_ref, q_ref, k_ref, v_ref, o_ref, lse_ref, bias, total, *, bq, unroll):
    i, g = pl.program_id(0), pl.program_id(1)
    length = k_ref.shape[0]
    start = first[i]
    lane = lax.div(lax.broadcasted_iota(jnp.int32, (1, LANES), 1), HEAD_DIM)
    lane_head = lax.broadcasted_iota(jnp.int32, (1, 128), 1)

    def span(width):
        begin = pl.multiple_of(start * GRAIN, GRAIN)

        @pl.when(g == 0)
        def _():
            seg_q = jnp.transpose(jnp.broadcast_to(seg_ref[0:1, pl.ds(pl.multiple_of(i * bq, bq), bq)], (128, bq)))[:, 0:1]
            place_q = i * bq + lax.broadcasted_iota(jnp.int32, (bq, width), 0)
            place_k = begin + lax.broadcasted_iota(jnp.int32, (bq, width), 1)
            allowed = (place_k <= place_q) & (seg_q == seg_ref[0:1, pl.ds(begin, width)])
            bias[:, :width] = jnp.where(allowed, 0.0, masked_score)

        total[...] = jnp.zeros_like(total)

        def head(h, logs):
            query = jnp.where(lane == h, q_ref[...], jnp.zeros((), jnp.bfloat16))
            s = mm(query, k_ref[pl.ds(begin, width), :], NT) * SCALE2 + bias[:, :width]
            top = jnp.max(s, axis=-1, keepdims=True)
            e = jnp.exp2(s - top)
            row = jnp.sum(e, axis=-1, keepdims=True)
            out = mm(e.astype(jnp.bfloat16), v_ref[pl.ds(begin, width), :])
            total[...] = jnp.where(lane == h, out / row, total[...])
            place = jnp.where(h < GROUP // 2, h, h + GROUP // 2)
            return jnp.where(lane_head == place, top + jnp.log2(row), logs)

        logs = lax.fori_loop(0, GROUP, head, jnp.zeros((bq, 128), jnp.float32), unroll=unroll)
        o_ref[...] = total[...].astype(o_ref.dtype)
        lse_ref[...] = jnp.transpose(logs)[:2 * GROUP]

    blocks = (i + 1) * (bq // GRAIN) - start
    for count in range(bq // GRAIN, length // GRAIN + 1):
        pl.when(blocks == count)(functools.partial(span, count * GRAIN))


def attend(first, seg, proj, bq=256, unroll=8):
    length, width = proj.shape
    groups = width // 3 // LANES
    grid_spec = pltpu.PrefetchScalarGridSpec(
        num_scalar_prefetch=1,
        grid=(length // bq, groups),
        in_specs=[
            pl.BlockSpec((1, length), lambda i, g, *_: (0, 0)),
            pl.BlockSpec((bq, LANES), lambda i, g, *_: (i, g)),
            pl.BlockSpec((length, LANES), lambda i, g, *_: (0, groups + g)),
            pl.BlockSpec((length, LANES), lambda i, g, *_: (0, 2 * groups + g)),
        ],
        out_specs=[
            pl.BlockSpec((bq, LANES), lambda i, g, *_: (i, g)),
            pl.BlockSpec((2 * GROUP, bq), lambda i, g, *_: (g, i)),
        ],
        scratch_shapes=[pltpu.VMEM((bq, length), jnp.float32), pltpu.VMEM((bq, LANES), jnp.float32)],
    )
    return pl.pallas_call(
        functools.partial(attend_kernel, bq=bq, unroll=unroll),
        grid_spec=grid_spec,
        out_shape=[
            jax.ShapeDtypeStruct((length, width // 3), jnp.bfloat16),
            jax.ShapeDtypeStruct((groups * 2 * GROUP, length), jnp.float32),
        ],
        compiler_params=pltpu.CompilerParams(vmem_limit_bytes=60 << 20),
        cost_estimate=pl.CostEstimate(flops=28 << 30, bytes_accessed=8 << 20, transcendentals=24 * length * length),
        name="attend",
    )(first, seg, proj, proj, proj)


def attend_back_kernel(last, seg_ref, q_ref, k_ref, v_ref, up_ref, o_ref, lse_ref, low_t_ref, *refs, bk):
    *riders, gq_ref, gk_ref, gv_ref, keep_ref, send_ref, bias, inner, key_t, value_t, q_t, up_t, gq_t, gk, gv = refs
    g, j = pl.program_id(0), pl.program_id(1)
    length, lanes = q_ref.shape
    heads = lanes // HEAD_DIM
    lane = lax.div(lax.broadcasted_iota(jnp.int32, (1, lanes), 1), HEAD_DIM)

    @pl.when(j == 0)
    def _():
        gq_t[...] = jnp.zeros_like(gq_t)
        q_t[...] = jnp.transpose(q_ref[...])
        up_t[...] = jnp.transpose(up_ref[...])
        pick = (lax.div(lax.broadcasted_iota(jnp.int32, (8, lanes), 1), HEAD_DIM)
                == lax.broadcasted_iota(jnp.int32, (8, lanes), 0)).astype(jnp.float32)
        product = up_ref[...].astype(jnp.float32) * o_ref[...].astype(jnp.float32)
        inner[...] = lax.dot_general(pick, product, NT, precision=lax.Precision.HIGHEST,
                                     preferred_element_type=jnp.float32)

    key_t[...] = jnp.transpose(k_ref[...])
    value_t[...] = jnp.transpose(v_ref[...])

    def span(width):
        begin = pl.multiple_of(j * bk, bk)
        here = pl.ds(begin, width)
        seg_k = jnp.transpose(jnp.broadcast_to(seg_ref[0:1, pl.ds(begin, bk)], (128, bk)))[:, 0:1]
        place_k = lax.broadcasted_iota(jnp.int32, (bk, width), 0)
        place_q = lax.broadcasted_iota(jnp.int32, (bk, width), 1)
        allowed = (place_k <= place_q) & (seg_k == seg_ref[0:1, here])
        bias[:, :width] = jnp.where(allowed, 0.0, masked_score)
        for h in range(heads):
            rows = slice(h * HEAD_DIM, (h + 1) * HEAD_DIM)
            key, value = jnp.transpose(key_t[rows, :]), jnp.transpose(value_t[rows, :])
            s = mm(key, q_t[rows, here]) * SCALE2 + (bias[:, :width] - lse_ref[h:h + 1, here])
            p = jnp.exp2(s)
            dp = mm(value, up_t[rows, here])
            ds = (p * (dp - inner[h:h + 1, here])).astype(jnp.bfloat16)
            grad_v = mm(p.astype(jnp.bfloat16), up_ref[here, :])
            grad_k = mm(ds, q_ref[here, :])
            gv[...] = jnp.where(lane == h, grad_v, gv[...]) if h else grad_v
            gk[...] = jnp.where(lane == h, grad_k, gk[...]) if h else grad_k
            gq_t[rows, here] += mm(key_t[rows, :], ds)

    blocks = last[j] - j * (bk // GRAIN)
    for count in range(bk // GRAIN, length // GRAIN + 1):
        pl.when(blocks == count)(functools.partial(span, count * GRAIN))

    here = pl.ds(pl.multiple_of(j * bk, bk), bk)
    gk_ref[here, :] = (gk[...] * SCALE).astype(gk_ref.dtype)
    gv_ref[here, :] = gv[...].astype(gv_ref.dtype)

    @pl.when(j == pl.num_programs(1) - 1)
    def _():
        gq_ref[...] = jnp.transpose((gq_t[...] * SCALE).astype(gq_ref.dtype))
        joined = jnp.concatenate([gq_ref[...], gk_ref[...], gv_ref[...]], axis=1)
        cut(mm(low_t_ref[...], joined), keep_ref, send_ref, g)

    if riders:
        @pl.when((g == 0) & (j == 0))
        def _():
            extra = riders[0].shape[0]
            for rider, target in zip(riders, (keep_ref, send_ref)):
                target[-extra:] = rider[...]


def attend_back(begin, count, last, seg, proj, up, o, lse, low_t, shards, riders=(), bk=256):
    length, width = proj.shape
    groups = width // 3 // SMALL
    half = width // 6
    group = lambda g: g + begin
    whole = lambda offset: pl.BlockSpec((length, SMALL), lambda g, j, *_: (0, offset + group(g)))
    block = lambda offset: pl.BlockSpec((bk, SMALL), lambda g, j, *_: (j, offset + group(g)))
    fixed = lambda *shape: pl.BlockSpec(shape, lambda g, j, *_: (0, 0), pipeline_mode=pl.Buffered(1))
    out = pl.BlockSpec((length, SMALL), lambda g, j, *_: (0, g))
    rows = 2 * half // shards
    piece = (half, PART) if rows % 8 else (shards // 2, rows, PART)
    lead = count + (riders[0].shape[0] if riders else 0)
    all_of = lambda *size: pl.BlockSpec(size, lambda g, j, *_: (0,) * len(size), pipeline_mode=pl.Buffered(1))
    split = all_of(lead, *piece)
    grid_spec = pltpu.PrefetchScalarGridSpec(
        num_scalar_prefetch=1,
        grid=(count, length // bk),
        in_specs=[
            fixed(1, length),
            whole(0),
            block(groups),
            block(2 * groups),
            whole(0),
            whole(0),
            pl.BlockSpec((8, length), lambda g, j, *_: (group(g), 0)),
            fixed(2 * half, length),
            *[all_of(*rider.shape) for rider in riders],
        ],
        out_specs=[out, out, out, split, split],
        scratch_shapes=[
            pltpu.VMEM((bk, length), jnp.float32),
            pltpu.VMEM((8, length), jnp.float32),
            pltpu.VMEM((SMALL, bk), jnp.bfloat16),
            pltpu.VMEM((SMALL, bk), jnp.bfloat16),
            pltpu.VMEM((SMALL, length), jnp.bfloat16),
            pltpu.VMEM((SMALL, length), jnp.bfloat16),
            pltpu.VMEM((SMALL, length), jnp.float32),
            pltpu.VMEM((bk, SMALL), jnp.float32),
            pltpu.VMEM((bk, SMALL), jnp.float32),
        ],
    )
    heads = jax.ShapeDtypeStruct((length, count * SMALL), jnp.bfloat16)
    parts = jax.ShapeDtypeStruct((lead, *piece), jnp.bfloat16)
    return pl.pallas_call(
        functools.partial(attend_back_kernel, bk=bk),
        grid_spec=grid_spec,
        out_shape=[heads, heads, heads, parts, parts],
        compiler_params=pltpu.CompilerParams(vmem_limit_bytes=60 << 20),
        cost_estimate=pl.CostEstimate(flops=(count * 10) << 30, bytes_accessed=8 << 20, transcendentals=count * 4 * length * length),
        name="attend_back",
    )(last, seg, proj, proj, proj, up, o, lse, low_t, *riders)


def bounds(seg, bq, bk):
    row = seg[0]
    first = jnp.sum(row[None, :] < row[::bq][:, None], axis=1) // GRAIN
    last = (jnp.sum(row[None, :] <= row[bk - 1::bk][:, None], axis=1) + GRAIN - 1) // GRAIN
    return first.astype(jnp.int32), last.astype(jnp.int32)


def gelu_pair(u):
    c = 0.7978845608028654
    square = u * u
    t = jnp.tanh(u * (c + (c * 0.044715) * square))
    half = 0.5 * t + 0.5
    slope = half + (0.5 * u) * (1.0 - t * t) * (c + (3 * c * 0.044715) * square)
    return u * half, slope


def row_stats(values):
    mean = jnp.mean(values, axis=-1, keepdims=True)
    centred = values - mean
    return mean, lax.rsqrt(jnp.mean(centred * centred, axis=-1, keepdims=True) + epsilon)


def norm_back(values, gain, upstream):
    mean, rate = row_stats(values)
    unit = (values - mean) * rate
    inner = upstream * gain
    level = jnp.mean(inner, axis=-1, keepdims=True)
    along = jnp.mean(inner * unit, axis=-1, keepdims=True)
    return rate * (inner - level - unit * along)


def shard_at(place, core_rel, q_rel):
    core, q = place[0] ^ core_rel, place[1] ^ q_rel
    return ((q >> 1) * 2 + core) * 2 + (q & 1)


def arranged(place, rows, source, target, shards):
    if rows % 8:
        target[...] = source[...].astype(target.dtype)
        return
    chips = shards // 2
    for at in range(0, shards, 2):
        pair = [
            source[pl.ds(pl.multiple_of(shard_at(place, b // chips, b % chips) * rows, 8), rows), :]
            for b in (at, at + 1)
        ]
        target[at * rows:(at + 2) * rows, :] = jnp.concatenate(pair).astype(target.dtype)


def cut(grad, keep, send, first):
    half = grad.shape[0] // 2
    for at in range(grad.shape[1] // PART):
        block = grad[:, at * PART:(at + 1) * PART]
        if len(keep.shape) == 3:
            keep[first + at] = block[:half].astype(keep.dtype)
            send[first + at] = block[half:].astype(send.dtype)
        else:
            chips, rows = keep.shape[1:3]
            for q in range(chips):
                keep[first + at, q] = block[q * rows:(q + 1) * rows].astype(keep.dtype)
                send[first + at, q] = block[half + q * rows:half + (q + 1) * rows].astype(send.dtype)


def before_kernel(place, x_ref, gain_ref, w_ref, *refs, shards, block):
    proj_ref, low_t_ref, low, flat = refs[-4:]
    length, width = x_ref.shape

    @pl.when(pl.program_id(0) == 0)
    def _():
        for at in range(0, length, block):
            at = slice(at, at + block)
            values = x_ref[at, :].astype(jnp.float32)
            mean, rate = row_stats(values)
            normed = (values - mean) * rate * gain_ref[...]
            low[at, :] = normed.astype(jnp.bfloat16)
            flat[:, at] = jnp.transpose(normed)
        arranged(place, width // shards, flat, low_t_ref, shards)

    proj_ref[...] = mm(low[...], w_ref[...]).astype(jnp.bfloat16)


def before(place, x, gain, w, shards, so_far=(), chunk=768, block=256):
    length, width = x.shape
    columns = w.shape[1]
    whole = lambda *shape: pl.BlockSpec(shape, lambda c, *_: (0, 0), pipeline_mode=pl.Buffered(1))
    grid_spec = pltpu.PrefetchScalarGridSpec(
        num_scalar_prefetch=1,
        grid=(columns // chunk,),
        in_specs=[whole(length, width), whole(1, width), pl.BlockSpec((width, chunk), lambda c, *_: (0, c))]
        + [pl.BlockSpec(memory_space=pl.ANY)] * len(so_far),
        out_specs=[
            pl.BlockSpec((length, chunk), lambda c, place: (place[2], c)),
            pl.BlockSpec((width, length), lambda c, place: (0, place[2])),
        ],
        scratch_shapes=[pltpu.VMEM((length, width), jnp.bfloat16), pltpu.VMEM((width, length), jnp.float32)],
    )
    return pl.pallas_call(
        functools.partial(before_kernel, shards=shards, block=block),
        grid_spec=grid_spec,
        out_shape=[
            jax.ShapeDtypeStruct((2 * length, columns), jnp.bfloat16),
            jax.ShapeDtypeStruct((width, 2 * length), jnp.bfloat16),
        ],
        input_output_aliases={4 + at: at for at in range(len(so_far))},
        compiler_params=pltpu.CompilerParams(vmem_limit_bytes=60 << 20),
        cost_estimate=pl.CostEstimate(flops=2 * length * width * columns, bytes_accessed=12 << 20, transcendentals=length),
        name="before",
    )(place, x, gain, w, *so_far)


def middle_kernel(place, x_kept, x_other, o_ref, gy_kept, gy_other, w_out_ref, gain_ref, w_up_ref, w_down_ref,
                  out_kept, out_other, gx_ref, go_ref, keep_up, send_up, keep_down, send_down, keep_out, send_out,
                  gy, x1, low, low_t, total, back, flat, part, *, shards, block):
    c = pl.program_id(0)
    length, width = o_ref.shape
    chunk = w_down_ref.shape[0]
    pieces = [slice(at, at + block) for at in range(0, length, block)]
    rows = width // shards
    half, window = width // 2, length // 2
    kept = pl.ds(pl.multiple_of(place[2] * window, window), window)
    other = pl.ds(pl.multiple_of((1 - place[2]) * window, window), window)

    @pl.when(c == 0)
    def _():
        gy[kept, :] = gy_kept[...]
        gy[other, :] = gy_other[...]
        x1[kept, :] = x_kept[...].astype(jnp.float32)
        x1[other, :] = x_other[...].astype(jnp.float32)
        for at in pieces:
            values = x1[at, :] + mm(o_ref[at, :], w_out_ref[...])
            x1[at, :] = values
            mean, rate = row_stats(values)
            normed = (values - mean) * rate * gain_ref[...]
            low[at, :] = normed.astype(jnp.bfloat16)
            flat[:, at] = jnp.transpose(normed)
            total[at, :] = values
            back[at, :] = jnp.zeros_like(values)
        arranged(place, rows, flat, low_t, shards)

    lifted, slopes = [], []
    for at in pieces:
        a, slope = gelu_pair(mm(low[at, :], w_up_ref[...]))
        a = a.astype(jnp.bfloat16)
        gu = (mm(gy[at, :], w_down_ref[...], NT) * slope).astype(jnp.bfloat16)
        total[at, :] += mm(a, w_down_ref[...])
        back[at, :] += mm(gu, w_up_ref[...], NT)
        lifted.append(jnp.transpose(a))
        slopes.append(gu)
    cut(mm(low_t[...], jnp.concatenate(slopes, axis=0)), keep_up, send_up, 0)
    grad_down = mm(jnp.concatenate(lifted, axis=1), gy[...])
    if rows % 8:
        for at in range(width // PART):
            for target, begin in ((keep_down, 0), (send_down, chunk // 2)):
                piece = grad_down[begin:begin + chunk // 2, at * PART:(at + 1) * PART]
                target[at] = piece.astype(jnp.bfloat16)
    else:
        part[...] = grad_down
        for rel, target in enumerate((keep_down, send_down)):
            for q_rel in range(4):
                q = (place[1] ^ q_rel) & 3
                source = (((q >> 1) * 2 + (place[0] ^ rel)) * 2 + (q & 1)) * 4 * rows
                for sub in range(4):
                    source_rows = pl.ds(pl.multiple_of(source + sub * rows, 8), rows)
                    for at in range(width // PART):
                        piece = part[source_rows, at * PART:(at + 1) * PART]
                        target[4 * at + sub, q_rel] = piece.astype(jnp.bfloat16)

    @pl.when(c == pl.num_programs(0) - 1)
    def _():
        branch = []
        out_kept[...] = total[kept, :].astype(jnp.bfloat16)
        out_other[...] = total[other, :].astype(jnp.bfloat16)
        for at in pieces:
            grad = gy[at, :].astype(jnp.float32) + norm_back(x1[at, :], gain_ref[...], back[at, :])
            gx_ref[at, :] = grad
            grad = grad.astype(jnp.bfloat16)
            branch.append(grad)
            go_ref[at, :] = mm(grad, w_out_ref[...], NT).astype(jnp.bfloat16)
            flat[:, at] = jnp.transpose(o_ref[at, :].astype(jnp.float32))
        arranged(place, rows, flat, low_t, shards)
        cut(mm(low_t[...], jnp.concatenate(branch, axis=0)), keep_out, send_out, 0)


def middle(place, x, o, gy, w_out, gain, w_up, w_down, shards, block=256):
    length, width = o.shape
    lift = w_up.shape[1]
    steps = 4
    chunk = lift // steps
    half, window = width // 2, length // 2
    at = (lambda c, place: c) if (width // shards) % 8 else (lambda c, place: c ^ (place[1] >> 2))
    whole = lambda *shape: pl.BlockSpec(shape, lambda c, *_: (0, 0), pipeline_mode=pl.Buffered(1))
    out = lambda *shape: pl.BlockSpec(shape, lambda c, *_: (0,) * len(shape), pipeline_mode=pl.Buffered(1))
    shape = jax.ShapeDtypeStruct
    rows = width // shards
    if rows % 8:
        up_shape, down_shape, out_shape = (lift // PART, half, PART), (width // PART, lift // 2, PART), (width // PART, half, PART)
        up = pl.BlockSpec((chunk // PART, half, PART), lambda c, place: (at(c, place), 0, 0))
        down = pl.BlockSpec((width // PART, chunk // 2, PART), lambda c, place: (0, c, 0))
    else:
        piece = (shards // 2, rows, PART)
        up_shape, down_shape, out_shape = (lift // PART, *piece), (lift // PART, *piece), (width // PART, *piece)
        up = pl.BlockSpec((chunk // PART, *piece), lambda c, place: (at(c, place), 0, 0, 0))
        down = pl.BlockSpec((lift // PART, 4, rows, PART), lambda c, place: (0, c, 0, 0))
    bf16 = jnp.bfloat16
    grid_spec = pltpu.PrefetchScalarGridSpec(
        num_scalar_prefetch=1,
        grid=(steps,),
        in_specs=[
            whole(window, width), whole(window, width), whole(length, width), whole(window, width),
            whole(window, width), whole(width, width), whole(1, width),
            pl.BlockSpec((width, chunk), lambda c, place: (0, at(c, place))),
            pl.BlockSpec((chunk, width), lambda c, place: (at(c, place), 0)),
        ],
        out_specs=[
            out(window, width), out(window, width), out(length, width), out(length, width), up, up, down, down,
            out(*out_shape), out(*out_shape),
        ],
        scratch_shapes=[
            pltpu.VMEM((length, width), bf16),
            pltpu.VMEM((length, width), jnp.float32),
            pltpu.VMEM((length, width), bf16),
            pltpu.VMEM((width, length), bf16),
            pltpu.VMEM((length, width), jnp.float32),
            pltpu.VMEM((length, width), jnp.float32),
            pltpu.VMEM((width, length), jnp.float32),
            pltpu.VMEM((chunk, width), jnp.float32),
        ],
    )
    return pl.pallas_call(
        functools.partial(middle_kernel, shards=shards, block=block),
        grid_spec=grid_spec,
        out_shape=[
            shape((window, width), bf16), shape((window, width), bf16),
            shape((length, width), jnp.float32), shape((length, width), bf16),
            *[shape(size, bf16) for size in (up_shape, up_shape, down_shape, down_shape, out_shape, out_shape)],
        ],
        compiler_params=pltpu.CompilerParams(vmem_limit_bytes=60 << 20),
        cost_estimate=pl.CostEstimate(flops=12 * length * width * lift, bytes_accessed=40 << 20, transcendentals=length * lift),
        name="middle",
    )(place, *x, o, *gy, w_out, gain, w_up, w_down)


def after_kernel(place, x_ref, gain_ref, gx_ref, w_ref, *refs):
    out_ref = refs[-1]
    width = x_ref.shape[1]
    back = jnp.zeros(gx_ref.shape, jnp.float32)
    at = 0
    for names in zip(*[iter(refs[:-1])] * 3):
        columns = names[0].shape[1]
        for third, ref in enumerate(names):
            begin = third * width + at
            back += mm(ref[...], w_ref[:, begin:begin + columns], NT)
        at += columns
    values = x_ref[...].astype(jnp.float32)
    out_ref[...] = (gx_ref[...] + norm_back(values, gain_ref[...], back)).astype(out_ref.dtype)


def after(place, x, gain, gx, w, pieces, block=256):
    length, width = x.shape
    steps = length // block
    rows = lambda columns: pl.BlockSpec((block, columns), lambda i, place: (place[2] * steps + i, 0))
    own = pl.BlockSpec((block, width), lambda i, place: (i, 0))
    whole = lambda *shape: pl.BlockSpec(shape, lambda i, place: (0, 0), pipeline_mode=pl.Buffered(1))
    grid_spec = pltpu.PrefetchScalarGridSpec(
        num_scalar_prefetch=1,
        grid=(steps,),
        in_specs=[own, whole(1, width), rows(width), whole(width, w.shape[1])] + [rows(piece.shape[1]) for piece in pieces],
        out_specs=own,
    )
    return pl.pallas_call(
        after_kernel,
        grid_spec=grid_spec,
        out_shape=jax.ShapeDtypeStruct((length, width), jnp.bfloat16),
        compiler_params=pltpu.CompilerParams(vmem_limit_bytes=60 << 20),
        cost_estimate=pl.CostEstimate(flops=6 * length * width * width, bytes_accessed=16 << 20, transcendentals=length),
        name="after",
    )(place, x, gain, gx, w, *pieces)


def swapped(block):
    return lax.ppermute(block, "seq", [(0, 1), (1, 0)])


def split_window(block):
    place = lax.axis_index("seq")
    take = lambda at: lax.dynamic_index_in_dim(block, at, 0, keepdims=False)
    return take(place), take(1 - place)


def joined(kept, other):
    place = lax.axis_index("seq")
    return jnp.where(place == 0, jnp.stack([kept, other]), jnp.stack([other, kept]))


def crossed(block, bits):
    if 0 in bits:
        block = swapped(block)
    step = sum(1 << abs(bit) if bit > 0 else 1 for bit in bits if bit)
    if step:
        block = lax.ppermute(block, "dp", [(i, i ^ step) for i in range(lax.axis_size("dp"))])
    return block


def picks(left, bits, mask):
    rest = [bit for bit in left if bit not in bits]
    found = []
    for number in range(1 << len(rest)):
        value = {bit: (number >> (len(rest) - 1 - at)) & 1 for at, bit in enumerate(rest)}
        value.update({bit: int(bit in mask) for bit in bits})
        found.append(sum(value[bit] << (len(left) - 1 - at) for at, bit in enumerate(left)))
    return found


def masks_of(bits):
    return [tuple(bit for e, bit in enumerate(bits) if number >> e & 1) for number in range(1, 1 << len(bits))]


def combine_kernel(*refs, work, steps):
    for lead, cut_up, terms, targets in work:
        def one(index, carry):
            for count, sources, places, target, offset in targets:
                for at, source in enumerate(sources):
                    total = None
                    for ref, begin in terms:
                        value = refs[ref][begin + index * places + source].astype(jnp.float32)
                        total = value if total is None else total + value
                    refs[target][offset + index * count + at] = total.astype(refs[target].dtype)
            return carry

        if cut_up:
            one(0, 0)
        elif steps > 1:
            @pl.when(pl.program_id(0) == 0)
            def _():
                lax.fori_loop(0, lead, one, 0)
        else:
            lax.fori_loop(0, lead, one, 0)


class Flow:
    def __init__(self, place, keep, send, chips, plan, blocks=0):
        if keep.ndim == 3:
            index = jnp.stack([shard_at(place, rel, q) for rel in range(2) for q in range(chips)])
            lead, half, columns = keep.shape
            both = jnp.stack([array.reshape(lead, max(blocks, 1), -1, columns) for array in (keep, send)], axis=2)
            parts = max(blocks, 1)
            both = both.reshape(lead, 2 * chips, parts, -1, columns)[:, index].transpose(0, 2, 1, 3, 4)
            both = both.reshape(lead * parts, 2 * chips, -1, columns)
            keep, send = both[:, :chips], both[:, chips:]
        self.lead, _, self.rows, self.columns = keep.shape
        self.left = list(reversed(range(chips.bit_length() - 1)))
        self.plan = list(plan)
        self.terms = [(keep.reshape(-1, self.rows, self.columns), 0)]
        self.first = send.reshape(-1, self.rows, self.columns)


def combine(flows, steps):
    inputs, in_specs, out_shapes, out_specs, work, sends = [], [], [], [], [], {}

    def spec(array, per):
        if per:
            return pl.BlockSpec((per, *array.shape[1:]), lambda i: (i, 0, 0))
        return pl.BlockSpec(array.shape, lambda i: (0, 0, 0), pipeline_mode=pl.Buffered(1))

    def place_of(array, per):
        for at, seen in enumerate(inputs):
            if seen is array:
                return at
        inputs.append(array)
        in_specs.append(spec(array, per))
        return len(inputs) - 1

    plans = []
    for flow in flows:
        bits = flow.plan.pop(0)
        places = 1 << len(flow.left)
        count = places >> len(bits)
        cut_up = steps > 1 and flow.lead == steps
        terms = [(place_of(array, cut_up and places), offset) for array, offset in flow.terms]
        kept = picks(flow.left, bits, ())
        plans.append((flow, bits, places, count, cut_up, terms, kept))
    sizes = {}
    for flow, bits, places, count, cut_up, terms, kept in plans:
        for mask in masks_of(bits):
            key = mask if steps == 1 else (mask, id(flow))
            sizes.setdefault(key, []).append((flow, flow.lead * count, cut_up and count, mask))
    outputs = []
    for flow, bits, places, count, cut_up, terms, kept in plans:
        shape = (flow.lead * count, flow.rows, flow.columns)
        outputs.append(jax.ShapeDtypeStruct(shape, jnp.bfloat16 if count > 4 else jnp.float32))
        out_specs.append(spec(outputs[-1], cut_up and count))
    for key, members in sizes.items():
        shape = (sum(size for _, size, _, _ in members), members[0][0].rows, members[0][0].columns)
        outputs.append(jax.ShapeDtypeStruct(shape, jnp.bfloat16))
        out_specs.append(spec(outputs[-1], members[0][2]))
    base = len(inputs)
    for at, (flow, bits, places, count, cut_up, terms, kept) in enumerate(plans):
        targets = [(count, kept, places, base + at, 0)]
        for number, (key, members) in enumerate(sizes.items()):
            offset = 0
            for member, size, _, mask in members:
                if member is flow:
                    targets.append((count, picks(flow.left, bits, mask), places, base + len(plans) + number, offset))
                offset += size
        work.append((flow.lead, cut_up, terms, targets))
    results = pl.pallas_call(
        functools.partial(combine_kernel, work=work, steps=steps),
        grid=(steps,),
        in_specs=in_specs,
        out_specs=out_specs,
        out_shape=outputs,
        compiler_params=pltpu.CompilerParams(vmem_limit_bytes=60 << 20),
        cost_estimate=pl.CostEstimate(flops=1 << 20, bytes_accessed=8 << 20, transcendentals=0),
        name="combine",
    )(*inputs)
    for (flow, bits, *_), kept in zip(plans, results):
        flow.terms = [(kept, 0)]
        flow.left = [bit for bit in flow.left if bit not in bits]
    return [
        (members[0][3], array, [(flow, size) for flow, size, _, _ in members])
        for members, array in zip(sizes.values(), results[len(plans):])
    ]


def leave(flows, value=None, steps=1):
    starting = [flow for flow in flows if flow.plan and flow.first is not None]
    going = [flow for flow in flows if flow.plan and flow.first is None]
    sent = [((-1,), flow.first, [(flow, flow.first.shape[0])]) for flow in starting]
    for flow in starting:
        flow.plan.pop(0)
        flow.first = None
    if going:
        sent = combine(going, steps) + sent
    value, arrays = lax.optimization_barrier((value, [array for _, array, _ in sent]))
    return value, [(crossed(array, mask), members) for array, (mask, _, members) in zip(arrays, sent)]


def arrive(transfers, value=None):
    moved, value = lax.optimization_barrier(([array for array, _ in transfers], value))
    for array, (_, members) in zip(moved, transfers):
        at = 0
        for flow, size in members:
            flow.terms.append((array, at))
            at += size
    return value


def finish_kernel(*refs, work, count):
    inputs, outputs = refs[:count], refs[count:]
    for terms, targets in work:
        for lead, (target, row, column, width, parts) in enumerate(targets):
            total = sum(inputs[ref][offset + lead].astype(jnp.float32) for ref, offset in terms)
            for part in range(parts):
                piece = slice(part * width, (part + 1) * width)
                begin = column + part * (outputs[target].shape[1] // parts if parts > 1 else 0)
                outputs[target][row:row + total.shape[0], begin:begin + width] = total[:, piece]
    for number, source in enumerate((0, 2)):
        weight, gain = inputs[count - 4 + 2 * number], inputs[count - 3 + 2 * number]
        outputs[4 + number][...] = jnp.sum(weight[...] * outputs[source][...], axis=1, keepdims=True) / gain[...]


def finish(up, down, out_and_one, two, three, out_lead, weights):
    inputs, work = [], []

    def place_of(array):
        for at, seen in enumerate(inputs):
            if seen is array:
                return at
        inputs.append(array)
        return len(inputs) - 1

    rows = up.rows
    heads = iter(range(6))
    third = lambda: (0, 0, next(heads) * SMALL, SMALL, 3)
    plans = (
        (up, [(2, 0, lead * PART, PART, 1) for lead in range(up.lead)]),
        (down, [(3, (lead % 4) * rows, (lead // 4) * PART, PART, 1) for lead in range(down.lead)]),
        (out_and_one, [third() for _ in range(out_and_one.lead - out_lead)]
         + [(1, 0, lead * PART, PART, 1) for lead in range(out_lead)]),
        (two, [third() for _ in range(two.lead)]),
        (three, [third() for _ in range(three.lead)]),
    )
    for flow, targets in plans:
        work.append(([(place_of(array), offset) for array, offset in flow.terms], targets))
    inputs += weights
    width = out_lead * PART
    shape = lambda *size: jax.ShapeDtypeStruct(size, jnp.float32)
    return pl.pallas_call(
        functools.partial(finish_kernel, work=work, count=len(inputs)),
        out_shape=[shape(rows, 3 * width), shape(rows, width), shape(rows, up.lead * PART), shape(4 * rows, width),
                   shape(rows, 1), shape(rows, 1)],
        compiler_params=pltpu.CompilerParams(vmem_limit_bytes=60 << 20),
        cost_estimate=pl.CostEstimate(flops=1 << 20, bytes_accessed=4 << 20, transcendentals=0),
        name="finish",
    )(*inputs)


def body(tokens, segments, cotangent, gain_attn, w_qkv, w_out, gain_ffn, w_up, w_down):
    chips = lax.axis_size("dp")
    shards = 2 * chips
    dp, seq = lax.axis_index("dp"), lax.axis_index("seq")
    here = jnp.stack([dp & 1, (dp >> 1) * 2 + seq, seq]).astype(jnp.int32)
    there = jnp.stack([dp & 1, (dp >> 1) * 2 + seq, 1 - seq]).astype(jnp.int32)
    far = tuple(range(2, chips.bit_length() - 1))
    wide = [far[at:at + 2] for at in range(0, len(far), 2)]

    x_kept, x_sent = split_window(tokens)
    seg_kept, seg_sent = split_window(segments)
    gy_kept, gy_sent = split_window(cotangent)
    x_other, seg_other, gy_other = swapped(x_sent), swapped(seg_sent), swapped(gy_sent)
    seg = jnp.where(seq == 0, jnp.concatenate([seg_kept, seg_other]), jnp.concatenate([seg_other, seg_kept]))[None]
    first, last = bounds(seg, 256, 256)
    gain_one, gain_two = gain_attn[None], gain_ffn[None]
    early = before(here, x_kept, gain_one, w_qkv, shards)
    proj, low_t = before(there, x_other, gain_one, w_qkv, shards, early)
    mixture, lse = attend(first, seg, proj)
    out_kept, out_sent, gx, go, keep_up, send_up, keep_down, send_down, keep_out, send_out = middle(
        here, (x_kept, x_other), mixture, (gy_kept, gy_other), w_out, gain_two, w_up, w_down, shards
    )

    core = (-1,)
    later = [(bit,) for bit in far[1:]]
    up = Flow(here, keep_up, send_up, chips, [core, (1,), (0,), *wide])
    down = Flow(here, keep_down, send_down, chips, [core, far[:1], (1,), (0,), *later], 4)
    heads = []

    def heads_back(begin, count, plan, riders=()):
        *grads, keep, send = attend_back(begin, count, last, seg, proj, go, mixture, lse, low_t, shards, riders)
        heads.append(grads)
        return Flow(here, keep, send, chips, [core, *plan])

    (go, out_sent), moving = leave([up, down], (go, out_sent))
    out_other = swapped(out_sent)
    one = heads_back(0, 2, [far[:1], (1,), *later, (0,)], (keep_out, send_out))
    out_other = arrive(moving, out_other)
    (go, out_other), moving = leave([up, down, one], (go, out_other), up.lead)
    two = heads_back(2, 3, [(0,), (1,), *wide])
    arrive(moving)
    go, moving = leave([up, down, one, two], go, up.lead)
    three = heads_back(5, 1, [(0, 1), *wide])
    arrive(moving)
    flows = [up, down, one, two, three]
    gx, moving = leave(flows, gx)
    pieces = [piece for grads in heads for piece in grads]
    other_rows = after(there, x_other, gain_one, gx, w_qkv, pieces)
    other_rows = arrive(moving, other_rows)
    rows_back = swapped(other_rows)
    gx, moving = leave(flows, gx)
    kept_rows = after(here, x_kept, gain_one, gx, w_qkv, pieces)
    while True:
        kept_rows = arrive(moving, kept_rows)
        if not any(flow.plan for flow in flows):
            break
        _, moving = leave(flows)
    begin = shard_at(here, 0, 0) * up.rows
    shard_of = lambda array: lax.dynamic_slice_in_dim(array, begin, up.rows, 0).astype(jnp.float32)
    weights = [shard_of(w_qkv), shard_of(gain_attn)[:, None], shard_of(w_up), shard_of(gain_ffn)[:, None]]
    grad_qkv, grad_out, grad_up, grad_down, grad_gain_attn, grad_gain_ffn = finish(
        up, down, one, two, three, w_out.shape[1] // PART, weights
    )
    return (
        joined(out_kept, out_other),
        joined(kept_rows, rows_back),
        grad_qkv,
        grad_out,
        grad_up,
        grad_down,
        grad_gain_attn[:, 0],
        grad_gain_ffn[:, 0],
    )


def solution(mesh):
    placed = (
        P("dp", "seq", None),
        P("dp", "seq"),
        P("dp", "seq", None),
        P(),
        P(),
        P(),
        P(),
        P(),
        P(),
    )
    return jax.shard_map(
        body,
        mesh=mesh,
        in_specs=placed,
        out_specs=(
            P("dp", "seq", None),
            P("dp", "seq", None),
            P(("dp", "seq"), None),
            P(("dp", "seq"), None),
            P(("dp", "seq"), None),
            P(("dp", "seq"), None),
            P(("dp", "seq")),
            P(("dp", "seq")),
        ),
        check_vma=False,
    )
```

time: 657 us -> 302 us (0.46)
  waiting for transfers between devices: 329 us -> 23.5 us
  Pallas kernels: 100 us -> 213 us
  matrix products: 109 us -> 0 us
  blocking collectives: 54.9 us -> 0 us
  starting transfers between devices: 7.54 us -> 34 us
  other arithmetic: 29.1 us -> 11.2 us
  between operations: 14.5 us -> 1.3 us
    reduce_scatter x4 -> x0, waiting for transfers between devices: 314 us -> none  [body(): lax.psum_scatter(grad, ('dp', 'seq'), scatter_dimension=0, tiled=True)]
    pallas_call x1 -> x14, Pallas kernels: 57.5 us -> 180 us  [the longest x3 69.7 us: attend_back(): pl.pallas_call(functools.partial(attend_back_kernel, bk=bk), grid_spec=gr...]
    dot_general x12 -> x0, matrix products: 109 us -> none  [mm(): return lax.dot_general(a, b, dims, preferred_element_type=jnp.float32)]
    unnamed x1 -> x0, blocking collectives: 54.9 us -> none
    ppermute x0 -> x19, starting transfers between devices: none -> 21.5 us  [crossed(): lax.ppermute(block, 'dp', [(i, i ^ step) for i in range(lax.axis_size('dp...]
    reduce_sum x5 -> x0, other arithmetic: 11.6 us -> none  [the longest x1 4.42 us: norm_gain(): return centred * lax.rsqrt(variance + epsilon) * gain_vector]
    pallas_call x1, Pallas kernels: 42.7 us -> 33.1 us  [attend(): pl.pallas_call(functools.partial(attend_kernel, bq=bq, unroll=unroll), gr...]
    ppermute x0 -> x19, waiting for transfers between devices: none -> 9.05 us  [crossed(): lax.ppermute(block, 'dp', [(i, i ^ step) for i in range(lax.axis_size('dp...]
  transfers between devices with their start and end apart: 9 -> 29, of which waited for: 4 -> 7; matrix products, arithmetic and copies ran while one was open for 17% -> 5% of each run, Pallas kernels for 15% -> 48%
where the time goes in v2:
time: 302 us; the launch traced here: 297 us
  Pallas kernels  213 us (71%)
  starting transfers between devices  34 us (11%)
  waiting for transfers between devices  23.5 us (8%)
  local copies, waits for them, and re-layouts  13.9 us (5%)
  other arithmetic  11.2 us (4%)
    pallas_call x3, Pallas kernels, attend_back(): pl.pallas_call(functools.partial(attend_back_kernel, bk=bk), grid_spec=gr...  69.7 us
    pallas_call x1, Pallas kernels, middle(): pl.pallas_call(functools.partial(middle_kernel, shards=shards, block=bloc...  50.5 us
    pallas_call x1, Pallas kernels, attend(): pl.pallas_call(functools.partial(attend_kernel, bq=bq, unroll=unroll), gr...  33.1 us
    pallas_call x5, Pallas kernels, combine(): pl.pallas_call(functools.partial(combine_kernel, work=work, steps=steps),...  26.9 us
    ppermute x19, starting transfers between devices, crossed(): lax.ppermute(block, 'dp', [(i, i ^ step) for i in range(lax.axis_size('dp...  21.5 us
    pallas_call x2, Pallas kernels, after(): pl.pallas_call(after_kernel, grid_spec=grid_spec, out_shape=jax.ShapeDtyp...  15.4 us
    pallas_call x2, Pallas kernels, before(): pl.pallas_call(functools.partial(before_kernel, shards=shards, block=bloc...  14.7 us
    ppermute x10, waiting for transfers between devices, swapped(): return lax.ppermute(block, 'seq', [(0, 1), (1, 0)])  14.5 us
  transfers between devices with their start and end apart: 29, of which 7 were waited for; matrix products, arithmetic and copies ran while one was open for 5% of the time, Pallas kernels for 48%

profile of v2, /device:TPU:0, one launch (start us, length us, event | category | flops | bytes accessed | tf_op | source)
XLA Modules:
  0.0 297.0 jit_solution(7867024053785827063)
XLA Ops:
  0.7 2.5 dynamic-slice_bitcast_fusion.2
  3.1 3.0 collective-permute-start
  10.5 7.4 %before.2 = (bf16[1024,2304]{1,0:T(8,128)(2,1)}, bf16[768,1024]{1,0:T(8,128)(2,1)}) custom-call(s32[3]{0:T(128)} %get-tuple-element.272.place, bf16[512,768]{1,0:T(8,128)(2,1)} %get-tuple-element.269.x_ref.x_kept, f32[1,768]{1,0:T(1,128)} %broadcast_in_dim.15.gain_ref, bf16[768,2304]{1,0:T(8,128)(2,1)} %w_ref.7), custom_call_target="tpu_custom_call" | custom-call | flops 1811939328 | bytes 12582912 | tf_op jit(solution)/shard_map/before/pallas_call | solution.py:312
  18.5 6.0 %collective-permute-done.1 = s32[512]{0:T(512)S(1)} collective-permute-done((s32[512]{0:T(512)S(1)}, s32[512]{0:T(512)S(1)}, u32[]{:S(2)}, u32[]{:S(2)}) %collective-permute-start.1) | collective-permute-done | bytes 2080 | tf_op jit(solution)/shard_map/ppermute | solution.py:496
  27.0 7.3 %before.3 = (bf16[1024,2304]{1,0:T(8,128)(2,1)}, bf16[768,1024]{1,0:T(8,128)(2,1)}) custom-call(s32[3]{0:T(128)} %get-tuple-element.273.place, bf16[512,768]{1,0:T(8,128)(2,1)} %copy-done, f32[1,768]{1,0:T(1,128)} %broadcast_in_dim.15.gain_ref, bf16[768,2304]{1,0:T(8,128)(2,1)} %w_ref.7, ...), custom_call_target="tpu_custom_call", output_to_operand_aliasing={{0}: (4, {}), {1}: (5, {})} | custom-call | flops 1811939328 | bytes 12582912 | tf_op jit(solution)/shard_map/before/pallas_call | solution.py:312
  34.3 33.1 %attend.1 = (bf16[1024,768]{1,0:T(8,128)(2,1)}, f32[48,1024]{1,0:T(8,128)}) custom-call(s32[4]{0:T(128)} %and_select_fusion.1.first, s32[1,1024]{1,0:T(1,128)} %broadcast_select_fusion.seg_ref, bf16[1024,2304]{1,0:T(8,128)(2,1)} %get-tuple-element.138.q_ref.k_ref.v_ref, bf16[1024,2304]{1,0:T(8,128)(2,1)} %get-tuple-element.138.q_ref.k_ref.v_ref, ...), custom_call_target="tpu_custom_call" | custom-call | flops 30064771072 | bytes 8388608 | tf_op jit(solution)/shard_map/attend/pallas_call | solution.py:86
  68.4 50.5 %middle.1 = (bf16[512,768]{1,0:T(8,128)(2,1)}, bf16[512,768]{1,0:T(8,128)(2,1)}, f32[1024,768]{1,0:T(8,128)}, bf16[1024,768]{1,0:T(8,128)(2,1)}, bf16[8,16,24,38...) custom-call(s32[3]{0:T(128)} %get-tuple-element.272.place, ...), custom_call_target="tpu_custom_call" | custom-call | flops 28991029248 | bytes 41943040 | tf_op jit(solution)/shard_map/middle/pallas_call | solution.py:444
  122.0 24.0 %attend_back.3 = (bf16[1024,256]{1,0:T(8,128)(2,1)}, bf16[1024,256]{1,0:T(8,128)(2,1)}, bf16[1024,256]{1,0:T(8,128)(2,1)}, bf16[4,16,24,384]{3,2,1,0:T(8,128)(2,1)}, bf16[4,16,24,384]{3,2,1,0:T(8,128)(2,1)}) custom-call(s32[4]{0:T(128)} %and_select_fusion.last, s32[1,1024]{1,0:T(1,128)} %broadcast_select_fusion.seg_ref, ...), custom_call_target="tpu_custom_call" | custom-call | flops 21474836480 | bytes 8388608 | tf_op jit(solution)/shard_map/attend_back/pallas_call | solution.py:206
  147.5 7.8 %combine.5 = (bf16[64,24,384]{2,1,0:T(8,128)(2,1)}, bf16[64,24,384]{2,1,0:T(8,128)(2,1)}, bf16[64,24,384]{2,1,0:T(8,128)(2,1)}, bf16[64,24,384]{2,1,0:T(8,128)(2,1)}) custom-call(bf16[128,24,384]{2,1,0:T(8,128)(2,1)} %bitcast.34, bf16[128,24,384]{2,1,0:T(8,128)(2,1)} %copy-done.2, bf16[128,24,384]{2,1,0:T(8,128)(2,1)} %bitcast.35, ...), custom_call_target="tpu_custom_call" | custom-call | flops 1048576 | bytes 8388608 | tf_op jit(solution)/shard_map/combine/pallas_call | solution.py:621
  158.8 32.7 %attend_back.4 = (bf16[1024,384]{1,0:T(8,128)(2,1)}, bf16[1024,384]{1,0:T(8,128)(2,1)}, bf16[1024,384]{1,0:T(8,128)(2,1)}, bf16[3,16,24,384]{3,2,1,0:T(8,128)(2,1)}, bf16[3,16,24,384]{3,2,1,0:T(8,128)(2,1)}) custom-call(s32[4]{0:T(128)} %and_select_fusion.last, s32[1,1024]{1,0:T(1,128)} %broadcast_select_fusion.seg_ref, ...), custom_call_target="tpu_custom_call" | custom-call | flops 32212254720 | bytes 8388608 | tf_op jit(solution)/shard_map/attend_back/pallas_call | solution.py:206
  193.3 8.3 %combine.6 = (f32[32,24,384]{2,1,0:T(8,128)}, f32[32,24,384]{2,1,0:T(8,128)}, bf16[32,24,384]{2,1,0:T(8,128)(2,1)}, bf16[32,24,384]{2,1,0:T(8,128)(2,1)}, bf16[3...) custom-call(bf16[64,24,384]{2,1,0:T(8,128)(2,1)} %get-tuple-element.162.refs_0_, bf16[64,24,384]{2,1,0:T(8,128)(2,1)} %copy-done.5, ...), custom_call_target="tpu_custom_call" | custom-call | flops 1048576 | bytes 8388608 | tf_op jit(solution)/shard_map/combine/pallas_call | solution.py:621
  204.7 13.0 %attend_back.5 = (bf16[1024,128]{1,0:T(8,128)(2,1)}, bf16[1024,128]{1,0:T(8,128)(2,1)}, bf16[1024,128]{1,0:T(8,128)(2,1)}, bf16[1,16,24,384]{3,2,1,0:T(8,128)(2,1)}, bf16[1,16,24,384]{3,2,1,0:T(8,128)(2,1)}) custom-call(s32[4]{0:T(128)} %and_select_fusion.last, s32[1,1024]{1,0:T(1,128)} %broadcast_select_fusion.seg_ref, ...), custom_call_target="tpu_custom_call" | custom-call | flops 10737418240 | bytes 8388608 | tf_op jit(solution)/shard_map/attend_back/pallas_call | solution.py:206
  217.8 2.4 collective-permute-done.11.refs_5_
  221.3 5.2 %combine.7 = (f32[8,24,384]{2,1,0:T(8,128)}, f32[16,24,384]{2,1,0:T(8,128)}, f32[16,24,384]{2,1,0:T(8,128)}, bf16[24,24,384]{2,1,0:T(8,128)(2,1)}, bf16[8,24,384...) custom-call(f32[32,24,384]{2,1,0:T(8,128)} %get-tuple-element.171.re, ...), custom_call_target="tpu_custom_call" | custom-call | flops 1048576 | bytes 8388608 | tf_op jit(solution)/shard_map/combine/pallas_call | solution.py:621
  234.6 7.7 %after.2 = bf16[512,768]{1,0:T(8,128)(2,1)} custom-call(s32[3]{0:T(128)} %get-tuple-element.273.place, bf16[512,768]{1,0:T(8,128)(2,1)} %copy-done, f32[1,768]{1,0:T(1,128)} %broadcast_in_dim.15.gain_ref, f32[1024,768]{1,0:T(8,128)} %get-tuple-element.228.gx_ref, bf16[768,2304]{1,0:T(8,128)(2,1)} %w_ref.7, bf16[1024,256]{1,0:T(8,128)(2,1)} %get-tuple-element.204.refs_0_, ...), custom_call_target="tpu_custom_call" | custom-call | flops 1811939328 | bytes 16777216 | tf_op jit(solution)/shard_map/after/pallas_call | solution.py:485
  246.3 3.3 %combine.8 = (f32[8,24,384]{2,1,0:T(8,128)}, f32[8,24,384]{2,1,0:T(8,128)}, f32[12,24,384]{2,1,0:T(8,128)}, f32[4,24,384]{2,1,0:T(8,128)}, bf16[16,24,384]{2,1,0...) custom-call(f32[16,24,384]{2,1,0:T(8,128)} %get-tuple-element.188.refs_0_, ...), custom_call_target="tpu_custom_call" | custom-call | flops 1048576 | bytes 8388608 | tf_op jit(solution)/shard_map/combine/pallas_call | solution.py:621
  249.7 3.4 %collective-permute-start.19 = (bf16[16,24,384]{2,1,0:T(8,128)(2,1)}, bf16[16,24,384]{2,1,0:T(8,128)(2,1)S(1)}, u32[]{:S(2)}, u32[]{:S(2)}) collective-permute-start(bf16[16,24,384]{2,1,0:T(8,128)(2,1)} %get-tuple-element.224), channel_id=1, source_target_pairs={{0,16},{2,18},{4,20},{6,22},{8,24},{10,26},{12,28},{14,30},{16,0},... | collective-permute-start | bytes 884744 | tf_op jit(solution)/shard_map/ppermute | solution.py:515
  258.7 7.8 %collective-permute-done.22 = bf16[4,24,384]{2,1,0:T(8,128)(2,1)S(1)} collective-permute-done((bf16[4,24,384]{2,1,0:T(8,128)(2,1)}, bf16[4,24,384]{2,1,0:T(8,128)(2,1)S(1)}, u32[]{:S(2)}, u32[]{:S(2)}) %collective-permute-start.22) | collective-permute-done | bytes 73760 | tf_op jit(solution)/shard_map/ppermute | solution.py:496
  267.6 7.7 %after.3 = bf16[512,768]{1,0:T(8,128)(2,1)} custom-call(s32[3]{0:T(128)} %get-tuple-element.272.place, bf16[512,768]{1,0:T(8,128)(2,1)} %get-tuple-element.269.x_ref.x_kept, f32[1,768]{1,0:T(1,128)} %broadcast_in_dim.15.gain_ref, f32[1024,768]{1,0:T(8,128)} %get-tuple-element.228.gx_ref, bf16[768,2304]{1,0:T(8,128)(2,1)} %w_ref.7, ...), custom_call_target="tpu_custom_call" | custom-call | flops 1811939328 | bytes 16777216 | tf_op jit(solution)/shard_map/after/pallas_call | solution.py:485
  276.2 2.3 combine.9
  279.8 3.2 %collective-permute-start.25 = (bf16[4,24,384]{2,1,0:T(8,128)(2,1)}, bf16[4,24,384]{2,1,0:T(8,128)(2,1)S(1)}, u32[]{:S(2)}, u32[]{:S(2)}) collective-permute-start(bf16[4,24,384]{2,1,0:T(8,128)(2,1)} %get-tuple-element.240), channel_id=1, source_target_pairs={{0,8},{2,10},{4,12},{6,14},{8,0},{10,2},{12,4},{14,6},{16,24},{18,... | collective-permute-start | bytes 221192 | tf_op jit(solution)/shard_map/ppermute | solution.py:515
  283.0 2.4 collective-permute-start.27
  286.8 2.7 collective-permute-done.26.refs_10_
  290.1 2.6 finish.1
  (137 shorter events, 49.4 us)
Async XLA Ops:
  3.1 22.9 %collective-permute-start = (bf16[512,768]{1,0:T(8,128)(2,1)S(1)}, bf16[512,768]{1,0:T(8,128)(2,1)S(1)}, u32[]{:S(2)}, u32[]{:S(2)}) collective-permute-start(bf16[512,768]{1,0:T(8,128)(2,1)S(1)} %get-tuple-element.268), channel_id=1, source_target_pairs={{0,1},{1,0},{2,3},{3,2},{4,5},{5,4},{6,7},{7,6},{8,9},{9,8},{10,11... | collective-permute-start | bytes 2359304 | tf_op jit(solution)/shard_map/ppermute | solution.py:496
  6.1 18.4 %collective-permute-start.1 = (s32[512]{0:T(512)S(1)}, s32[512]{0:T(512)S(1)}, u32[]{:S(2)}, u32[]{:S(2)}) collective-permute-start(s32[512]{0:T(512)S(1)} %bitcast.44), channel_id=1, source_target_pairs={{0,1},{1,0},{2,3},{3,2},{4,5},{5,4},{6,7},{7,6},{8,9},{9,8},{10,11... | collective-permute-start | bytes 6152 | tf_op jit(solution)/shard_map/ppermute | solution.py:496
  7.2 60.2 %collective-permute-start.2 = (bf16[512,768]{1,0:T(8,128)(2,1)S(1)}, bf16[512,768]{1,0:T(8,128)(2,1)S(1)}, u32[]{:S(2)}, u32[]{:S(2)}) collective-permute-start(bf16[512,768]{1,0:T(8,128)(2,1)S(1)} %get-tuple-element.266), channel_id=1, source_target_pairs={{0,1},{1,0},{2,3},{3,2},{4,5},{5,4},{6,7},{7,6},{8,9},{9,8},{10,11... | collective-permute-start | bytes 2359304 | tf_op jit(solution)/shard_map/ppermute | solution.py:496
  118.9 27.2 %collective-permute-start.3 = (bf16[128,24,384]{2,1,0:T(8,128)(2,1)}, bf16[128,24,384]{2,1,0:T(8,128)(2,1)S(1)}, u32[]{:S(2)}, u32[]{:S(2)}) collective-permute-start(bf16[128,24,384]{2,1,0:T(8,128)(2,1)} %bitcast.46), channel_id=1, source_target_pairs={{0,2},{2,0},{4,6},{6,4},{8,10},{10,8},{12,14},{14,12},{16,18},{18,... | collective-permute-start | bytes 7077896 | tf_op jit(solution)/shard_map/ppermute | solution.py:515
  118.9 27.1 %collective-permute-start.4 = (bf16[128,24,384]{2,1,0:T(8,128)(2,1)}, bf16[128,24,384]{2,1,0:T(8,128)(2,1)}, u32[]{:S(2)}, u32[]{:S(2)}) collective-permute-start(bf16[128,24,384]{2,1,0:T(8,128)(2,1)} %bitcast.45), channel_id=1, source_target_pairs={{0,2},{2,0},{4,6},{6,4},{8,10},{10,8},{12,14},{14,12},{16,18},{18,... | collective-permute-start | bytes 7077896 | tf_op jit(solution)/shard_map/ppermute | solution.py:515
  120.0 26.1 %collective-permute-start.5 = (bf16[512,768]{1,0:T(8,128)(2,1)}, bf16[512,768]{1,0:T(8,128)(2,1)S(1)}, u32[]{:S(2)}, u32[]{:S(2)}) collective-permute-start(bf16[512,768]{1,0:T(8,128)(2,1)} %get-tuple-element.148), channel_id=1, source_target_pairs={{0,1},{1,0},{2,3},{3,2},{4,5},{5,4},{6,7},{7,6},{8,9},{9,8},{10,11... | collective-permute-start | bytes 2359304 | tf_op jit(solution)/shard_map/ppermute | solution.py:496
  155.3 36.2 %collective-permute-start.6 = (bf16[64,24,384]{2,1,0:T(8,128)(2,1)}, bf16[64,24,384]{2,1,0:T(8,128)(2,1)S(1)}, u32[]{:S(2)}, u32[]{:S(2)}) collective-permute-start(bf16[64,24,384]{2,1,0:T(8,128)(2,1)} %get-tuple-element.163), channel_id=1, source_target_pairs={{0,4},{2,6},{4,0},{6,2},{8,12},{10,14},{12,8},{14,10},{16,20},{18,... | collective-permute-start | bytes 3538952 | tf_op jit(solution)/shard_map/ppermute | solution.py:515
  156.9 34.7 %collective-permute-start.7 = (bf16[64,24,384]{2,1,0:T(8,128)(2,1)}, bf16[64,24,384]{2,1,0:T(8,128)(2,1)S(1)}, u32[]{:S(2)}, u32[]{:S(2)}) collective-permute-start(bf16[64,24,384]{2,1,0:T(8,128)(2,1)} %get-tuple-element.164), channel_id=1, source_target_pairs={{0,8},{2,10},{4,12},{6,14},{8,0},{10,2},{12,4},{14,6},{16,24},{18,... | collective-permute-start | bytes 3538952 | tf_op jit(solution)/shard_map/ppermute | solution.py:515
  158.8 32.8 %collective-permute-start.8 = (bf16[64,24,384]{2,1,0:T(8,128)(2,1)}, bf16[64,24,384]{2,1,0:T(8,128)(2,1)S(1)}, u32[]{:S(2)}, u32[]{:S(2)}) collective-permute-start(bf16[64,24,384]{2,1,0:T(8,128)(2,1)} %bitcast.47), channel_id=1, source_target_pairs={{0,2},{2,0},{4,6},{6,4},{8,10},{10,8},{12,14},{14,12},{16,18},{18,... | collective-permute-start | bytes 3538952 | tf_op jit(solution)/shard_map/ppermute | solution.py:515
  201.6 16.1 %collective-permute-start.9 = (bf16[32,24,384]{2,1,0:T(8,128)(2,1)}, bf16[32,24,384]{2,1,0:T(8,128)(2,1)S(1)}, u32[]{:S(2)}, u32[]{:S(2)}) collective-permute-start(bf16[32,24,384]{2,1,0:T(8,128)(2,1)} %get-tuple-element.177), channel_id=1, source_target_pairs={{0,1},{1,0},{2,3},{3,2},{4,5},{5,4},{6,7},{7,6},{8,9},{9,8},{10,11... | collective-permute-start | bytes 1769480 | tf_op jit(solution)/shard_map/ppermute | solution.py:496
  201.8 16.0 %collective-permute-start.10 = (bf16[32,24,384]{2,1,0:T(8,128)(2,1)}, bf16[32,24,384]{2,1,0:T(8,128)(2,1)S(1)}, u32[]{:S(2)}, u32[]{:S(2)}) collective-permute-start(bf16[32,24,384]{2,1,0:T(8,128)(2,1)} %get-tuple-element.178), channel_id=1, source_target_pairs={{0,4},{2,6},{4,0},{6,2},{8,12},{10,14},{12,8},{14,10},{16,20},{18,... | collective-permute-start | bytes 1769480 | tf_op jit(solution)/shard_map/ppermute | solution.py:515
  203.8 16.4 %collective-permute-start.11 = (bf16[32,24,384]{2,1,0:T(8,128)(2,1)}, bf16[32,24,384]{2,1,0:T(8,128)(2,1)S(1)}, u32[]{:S(2)}, u32[]{:S(2)}) collective-permute-start(bf16[32,24,384]{2,1,0:T(8,128)(2,1)} %get-tuple-element.179), channel_id=1, source_target_pairs={{0,8},{2,10},{4,12},{6,14},{8,0},{10,2},{12,4},{14,6},{16,24},{18,... | collective-permute-start | bytes 1769480 | tf_op jit(solution)/shard_map/ppermute | solution.py:515
  204.7 15.5 %collective-permute-start.12 = (bf16[48,24,384]{2,1,0:T(8,128)(2,1)}, bf16[48,24,384]{2,1,0:T(8,128)(2,1)S(1)}, u32[]{:S(2)}, u32[]{:S(2)}) collective-permute-start(bf16[48,24,384]{2,1,0:T(8,128)(2,1)} %bitcast.48), channel_id=1, source_target_pairs={{0,2},{2,0},{4,6},{6,4},{8,10},{10,8},{12,14},{14,12},{16,18},{18,... | collective-permute-start | bytes 2654216 | tf_op jit(solution)/shard_map/ppermute | solution.py:515
  226.5 18.7 %collective-permute-start.16 = (bf16[40,24,384]{2,1,0:T(8,128)(2,1)}, bf16[40,24,384]{2,1,0:T(8,128)(2,1)S(1)}, u32[]{:S(2)}, u32[]{:S(2)}) collective-permute-start(bf16[40,24,384]{2,1,0:T(8,128)(2,1)} %get-tuple-element.200), channel_id=1, source_target_pairs={{0,1},{1,0},{2,3},{3,2},{4,5},{5,4},{6,7},{7,6},{8,9},{9,8},{10,11... | collective-permute-start | bytes 2211848 | tf_op jit(solution)/shard_map/ppermute | solution.py:496
  227.7 16.9 %collective-permute-start.17 = (bf16[16,24,384]{2,1,0:T(8,128)(2,1)}, bf16[16,24,384]{2,1,0:T(8,128)(2,1)S(1)}, u32[]{:S(2)}, u32[]{:S(2)}) collective-permute-start(bf16[16,24,384]{2,1,0:T(8,128)(2,1)} %get-tuple-element.201), channel_id=1, source_target_pairs={{0,4},{2,6},{4,0},{6,2},{8,12},{10,14},{12,8},{14,10},{16,20},{18,... | collective-permute-start | bytes 884744 | tf_op jit(solution)/shard_map/ppermute | solution.py:515
  228.9 15.7 %collective-permute-start.18 = (bf16[16,24,384]{2,1,0:T(8,128)(2,1)S(1)}, bf16[16,24,384]{2,1,0:T(8,128)(2,1)S(1)}, u32[]{:S(2)}, u32[]{:S(2)}) collective-permute-start(bf16[16,24,384]{2,1,0:T(8,128)(2,1)S(1)} %bitcast.49), channel_id=1, source_target_pairs={{0,2},{2,0},{4,6},{6,4},{8,10},{10,8},{12,14},{14,12},{16,18},{18,... | collective-permute-start | bytes 884744 | tf_op jit(solution)/shard_map/ppermute | solution.py:515
  230.5 14.1 %collective-permute-start.14 = (bf16[8,24,384]{2,1,0:T(8,128)(2,1)}, bf16[8,24,384]{2,1,0:T(8,128)(2,1)S(1)}, u32[]{:S(2)}, u32[]{:S(2)}) collective-permute-start(bf16[8,24,384]{2,1,0:T(8,128)(2,1)} %get-tuple-element.198), channel_id=1, source_target_pairs={{0,16},{2,18},{4,20},{6,22},{8,24},{10,26},{12,28},{14,30},{16,0},... | collective-permute-start | bytes 442376 | tf_op jit(solution)/shard_map/ppermute | solution.py:515
  233.4 11.2 %collective-permute-start.15 = (bf16[8,24,384]{2,1,0:T(8,128)(2,1)}, bf16[8,24,384]{2,1,0:T(8,128)(2,1)S(1)}, u32[]{:S(2)}, u32[]{:S(2)}) collective-permute-start(bf16[8,24,384]{2,1,0:T(8,128)(2,1)} %get-tuple-element.199), channel_id=1, source_target_pairs={{0,24},{2,26},{4,28},{6,30},{8,16},{10,18},{12,20},{14,22},{16,8},... | collective-permute-start | bytes 442376 | tf_op jit(solution)/shard_map/ppermute | solution.py:515
  245.2 50.2 %collective-permute-start.28 = (bf16[512,768]{1,0:T(8,128)(2,1)}, bf16[512,768]{1,0:T(8,128)(2,1)S(1)}, u32[]{:S(2)}, u32[]{:S(2)}) collective-permute-start(bf16[512,768]{1,0:T(8,128)(2,1)} %after.2), channel_id=1, source_target_pairs={{0,1},{1,0},{2,3},{3,2},{4,5},{5,4},{6,7},{7,6},{8,9},{9,8},{10,11... | collective-permute-start | bytes 2359304 | tf_op jit(solution)/shard_map/ppermute | solution.py:496
  249.7 25.8 %collective-permute-start.19 = (bf16[16,24,384]{2,1,0:T(8,128)(2,1)}, bf16[16,24,384]{2,1,0:T(8,128)(2,1)S(1)}, u32[]{:S(2)}, u32[]{:S(2)}) collective-permute-start(bf16[16,24,384]{2,1,0:T(8,128)(2,1)} %get-tuple-element.224), channel_id=1, source_target_pairs={{0,16},{2,18},{4,20},{6,22},{8,24},{10,26},{12,28},{14,30},{16,0},... | collective-permute-start | bytes 884744 | tf_op jit(solution)/shard_map/ppermute | solution.py:515
  253.0 22.4 %collective-permute-start.20 = (bf16[16,24,384]{2,1,0:T(8,128)(2,1)}, bf16[16,24,384]{2,1,0:T(8,128)(2,1)S(1)}, u32[]{:S(2)}, u32[]{:S(2)}) collective-permute-start(bf16[16,24,384]{2,1,0:T(8,128)(2,1)} %get-tuple-element.225), channel_id=1, source_target_pairs={{0,4},{2,6},{4,0},{6,2},{8,12},{10,14},{12,8},{14,10},{16,20},{18,... | collective-permute-start | bytes 884744 | tf_op jit(solution)/shard_map/ppermute | solution.py:515
  255.2 11.3 %collective-permute-start.22 = (bf16[4,24,384]{2,1,0:T(8,128)(2,1)}, bf16[4,24,384]{2,1,0:T(8,128)(2,1)S(1)}, u32[]{:S(2)}, u32[]{:S(2)}) collective-permute-start(bf16[4,24,384]{2,1,0:T(8,128)(2,1)} %get-tuple-element.227), channel_id=1, source_target_pairs={{0,1},{1,0},{2,3},{3,2},{4,5},{5,4},{6,7},{7,6},{8,9},{9,8},{10,11... | collective-permute-start | bytes 221192 | tf_op jit(solution)/shard_map/ppermute | solution.py:496
  257.7 17.7 %collective-permute-start.21 = (bf16[4,24,384]{2,1,0:T(8,128)(2,1)}, bf16[4,24,384]{2,1,0:T(8,128)(2,1)S(1)}, u32[]{:S(2)}, u32[]{:S(2)}) collective-permute-start(bf16[4,24,384]{2,1,0:T(8,128)(2,1)} %get-tuple-element.226), channel_id=1, source_target_pairs={{0,1},{1,0},{2,3},{3,2},{4,5},{5,4},{6,7},{7,6},{8,9},{9,8},{10,11... | collective-permute-start | bytes 221192 | tf_op jit(solution)/shard_map/ppermute | solution.py:496
  266.5 8.9 %collective-permute-start.23 = (bf16[4,24,384]{2,1,0:T(8,128)(2,1)S(1)}, bf16[4,24,384]{2,1,0:T(8,128)(2,1)S(1)}, u32[]{:S(2)}, u32[]{:S(2)}) collective-permute-start(bf16[4,24,384]{2,1,0:T(8,128)(2,1)S(1)} %collective-permute-done.22), channel_id=1, source_target_pairs={{0,4},{2,6},{4,0},{6,2},{8,12},{10,14},{12,8},{14,10},{16,20},{18,... | collective-permute-start | bytes 221192 | tf_op jit(solution)/shard_map/ppermute | solution.py:515
  (38 other events, 200.8 us)

commit v3 on v2

--- a/solution.py
+++ b/solution.py
@@ -508,22 +508,9 @@
 
 
 def crossed(block, bits):
-    if 0 in bits:
-        block = swapped(block)
-    step = sum(1 << abs(bit) if bit > 0 else 1 for bit in bits if bit)
-    if step:
-        block = lax.ppermute(block, "dp", [(i, i ^ step) for i in range(lax.axis_size("dp"))])
-    return block
-
-
-def picks(left, bits, mask):
-    rest = [bit for bit in left if bit not in bits]
-    found = []
-    for number in range(1 << len(rest)):
-        value = {bit: (number >> (len(rest) - 1 - at)) & 1 for at, bit in enumerate(rest)}
-        value.update({bit: int(bit in mask) for bit in bits})
-        found.append(sum(value[bit] << (len(left) - 1 - at) for at, bit in enumerate(left)))
-    return found
+    step = sum(1 if bit == 0 else 2 if bit == -1 else 2 << bit for bit in bits)
+    count = 2 * lax.axis_size("dp")
+    return lax.ppermute(block, ("dp", "seq"), [(i, i ^ step) for i in range(count)])
 
 
 def masks_of(bits):
@@ -531,19 +518,20 @@
 
 
 def combine_kernel(*refs, work, steps):
-    for lead, cut_up, terms, targets in work:
+    for lead, cut_up, targets in work:
         def one(index, carry):
-            for count, sources, places, target, offset in targets:
-                for at, source in enumerate(sources):
+            for target, offset, count, sources in targets:
+                for at, terms in enumerate(sources):
                     total = None
-                    for ref, begin in terms:
-                        value = refs[ref][begin + index * places + source].astype(jnp.float32)
+                    for ref, begin, per, place in terms:
+                        where = (index, *place) if per is None else (begin + index * per + place,)
+                        value = refs[ref][where].astype(jnp.float32)
                         total = value if total is None else total + value
                     refs[target][offset + index * count + at] = total.astype(refs[target].dtype)
             return carry
 
         if cut_up:
-            one(0, 0)
+            lax.fori_loop(0, lead // steps, one, 0)
         elif steps > 1:
             @pl.when(pl.program_id(0) == 0)
             def _():
@@ -565,87 +553,99 @@
         self.lead, _, self.rows, self.columns = keep.shape
         self.left = list(reversed(range(chips.bit_length() - 1)))
         self.plan = list(plan)
-        self.terms = [(keep.reshape(-1, self.rows, self.columns), 0)]
+        self.terms = [(keep.reshape(-1, self.rows, self.columns), list(self.left), None)]
         self.first = send.reshape(-1, self.rows, self.columns)
 
 
+class Operands:
+    def __init__(self):
+        self.arrays, self.specs, self.seen = [], [], {}
+
+    def add(self, array, spec):
+        self.arrays.append(array)
+        self.specs.append(spec)
+        return len(self.arrays) - 1
+
+    def finder(self, flow, term, fixed, cut_up):
+        array, bits, offset = term
+        if offset is not None:
+            if id(array) not in self.seen:
+                self.seen[id(array)] = self.add(array, pl.BlockSpec(array.shape, lambda i: (0, 0, 0), pipeline_mode=pl.Buffered(1)))
+            ref, per = self.seen[id(array)], 1 << len(bits)
+            return lambda value: (ref, offset, per, sum(value[bit] << (len(bits) - 1 - at) for at, bit in enumerate(bits)))
+        view = array.reshape(flow.lead, *(2,) * len(bits), flow.rows, flow.columns)
+        block = (flow.lead // cut_up if cut_up else flow.lead, *[1 if bit in fixed else 2 for bit in bits], flow.rows, flow.columns)
+        index = tuple(fixed.get(bit, 0) for bit in bits)
+        mode = {} if cut_up else dict(pipeline_mode=pl.Buffered(1))
+        ref = self.add(view, pl.BlockSpec(block, lambda i: (i if cut_up else 0, *index, 0, 0), **mode))
+        return lambda value: (ref, 0, None, tuple(0 if bit in fixed else value[bit] for bit in bits))
+
+
 def combine(flows, steps):
-    inputs, in_specs, out_shapes, out_specs, work, sends = [], [], [], [], [], {}
-
-    def spec(array, per):
-        if per:
-            return pl.BlockSpec((per, *array.shape[1:]), lambda i: (i, 0, 0))
-        return pl.BlockSpec(array.shape, lambda i: (0, 0, 0), pipeline_mode=pl.Buffered(1))
-
-    def place_of(array, per):
-        for at, seen in enumerate(inputs):
-            if seen is array:
-                return at
-        inputs.append(array)
-        in_specs.append(spec(array, per))
-        return len(inputs) - 1
-
-    plans = []
+    operands, plans, sizes = Operands(), [], {}
     for flow in flows:
         bits = flow.plan.pop(0)
-        places = 1 << len(flow.left)
-        count = places >> len(bits)
-        cut_up = steps > 1 and flow.lead == steps
-        terms = [(place_of(array, cut_up and places), offset) for array, offset in flow.terms]
-        kept = picks(flow.left, bits, ())
-        plans.append((flow, bits, places, count, cut_up, terms, kept))
-    sizes = {}
-    for flow, bits, places, count, cut_up, terms, kept in plans:
+        rest = [bit for bit in flow.left if bit not in bits]
+        cut_up = steps if steps > 1 and flow.lead % steps == 0 else 0
+        gone = {bit: 0 for bit in range(64) if bit not in flow.left}
+        fixed = {**gone, bits[0]: 1} if len(bits) == 1 else gone
+        finders = [operands.finder(flow, term, fixed, cut_up) for term in flow.terms]
+        plans.append((flow, bits, rest, cut_up, gone, finders))
         for mask in masks_of(bits):
+            size = flow.lead << len(rest)
             key = mask if steps == 1 else (mask, id(flow))
-            sizes.setdefault(key, []).append((flow, flow.lead * count, cut_up and count, mask))
-    outputs = []
-    for flow, bits, places, count, cut_up, terms, kept in plans:
-        shape = (flow.lead * count, flow.rows, flow.columns)
-        outputs.append(jax.ShapeDtypeStruct(shape, jnp.bfloat16 if count > 4 else jnp.float32))
-        out_specs.append(spec(outputs[-1], cut_up and count))
-    for key, members in sizes.items():
+            sizes.setdefault(key, []).append((flow, size, cut_up and size // cut_up, mask))
+    outputs, out_specs = [], []
+    for members in sizes.values():
         shape = (sum(size for _, size, _, _ in members), members[0][0].rows, members[0][0].columns)
         outputs.append(jax.ShapeDtypeStruct(shape, jnp.bfloat16))
-        out_specs.append(spec(outputs[-1], members[0][2]))
-    base = len(inputs)
-    for at, (flow, bits, places, count, cut_up, terms, kept) in enumerate(plans):
-        targets = [(count, kept, places, base + at, 0)]
-        for number, (key, members) in enumerate(sizes.items()):
+        cut = members[0][2]
+        out_specs.append(
+            pl.BlockSpec((cut, *shape[1:]), lambda i: (i, 0, 0)) if cut
+            else pl.BlockSpec(shape, lambda i: (0, 0, 0), pipeline_mode=pl.Buffered(1))
+        )
+    work = []
+    for flow, bits, rest, cut_up, gone, finders in plans:
+        targets = []
+        for number, members in enumerate(sizes.values()):
             offset = 0
             for member, size, _, mask in members:
                 if member is flow:
-                    targets.append((count, picks(flow.left, bits, mask), places, base + len(plans) + number, offset))
+                    sources = []
+                    for at in range(1 << len(rest)):
+                        value = {bit: (at >> (len(rest) - 1 - e)) & 1 for e, bit in enumerate(rest)}
+                        value.update(gone)
+                        value.update({bit: int(bit in mask) for bit in bits})
+                        sources.append([find(value) for find in finders])
+                    targets.append((len(operands.arrays) + number, offset, 1 << len(rest), sources))
                 offset += size
-        work.append((flow.lead, cut_up, terms, targets))
+        work.append((flow.lead, cut_up, targets))
+        flow.left = rest
     results = pl.pallas_call(
         functools.partial(combine_kernel, work=work, steps=steps),
         grid=(steps,),
-        in_specs=in_specs,
+        in_specs=operands.specs,
         out_specs=out_specs,
         out_shape=outputs,
         compiler_params=pltpu.CompilerParams(vmem_limit_bytes=60 << 20),
         cost_estimate=pl.CostEstimate(flops=1 << 20, bytes_accessed=8 << 20, transcendentals=0),
         name="combine",
-    )(*inputs)
-    for (flow, bits, *_), kept in zip(plans, results):
-        flow.terms = [(kept, 0)]
-        flow.left = [bit for bit in flow.left if bit not in bits]
+    )(*operands.arrays)
     return [
         (members[0][3], array, [(flow, size) for flow, size, _, _ in members])
-        for members, array in zip(sizes.values(), results[len(plans):])
+        for members, array in zip(sizes.values(), results)
     ]
 
 
 def leave(flows, value=None, steps=1):
-    starting = [flow for flow in flows if flow.plan and flow.first is not None]
-    going = [flow for flow in flows if flow.plan and flow.first is None]
-    sent = [((-1,), flow.first, [(flow, flow.first.shape[0])]) for flow in starting]
-    for flow in starting:
+    flows = [flow for flow in flows if flow.plan]
+    starting = [flow for flow in flows if flow.plan[0] == (-1,)]
+    waiting = [flow for flow in flows if flow.plan[0] == ()]
+    going = [flow for flow in flows if flow not in starting and flow not in waiting]
+    for flow in starting + waiting:
         flow.plan.pop(0)
-        flow.first = None
-    if going:
-        sent = combine(going, steps) + sent
+    sent = combine(going, steps) if going else []
+    sent += [((-1,), flow.first, [(flow, flow.first.shape[0])]) for flow in starting]
     value, arrays = lax.optimization_barrier((value, [array for _, array, _ in sent]))
     return value, [(crossed(array, mask), members) for array, (mask, _, members) in zip(arrays, sent)]
 
@@ -655,7 +655,7 @@
     for array, (_, members) in zip(moved, transfers):
         at = 0
         for flow, size in members:
-            flow.terms.append((array, at))
+            flow.terms.append((array, list(flow.left), at if len(members) > 1 else None))
             at += size
     return value
 
@@ -664,50 +664,53 @@
     inputs, outputs = refs[:count], refs[count:]
     for terms, targets in work:
         for lead, (target, row, column, width, parts) in enumerate(targets):
-            total = sum(inputs[ref][offset + lead].astype(jnp.float32) for ref, offset in terms)
+            total = None
+            for ref, begin, per, place in terms:
+                where = (lead, *place) if per is None else (begin + lead * per + place,)
+                value = inputs[ref][where].astype(jnp.float32)
+                total = value if total is None else total + value
             for part in range(parts):
                 piece = slice(part * width, (part + 1) * width)
                 begin = column + part * (outputs[target].shape[1] // parts if parts > 1 else 0)
                 outputs[target][row:row + total.shape[0], begin:begin + width] = total[:, piece]
     for number, source in enumerate((0, 2)):
         weight, gain = inputs[count - 4 + 2 * number], inputs[count - 3 + 2 * number]
-        outputs[4 + number][...] = jnp.sum(weight[...] * outputs[source][...], axis=1, keepdims=True) / gain[...]
-
-
-def finish(up, down, out_and_one, two, three, out_lead, weights):
-    inputs, work = [], []
-
-    def place_of(array):
-        for at, seen in enumerate(inputs):
-            if seen is array:
-                return at
-        inputs.append(array)
-        return len(inputs) - 1
-
+        ones = jnp.ones((8, weight.shape[1]), jnp.float32)
+        sums = lax.dot_general(ones, weight[...] * outputs[source][...], NT, precision=lax.Precision.HIGHEST,
+                               preferred_element_type=jnp.float32)
+        outputs[4 + number][...] = sums[:1] / gain[...]
+
+
+def finish(up, down, out_and_one, others, out_lead, weights):
+    operands, work = Operands(), []
     rows = up.rows
-    heads = iter(range(6))
+    heads = iter(range(64))
     third = lambda: (0, 0, next(heads) * SMALL, SMALL, 3)
-    plans = (
+    plans = [
         (up, [(2, 0, lead * PART, PART, 1) for lead in range(up.lead)]),
         (down, [(3, (lead % 4) * rows, (lead // 4) * PART, PART, 1) for lead in range(down.lead)]),
         (out_and_one, [third() for _ in range(out_and_one.lead - out_lead)]
          + [(1, 0, lead * PART, PART, 1) for lead in range(out_lead)]),
-        (two, [third() for _ in range(two.lead)]),
-        (three, [third() for _ in range(three.lead)]),
-    )
+    ]
+    plans += [(flow, [third() for _ in range(flow.lead)]) for flow in others]
+    gone = {bit: 0 for bit in range(64)}
     for flow, targets in plans:
-        work.append(([(place_of(array), offset) for array, offset in flow.terms], targets))
-    inputs += weights
+        finders = [operands.finder(flow, term, gone, False) for term in flow.terms]
+        work.append(([find(gone) for find in finders], targets))
+    for weight in weights:
+        operands.add(weight, pl.BlockSpec(weight.shape, lambda i: (0, 0), pipeline_mode=pl.Buffered(1)))
     width = out_lead * PART
-    shape = lambda *size: jax.ShapeDtypeStruct(size, jnp.float32)
+    sizes = [(rows, 3 * width), (rows, width), (rows, up.lead * PART), (4 * rows, width), (1, rows), (1, rows)]
     return pl.pallas_call(
-        functools.partial(finish_kernel, work=work, count=len(inputs)),
-        out_shape=[shape(rows, 3 * width), shape(rows, width), shape(rows, up.lead * PART), shape(4 * rows, width),
-                   shape(rows, 1), shape(rows, 1)],
+        functools.partial(finish_kernel, work=work, count=len(operands.arrays)),
+        grid=(1,),
+        in_specs=operands.specs,
+        out_specs=[pl.BlockSpec(size, lambda i: (0, 0), pipeline_mode=pl.Buffered(1)) for size in sizes],
+        out_shape=[jax.ShapeDtypeStruct(size, jnp.float32) for size in sizes],
         compiler_params=pltpu.CompilerParams(vmem_limit_bytes=60 << 20),
         cost_estimate=pl.CostEstimate(flops=1 << 20, bytes_accessed=4 << 20, transcendentals=0),
         name="finish",
-    )(*inputs)
+    )(*operands.arrays)
 
 
 def body(tokens, segments, cotangent, gain_attn, w_qkv, w_out, gain_ffn, w_up, w_down):
@@ -720,12 +723,17 @@
     wide = [far[at:at + 2] for at in range(0, len(far), 2)]
 
     x_kept, x_sent = split_window(tokens)
+    segments, cotangent, x_sent = lax.optimization_barrier((segments, cotangent, x_sent))
     seg_kept, seg_sent = split_window(segments)
     gy_kept, gy_sent = split_window(cotangent)
     x_other, seg_other, gy_other = swapped(x_sent), swapped(seg_sent), swapped(gy_sent)
     seg = jnp.where(seq == 0, jnp.concatenate([seg_kept, seg_other]), jnp.concatenate([seg_other, seg_kept]))[None]
     first, last = bounds(seg, 256, 256)
     gain_one, gain_two = gain_attn[None], gain_ffn[None]
+    begin = shard_at(here, 0, 0) * (w_out.shape[0] // shards)
+    shard_of = lambda array: lax.dynamic_slice_in_dim(array, begin, w_out.shape[0] // shards, 0).astype(jnp.float32)
+    weights = [shard_of(w_qkv), shard_of(gain_attn)[None], shard_of(w_up), shard_of(gain_ffn)[None]]
+    x_other, weights = lax.optimization_barrier((x_other, weights))
     early = before(here, x_kept, gain_one, w_qkv, shards)
     proj, low_t = before(there, x_other, gain_one, w_qkv, shards, early)
     mixture, lse = attend(first, seg, proj)
@@ -733,10 +741,9 @@
         here, (x_kept, x_other), mixture, (gy_kept, gy_other), w_out, gain_two, w_up, w_down, shards
     )
 
-    core = (-1,)
-    later = [(bit,) for bit in far[1:]]
-    up = Flow(here, keep_up, send_up, chips, [core, (1,), (0,), *wide])
-    down = Flow(here, keep_down, send_down, chips, [core, far[:1], (1,), (0,), *later], 4)
+    core, near = (-1,), [(bit,) for bit in far]
+    up = Flow(here, keep_up, send_up, chips, [core, (1,), (0,), *near])
+    down = Flow(here, keep_down, send_down, chips, [core, *near[:1], (1,), (0,), *near[1:]], 4)
     heads = []
 
     def heads_back(begin, count, plan, riders=()):
@@ -746,12 +753,12 @@
 
     (go, out_sent), moving = leave([up, down], (go, out_sent))
     out_other = swapped(out_sent)
-    one = heads_back(0, 2, [far[:1], (1,), *later, (0,)], (keep_out, send_out))
+    one = heads_back(0, 2, [*near[:1], (0,), (1,), *near[1:]], (keep_out, send_out))
     out_other = arrive(moving, out_other)
-    (go, out_other), moving = leave([up, down, one], (go, out_other), up.lead)
-    two = heads_back(2, 3, [(0,), (1,), *wide])
+    (go, out_other), moving = leave([up, down, one], (go, out_other), 2)
+    two = heads_back(2, 3, [(1,), (0,), *wide])
     arrive(moving)
-    go, moving = leave([up, down, one, two], go, up.lead)
+    go, moving = leave([up, down, one, two], go, 2)
     three = heads_back(5, 1, [(0, 1), *wide])
     arrive(moving)
     flows = [up, down, one, two, three]
@@ -767,11 +774,8 @@
         if not any(flow.plan for flow in flows):
             break
         _, moving = leave(flows)
-    begin = shard_at(here, 0, 0) * up.rows
-    shard_of = lambda array: lax.dynamic_slice_in_dim(array, begin, up.rows, 0).astype(jnp.float32)
-    weights = [shard_of(w_qkv), shard_of(gain_attn)[:, None], shard_of(w_up), shard_of(gain_ffn)[:, None]]
     grad_qkv, grad_out, grad_up, grad_down, grad_gain_attn, grad_gain_ffn = finish(
-        up, down, one, two, three, w_out.shape[1] // PART, weights
+        up, down, one, [two, three], w_out.shape[1] // PART, weights
     )
     return (
         joined(out_kept, out_other),
@@ -780,8 +784,8 @@
         grad_out,
         grad_up,
         grad_down,
-        grad_gain_attn[:, 0],
-        grad_gain_ffn[:, 0],
+        grad_gain_attn[0],
+        grad_gain_ffn[0],
     )
 
 

time: 302 us -> 285 us (0.944)
  Pallas kernels: 213 us -> 204 us
  starting transfers between devices: 34 us -> 29.8 us
    ppermute x19 -> x20, waiting for transfers between devices: 9.05 us -> 21.1 us  [crossed(): lax.ppermute(block, ('dp', 'seq'), [(i, i ^ step) for i in range(count)])]
    ppermute x10 -> x5, waiting for transfers between devices: 14.5 us -> 2.76 us  [swapped(): return lax.ppermute(block, 'seq', [(0, 1), (1, 0)])]
    pallas_call x5, Pallas kernels: 26.9 us -> 17.2 us  [combine(): pl.pallas_call(functools.partial(combine_kernel, work=work, steps=steps),...]
    ppermute x10 -> x5, starting transfers between devices: 12.5 us -> 6.32 us  [swapped(): return lax.ppermute(block, 'seq', [(0, 1), (1, 0)])]
    ppermute x19 -> x20, starting transfers between devices: 21.5 us -> 23.5 us  [crossed(): lax.ppermute(block, ('dp', 'seq'), [(i, i ^ step) for i in range(count)])]
    unnamed x66 -> x60, local copies, waits for them, and re-layouts: 7.63 us -> 7.74 us
  transfers between devices with their start and end apart: 29 -> 25, of which waited for: 7 -> 10; matrix products, arithmetic and copies ran while one was open for 5% -> 4% of each run, Pallas kernels for 48% -> 51%
where the time goes in v3:
time: 285 us; the launch traced here: 280 us
  Pallas kernels  204 us (72%)
  starting transfers between devices  29.8 us (10%)
  waiting for transfers between devices  23.8 us (8%)
  local copies, waits for them, and re-layouts  13.2 us (5%)
  other arithmetic  8.53 us (3%)
    pallas_call x3, Pallas kernels, attend_back(): pl.pallas_call(functools.partial(attend_back_kernel, bk=bk), grid_spec=gr...  69.7 us
    pallas_call x1, Pallas kernels, middle(): pl.pallas_call(functools.partial(middle_kernel, shards=shards, block=bloc...  49.7 us
    pallas_call x1, Pallas kernels, attend(): pl.pallas_call(functools.partial(attend_kernel, bq=bq, unroll=unroll), gr...  33.3 us
    ppermute x20, starting transfers between devices, crossed(): lax.ppermute(block, ('dp', 'seq'), [(i, i ^ step) for i in range(count)])  23.5 us
    ppermute x20, waiting for transfers between devices, crossed(): lax.ppermute(block, ('dp', 'seq'), [(i, i ^ step) for i in range(count)])  21.1 us
    pallas_call x5, Pallas kernels, combine(): pl.pallas_call(functools.partial(combine_kernel, work=work, steps=steps),...  17.2 us
    pallas_call x2, Pallas kernels, after(): pl.pallas_call(after_kernel, grid_spec=grid_spec, out_shape=jax.ShapeDtyp...  15.4 us
    pallas_call x2, Pallas kernels, before(): pl.pallas_call(functools.partial(before_kernel, shards=shards, block=bloc...  14.8 us
  transfers between devices with their start and end apart: 25, of which 10 were waited for; matrix products, arithmetic and copies ran while one was open for 4% of the time, Pallas kernels for 51%

profile of v3, /device:TPU:0, one launch (start us, length us, event | category | flops | bytes accessed | tf_op | source)
XLA Modules:
  0.0 280.2 jit_solution(7157263322294218004)
XLA Ops:
  0.7 2.5 dynamic-slice_bitcast_fusion.2
  3.2 3.0 %collective-permute-start.1 = (s32[512]{0:T(512)S(1)}, s32[512]{0:T(512)S(1)}, u32[]{:S(2)}, u32[]{:S(2)}) collective-permute-start(s32[512]{0:T(512)S(1)} %bitcast.118), channel_id=1, source_target_pairs={{0,1},{1,0},{2,3},{3,2},{4,5},{5,4},{6,7},{7,6},{8,9},{9,8},{10,11... | collective-permute-start | bytes 6152 | tf_op jit(solution)/shard_map/ppermute | solution.py:496
  13.7 7.4 %before.2 = (bf16[1024,2304]{1,0:T(8,128)(2,1)}, bf16[768,1024]{1,0:T(8,128)(2,1)}) custom-call(s32[3]{0:T(128)} %get-tuple-element.232.place, bf16[512,768]{1,0:T(8,128)(2,1)} %get-tuple-element.229.x_ref.x_kept, f32[1,768]{1,0:T(1,128)} %broadcast_in_dim.17.gain_ref, bf16[768,2304]{1,0:T(8,128)(2,1)} %w_ref.7), custom_call_target="tpu_custom_call" | custom-call | flops 1811939328 | bytes 12582912 | tf_op jit(solution)/shard_map/before/pallas_call | solution.py:312
  23.9 2.7 collective-permute-done.x_ref.x_other
  27.5 7.3 %before.3 = (bf16[1024,2304]{1,0:T(8,128)(2,1)}, bf16[768,1024]{1,0:T(8,128)(2,1)}) custom-call(s32[3]{0:T(128)} %get-tuple-element.233.place, bf16[512,768]{1,0:T(8,128)(2,1)} %copy-done.10, f32[1,768]{1,0:T(1,128)} %broadcast_in_dim.17.gain_ref, bf16[768,2304]{1,0:T(8,128)(2,1)} %w_ref.7, ...), custom_call_target="tpu_custom_call", output_to_operand_aliasing={{0}: (4, {}), {1}: (5, {})} | custom-call | flops 1811939328 | bytes 12582912 | tf_op jit(solution)/shard_map/before/pallas_call | solution.py:312
  34.9 33.3 %attend.1 = (bf16[1024,768]{1,0:T(8,128)(2,1)}, f32[48,1024]{1,0:T(8,128)}) custom-call(s32[4]{0:T(128)} %and_select_fusion.1.first, s32[1,1024]{1,0:T(1,128)} %broadcast_select_fusion.seg_ref, bf16[1024,2304]{1,0:T(8,128)(2,1)} %get-tuple-element.121.q_ref.k_ref.v_ref, bf16[1024,2304]{1,0:T(8,128)(2,1)} %get-tuple-element.121.q_ref.k_ref.v_ref, ...), custom_call_target="tpu_custom_call" | custom-call | flops 30064771072 | bytes 8388608 | tf_op jit(solution)/shard_map/attend/pallas_call | solution.py:86
  69.2 49.7 %middle.1 = (bf16[512,768]{1,0:T(8,128)(2,1)}, bf16[512,768]{1,0:T(8,128)(2,1)}, f32[1024,768]{1,0:T(8,128)}, bf16[1024,768]{1,0:T(8,128)(2,1)}, bf16[8,16,24,38...) custom-call(s32[3]{0:T(128)} %get-tuple-element.232.place, ...), custom_call_target="tpu_custom_call" | custom-call | flops 28991029248 | bytes 41943040 | tf_op jit(solution)/shard_map/middle/pallas_call | solution.py:444
  120.0 24.0 %attend_back.3 = (bf16[1024,256]{1,0:T(8,128)(2,1)}, bf16[1024,256]{1,0:T(8,128)(2,1)}, bf16[1024,256]{1,0:T(8,128)(2,1)}, bf16[4,16,24,384]{3,2,1,0:T(8,128)(2,1)}, bf16[4,16,24,384]{3,2,1,0:T(8,128)(2,1)}) custom-call(s32[4]{0:T(128)} %and_select_fusion.last, s32[1,1024]{1,0:T(1,128)} %broadcast_select_fusion.seg_ref, ...), custom_call_target="tpu_custom_call" | custom-call | flops 21474836480 | bytes 8388608 | tf_op jit(solution)/shard_map/attend_back/pallas_call | solution.py:206
  145.5 3.6 %combine.5 = (bf16[64,24,384]{2,1,0:T(8,128)(2,1)}, bf16[64,24,384]{2,1,0:T(8,128)(2,1)}) custom-call(bf16[8,2,2,2,2,24,384]{6,5,4,3,2,1,0:T(8,128)(2,1)} %bitcast.48, bf16[8,2,2,2,2,24,384]{6,5,4,3,2,1,0:T(8,128)(2,1)} %bitcast.58, bf16[8,2,2,2,2,24,384]{6,5,4,3,2,1,0:T(8,128)(2,1)} %bitcast.53, ...), custom_call_target="tpu_custom_call" | custom-call | flops 1048576 | bytes 8388608 | tf_op jit(solution)/shard_map/combine/pallas_call | solution.py:624
  151.1 4.3 %collective-permute-start.7 = (bf16[64,24,384]{2,1,0:T(8,128)(2,1)}, bf16[64,24,384]{2,1,0:T(8,128)(2,1)S(1)}, u32[]{:S(2)}, u32[]{:S(2)}) collective-permute-start(bf16[64,24,384]{2,1,0:T(8,128)(2,1)} %get-tuple-element.148), channel_id=1, source_target_pairs={{0,8},{1,9},{2,10},{3,11},{4,12},{5,13},{6,14},{7,15},{8,0},{9,1},... | collective-permute-start | bytes 3538952 | tf_op jit(solution)/shard_map/ppermute | solution.py:513
  155.3 32.7 %attend_back.4 = (bf16[1024,384]{1,0:T(8,128)(2,1)}, bf16[1024,384]{1,0:T(8,128)(2,1)}, bf16[1024,384]{1,0:T(8,128)(2,1)}, bf16[3,16,24,384]{3,2,1,0:T(8,128)(2,1)}, bf16[3,16,24,384]{3,2,1,0:T(8,128)(2,1)}) custom-call(s32[4]{0:T(128)} %and_select_fusion.last, s32[1,1024]{1,0:T(1,128)} %broadcast_select_fusion.seg_ref, ...), custom_call_target="tpu_custom_call" | custom-call | flops 32212254720 | bytes 8388608 | tf_op jit(solution)/shard_map/attend_back/pallas_call | solution.py:206
  189.8 3.6 %combine.6 = (bf16[32,24,384]{2,1,0:T(8,128)(2,1)}, bf16[32,24,384]{2,1,0:T(8,128)(2,1)}, bf16[32,24,384]{2,1,0:T(8,128)(2,1)}) custom-call(bf16[8,2,2,2,2,24,384]{6,5,4,3,2,1,0:T(8,128)(2,1)} %bitcast.49, bf16[8,2,2,2,2,24,384]{6,5,4,3,2,1,0:T(8,128)(2,1)} %bitcast.59, bf16[8,2,2,2,24,384]{5,4,3,2,1,0:T(8,128)(2,1)} %bitcast.73, ...), custom_call_target="tpu_custom_call" | custom-call | flops 1048576 | bytes 8388608 | tf_op jit(solution)/shard_map/combine/pallas_call | solution.py:624
  194.2 13.0 %attend_back.5 = (bf16[1024,128]{1,0:T(8,128)(2,1)}, bf16[1024,128]{1,0:T(8,128)(2,1)}, bf16[1024,128]{1,0:T(8,128)(2,1)}, bf16[1,16,24,384]{3,2,1,0:T(8,128)(2,1)}, bf16[1,16,24,384]{3,2,1,0:T(8,128)(2,1)}) custom-call(s32[4]{0:T(128)} %and_select_fusion.last, s32[1,1024]{1,0:T(1,128)} %broadcast_select_fusion.seg_ref, ...), custom_call_target="tpu_custom_call" | custom-call | flops 10737418240 | bytes 8388608 | tf_op jit(solution)/shard_map/attend_back/pallas_call | solution.py:206
  210.9 3.9 %combine.7 = (bf16[16,24,384]{2,1,0:T(8,128)(2,1)}, bf16[32,24,384]{2,1,0:T(8,128)(2,1)}, bf16[24,24,384]{2,1,0:T(8,128)(2,1)}) custom-call(bf16[8,2,2,2,2,24,384]{6,5,4,3,2,1,0:T(8,128)(2,1)} %bitcast.50, bf16[8,2,2,2,2,24,384]{6,5,4,3,2,1,0:T(8,128)(2,1)} %bitcast.60, bf16[8,2,2,2,24,384]{5,4,3,2,1,0:T(8,128)(2,1)} %bitcast.74, ...), custom_call_target="tpu_custom_call" | custom-call | flops 1048576 | bytes 8388608 | tf_op jit(solution)/shard_map/combine/pallas_call | solution.py:624
  218.1 7.7 %after.2 = bf16[512,768]{1,0:T(8,128)(2,1)} custom-call(s32[3]{0:T(128)} %get-tuple-element.233.place, bf16[512,768]{1,0:T(8,128)(2,1)} %copy-done.10, f32[1,768]{1,0:T(1,128)} %broadcast_in_dim.17.gain_ref, f32[1024,768]{1,0:T(8,128)} %get-tuple-element.200.gx_ref, bf16[768,2304]{1,0:T(8,128)(2,1)} %w_ref.7, bf16[1024,256]{1,0:T(8,128)(2,1)} %get-tuple-element.178.refs_0_, ...), custom_call_target="tpu_custom_call" | custom-call | flops 1811939328 | bytes 16777216 | tf_op jit(solution)/shard_map/after/pallas_call | solution.py:485
  231.2 3.5 %combine.8 = (bf16[16,24,384]{2,1,0:T(8,128)(2,1)}, bf16[12,24,384]{2,1,0:T(8,128)(2,1)}, bf16[16,24,384]{2,1,0:T(8,128)(2,1)}, bf16[4,24,384]{2,1,0:T(8,128)(2,1)}) custom-call(bf16[8,2,2,2,2,24,384]{6,5,4,3,2,1,0:T(8,128)(2,1)} %bitcast.51, bf16[8,2,2,2,2,24,384]{6,5,4,3,2,1,0:T(8,128)(2,1)} %bitcast.61, bf16[8,2,2,2,24,384]{5,4,3,2,1,0:T(8,128)(2,1)} %bitcast.75, ...), custom_call_target="tpu_custom_call" | custom-call | flops 1048576 | bytes 8388608 | tf_op jit(solution)/shard_map/combine/pallas_call | solution.py:624
  234.6 3.7 %collective-permute-start.17 = (bf16[16,24,384]{2,1,0:T(8,128)(2,1)}, bf16[16,24,384]{2,1,0:T(8,128)(2,1)S(1)}, u32[]{:S(2)}, u32[]{:S(2)}) collective-permute-start(bf16[16,24,384]{2,1,0:T(8,128)(2,1)} %get-tuple-element.196), channel_id=1, source_target_pairs={{0,16},{1,17},{2,18},{3,19},{4,20},{5,21},{6,22},{7,23},{8,24},{9,... | collective-permute-start | bytes 884744 | tf_op jit(solution)/shard_map/ppermute | solution.py:513
  241.8 7.7 %after.3 = bf16[512,768]{1,0:T(8,128)(2,1)} custom-call(s32[3]{0:T(128)} %get-tuple-element.232.place, bf16[512,768]{1,0:T(8,128)(2,1)} %get-tuple-element.229.x_ref.x_kept, f32[1,768]{1,0:T(1,128)} %broadcast_in_dim.17.gain_ref, f32[1024,768]{1,0:T(8,128)} %get-tuple-element.200.gx_ref, bf16[768,2304]{1,0:T(8,128)(2,1)} %w_ref.7, ...), custom_call_target="tpu_custom_call" | custom-call | flops 1811939328 | bytes 16777216 | tf_op jit(solution)/shard_map/after/pallas_call | solution.py:485
  250.7 5.7 %collective-permute-done.19.refs_8_.refs_19_ = bf16[16,24,384]{2,1,0:T(8,128)(2,1)S(1)} collective-permute-done((bf16[16,24,384]{2,1,0:T(8,128)(2,1)}, bf16[16,24,384]{2,1,0:T(8,128)(2,1)S(1)}, u32[]{:S(2)}, u32[]{:S(2)}) %collective-permute-start.19) | collective-permute-done | bytes 294944 | tf_op jit(solution)/shard_map/ppermute | solution.py:513
  257.0 2.6 combine.9
  260.2 4.8 %collective-permute-start.23 = (bf16[4,24,384]{2,1,0:T(8,128)(2,1)}, bf16[4,24,384]{2,1,0:T(8,128)(2,1)S(1)}, u32[]{:S(2)}, u32[]{:S(2)}) collective-permute-start(bf16[4,24,384]{2,1,0:T(8,128)(2,1)} %get-tuple-element.206), channel_id=1, source_target_pairs={{0,24},{1,25},{2,26},{3,27},{4,28},{5,29},{6,30},{7,31},{8,16},{9,... | collective-permute-start | bytes 221192 | tf_op jit(solution)/shard_map/ppermute | solution.py:513
  266.4 3.4 %collective-permute-done.23.refs_21_ = bf16[4,24,384]{2,1,0:T(8,128)(2,1)S(1)} collective-permute-done((bf16[4,24,384]{2,1,0:T(8,128)(2,1)}, bf16[4,24,384]{2,1,0:T(8,128)(2,1)S(1)}, u32[]{:S(2)}, u32[]{:S(2)}) %collective-permute-start.23) | collective-permute-done | bytes 73760 | tf_op jit(solution)/shard_map/ppermute | solution.py:513
  269.7 4.5 %collective-permute-done.21.refs_15_ = bf16[8,24,384]{2,1,0:T(8,128)(2,1)S(1)} collective-permute-done((bf16[8,24,384]{2,1,0:T(8,128)(2,1)}, bf16[8,24,384]{2,1,0:T(8,128)(2,1)S(1)}, u32[]{:S(2)}, u32[]{:S(2)}) %collective-permute-start.21) | collective-permute-done | bytes 147488 | tf_op jit(solution)/shard_map/ppermute | solution.py:513
  274.9 3.6 %finish.1 = (f32[24,2304]{1,0:T(8,128)}, f32[24,768]{1,0:T(8,128)}, f32[24,3072]{1,0:T(8,128)}, f32[96,768]{1,0:T(8,128)}, f32[1,24]{1,0:T(1,128)}, /*index=5*/f32[1,24]{1,0:T(1,128)}) custom-call(bf16[8,2,2,2,2,24,384]{6,5,4,3,2,1,0:T(8,128)(2,1)} %bitcast.52, bf16[8,2,2,2,2,24,384]{6,5,4,3,2,1,0:T(8,128)(2,1)} %bitcast.62, ...), custom_call_target="tpu_custom_call" | custom-call | flops 1048576 | bytes 4194304 | tf_op jit(solution)/shard_map/finish/pallas_call | solution.py:704
  (119 shorter events, 40.8 us)
Async XLA Ops:
  3.2 19.2 %collective-permute-start.1 = (s32[512]{0:T(512)S(1)}, s32[512]{0:T(512)S(1)}, u32[]{:S(2)}, u32[]{:S(2)}) collective-permute-start(s32[512]{0:T(512)S(1)} %bitcast.118), channel_id=1, source_target_pairs={{0,1},{1,0},{2,3},{3,2},{4,5},{5,4},{6,7},{7,6},{8,9},{9,8},{10,11... | collective-permute-start | bytes 6152 | tf_op jit(solution)/shard_map/ppermute | solution.py:496
  6.2 20.5 %collective-permute-start = (bf16[512,768]{1,0:T(8,128)(2,1)S(1)}, bf16[512,768]{1,0:T(8,128)(2,1)S(1)}, u32[]{:S(2)}, u32[]{:S(2)}) collective-permute-start(bf16[512,768]{1,0:T(8,128)(2,1)S(1)} %get-tuple-element.116), channel_id=1, source_target_pairs={{0,1},{1,0},{2,3},{3,2},{4,5},{5,4},{6,7},{7,6},{8,9},{9,8},{10,11... | collective-permute-start | bytes 2359304 | tf_op jit(solution)/shard_map/ppermute | solution.py:496
  7.3 60.9 %collective-permute-start.2 = (bf16[512,768]{1,0:T(8,128)(2,1)S(1)}, bf16[512,768]{1,0:T(8,128)(2,1)S(1)}, u32[]{:S(2)}, u32[]{:S(2)}) collective-permute-start(bf16[512,768]{1,0:T(8,128)(2,1)S(1)} %get-tuple-element.226), channel_id=1, source_target_pairs={{0,1},{1,0},{2,3},{3,2},{4,5},{5,4},{6,7},{7,6},{8,9},{9,8},{10,11... | collective-permute-start | bytes 2359304 | tf_op jit(solution)/shard_map/ppermute | solution.py:496
  118.8 25.2 %collective-permute-start.3 = (bf16[128,24,384]{2,1,0:T(8,128)(2,1)}, bf16[128,24,384]{2,1,0:T(8,128)(2,1)S(1)}, u32[]{:S(2)}, u32[]{:S(2)}) collective-permute-start(bf16[128,24,384]{2,1,0:T(8,128)(2,1)} %bitcast.120), channel_id=1, source_target_pairs={{0,2},{1,3},{2,0},{3,1},{4,6},{5,7},{6,4},{7,5},{8,10},{9,11},{10,... | collective-permute-start | bytes 7077896 | tf_op jit(solution)/shard_map/ppermute | solution.py:513
  118.9 25.1 %collective-permute-start.4 = (bf16[128,24,384]{2,1,0:T(8,128)(2,1)}, bf16[128,24,384]{2,1,0:T(8,128)(2,1)}, u32[]{:S(2)}, u32[]{:S(2)}) collective-permute-start(bf16[128,24,384]{2,1,0:T(8,128)(2,1)} %bitcast.119), channel_id=1, source_target_pairs={{0,2},{1,3},{2,0},{3,1},{4,6},{5,7},{6,4},{7,5},{8,10},{9,11},{10,... | collective-permute-start | bytes 7077896 | tf_op jit(solution)/shard_map/ppermute | solution.py:513
  119.9 24.1 %collective-permute-start.5 = (bf16[512,768]{1,0:T(8,128)(2,1)}, bf16[512,768]{1,0:T(8,128)(2,1)S(1)}, u32[]{:S(2)}, u32[]{:S(2)}) collective-permute-start(bf16[512,768]{1,0:T(8,128)(2,1)} %get-tuple-element.132), channel_id=1, source_target_pairs={{0,1},{1,0},{2,3},{3,2},{4,5},{5,4},{6,7},{7,6},{8,9},{9,8},{10,11... | collective-permute-start | bytes 2359304 | tf_op jit(solution)/shard_map/ppermute | solution.py:496
  149.1 38.9 %collective-permute-start.6 = (bf16[64,24,384]{2,1,0:T(8,128)(2,1)}, bf16[64,24,384]{2,1,0:T(8,128)(2,1)S(1)}, u32[]{:S(2)}, u32[]{:S(2)}) collective-permute-start(bf16[64,24,384]{2,1,0:T(8,128)(2,1)} %get-tuple-element.147), channel_id=1, source_target_pairs={{0,4},{1,5},{2,6},{3,7},{4,0},{5,1},{6,2},{7,3},{8,12},{9,13},{10,... | collective-permute-start | bytes 3538952 | tf_op jit(solution)/shard_map/ppermute | solution.py:513
  151.1 37.0 %collective-permute-start.7 = (bf16[64,24,384]{2,1,0:T(8,128)(2,1)}, bf16[64,24,384]{2,1,0:T(8,128)(2,1)S(1)}, u32[]{:S(2)}, u32[]{:S(2)}) collective-permute-start(bf16[64,24,384]{2,1,0:T(8,128)(2,1)} %get-tuple-element.148), channel_id=1, source_target_pairs={{0,8},{1,9},{2,10},{3,11},{4,12},{5,13},{6,14},{7,15},{8,0},{9,1},... | collective-permute-start | bytes 3538952 | tf_op jit(solution)/shard_map/ppermute | solution.py:513
  155.3 32.7 %collective-permute-start.8 = (bf16[64,24,384]{2,1,0:T(8,128)(2,1)}, bf16[64,24,384]{2,1,0:T(8,128)(2,1)S(1)}, u32[]{:S(2)}, u32[]{:S(2)}) collective-permute-start(bf16[64,24,384]{2,1,0:T(8,128)(2,1)} %bitcast.121), channel_id=1, source_target_pairs={{0,2},{1,3},{2,0},{3,1},{4,6},{5,7},{6,4},{7,5},{8,10},{9,11},{10,... | collective-permute-start | bytes 3538952 | tf_op jit(solution)/shard_map/ppermute | solution.py:513
  193.4 16.0 %collective-permute-start.9 = (bf16[32,24,384]{2,1,0:T(8,128)(2,1)}, bf16[32,24,384]{2,1,0:T(8,128)(2,1)S(1)}, u32[]{:S(2)}, u32[]{:S(2)}) collective-permute-start(bf16[32,24,384]{2,1,0:T(8,128)(2,1)} %get-tuple-element.158), channel_id=1, source_target_pairs={{0,1},{1,0},{2,3},{3,2},{4,5},{5,4},{6,7},{7,6},{8,9},{9,8},{10,11... | collective-permute-start | bytes 1769480 | tf_op jit(solution)/shard_map/ppermute | solution.py:513
  193.4 16.0 %collective-permute-start.10 = (bf16[32,24,384]{2,1,0:T(8,128)(2,1)}, bf16[32,24,384]{2,1,0:T(8,128)(2,1)S(1)}, u32[]{:S(2)}, u32[]{:S(2)}) collective-permute-start(bf16[32,24,384]{2,1,0:T(8,128)(2,1)} %get-tuple-element.159), channel_id=1, source_target_pairs={{0,4},{1,5},{2,6},{3,7},{4,0},{5,1},{6,2},{7,3},{8,12},{9,13},{10,... | collective-permute-start | bytes 1769480 | tf_op jit(solution)/shard_map/ppermute | solution.py:513
  193.6 15.9 %collective-permute-start.11 = (bf16[32,24,384]{2,1,0:T(8,128)(2,1)}, bf16[32,24,384]{2,1,0:T(8,128)(2,1)S(1)}, u32[]{:S(2)}, u32[]{:S(2)}) collective-permute-start(bf16[32,24,384]{2,1,0:T(8,128)(2,1)} %get-tuple-element.160), channel_id=1, source_target_pairs={{0,8},{1,9},{2,10},{3,11},{4,12},{5,13},{6,14},{7,15},{8,0},{9,1},... | collective-permute-start | bytes 1769480 | tf_op jit(solution)/shard_map/ppermute | solution.py:513
  193.7 15.9 %collective-permute-start.12 = (bf16[48,24,384]{2,1,0:T(8,128)(2,1)}, bf16[48,24,384]{2,1,0:T(8,128)(2,1)S(1)}, u32[]{:S(2)}, u32[]{:S(2)}) collective-permute-start(bf16[48,24,384]{2,1,0:T(8,128)(2,1)} %bitcast.122), channel_id=1, source_target_pairs={{0,2},{1,3},{2,0},{3,1},{4,6},{5,7},{6,4},{7,5},{8,10},{9,11},{10,... | collective-permute-start | bytes 2654216 | tf_op jit(solution)/shard_map/ppermute | solution.py:513
  214.7 15.2 %collective-permute-start.14 = (bf16[32,24,384]{2,1,0:T(8,128)(2,1)}, bf16[32,24,384]{2,1,0:T(8,128)(2,1)S(1)}, u32[]{:S(2)}, u32[]{:S(2)}) collective-permute-start(bf16[32,24,384]{2,1,0:T(8,128)(2,1)} %get-tuple-element.174), channel_id=1, source_target_pairs={{0,1},{1,0},{2,3},{3,2},{4,5},{5,4},{6,7},{7,6},{8,9},{9,8},{10,11... | collective-permute-start | bytes 1769480 | tf_op jit(solution)/shard_map/ppermute | solution.py:513
  216.3 11.4 %collective-permute-start.15 = (bf16[24,24,384]{2,1,0:T(8,128)(2,1)}, bf16[24,24,384]{2,1,0:T(8,128)(2,1)S(1)}, u32[]{:S(2)}, u32[]{:S(2)}) collective-permute-start(bf16[24,24,384]{2,1,0:T(8,128)(2,1)} %get-tuple-element.175), channel_id=1, source_target_pairs={{0,4},{1,5},{2,6},{3,7},{4,0},{5,1},{6,2},{7,3},{8,12},{9,13},{10,... | collective-permute-start | bytes 1327112 | tf_op jit(solution)/shard_map/ppermute | solution.py:513
  217.8 8.0 %collective-permute-start.13 = (bf16[16,24,384]{2,1,0:T(8,128)(2,1)}, bf16[16,24,384]{2,1,0:T(8,128)(2,1)S(1)}, u32[]{:S(2)}, u32[]{:S(2)}) collective-permute-start(bf16[16,24,384]{2,1,0:T(8,128)(2,1)} %get-tuple-element.173), channel_id=1, source_target_pairs={{0,8},{1,9},{2,10},{3,11},{4,12},{5,13},{6,14},{7,15},{8,0},{9,1},... | collective-permute-start | bytes 884744 | tf_op jit(solution)/shard_map/ppermute | solution.py:513
  218.1 7.7 %collective-permute-start.16 = (bf16[16,24,384]{2,1,0:T(8,128)(2,1)S(1)}, bf16[16,24,384]{2,1,0:T(8,128)(2,1)S(1)}, u32[]{:S(2)}, u32[]{:S(2)}) collective-permute-start(bf16[16,24,384]{2,1,0:T(8,128)(2,1)S(1)} %bitcast.123), channel_id=1, source_target_pairs={{0,2},{1,3},{2,0},{3,1},{4,6},{5,7},{6,4},{7,5},{8,10},{9,11},{10,... | collective-permute-start | bytes 884744 | tf_op jit(solution)/shard_map/ppermute | solution.py:513
  229.9 48.6 %collective-permute-start.24 = (bf16[512,768]{1,0:T(8,128)(2,1)}, bf16[512,768]{1,0:T(8,128)(2,1)S(1)}, u32[]{:S(2)}, u32[]{:S(2)}) collective-permute-start(bf16[512,768]{1,0:T(8,128)(2,1)} %after.2), channel_id=1, source_target_pairs={{0,1},{1,0},{2,3},{3,2},{4,5},{5,4},{6,7},{7,6},{8,9},{9,8},{10,11... | collective-permute-start | bytes 2359304 | tf_op jit(solution)/shard_map/ppermute | solution.py:496
  234.6 16.0 %collective-permute-start.17 = (bf16[16,24,384]{2,1,0:T(8,128)(2,1)}, bf16[16,24,384]{2,1,0:T(8,128)(2,1)S(1)}, u32[]{:S(2)}, u32[]{:S(2)}) collective-permute-start(bf16[16,24,384]{2,1,0:T(8,128)(2,1)} %get-tuple-element.196), channel_id=1, source_target_pairs={{0,16},{1,17},{2,18},{3,19},{4,20},{5,21},{6,22},{7,23},{8,24},{9,... | collective-permute-start | bytes 884744 | tf_op jit(solution)/shard_map/ppermute | solution.py:513
  238.3 18.0 %collective-permute-start.19 = (bf16[16,24,384]{2,1,0:T(8,128)(2,1)}, bf16[16,24,384]{2,1,0:T(8,128)(2,1)S(1)}, u32[]{:S(2)}, u32[]{:S(2)}) collective-permute-start(bf16[16,24,384]{2,1,0:T(8,128)(2,1)} %get-tuple-element.198), channel_id=1, source_target_pairs={{0,1},{1,0},{2,3},{3,2},{4,5},{5,4},{6,7},{7,6},{8,9},{9,8},{10,11... | collective-permute-start | bytes 884744 | tf_op jit(solution)/shard_map/ppermute | solution.py:513
  239.6 10.0 %collective-permute-start.18 = (bf16[12,24,384]{2,1,0:T(8,128)(2,1)}, bf16[12,24,384]{2,1,0:T(8,128)(2,1)S(1)}, u32[]{:S(2)}, u32[]{:S(2)}) collective-permute-start(bf16[12,24,384]{2,1,0:T(8,128)(2,1)} %get-tuple-element.197), channel_id=1, source_target_pairs={{0,4},{1,5},{2,6},{3,7},{4,0},{5,1},{6,2},{7,3},{8,12},{9,13},{10,... | collective-permute-start | bytes 663560 | tf_op jit(solution)/shard_map/ppermute | solution.py:513
  240.5 9.0 %collective-permute-start.20 = (bf16[4,24,384]{2,1,0:T(8,128)(2,1)}, bf16[4,24,384]{2,1,0:T(8,128)(2,1)S(1)}, u32[]{:S(2)}, u32[]{:S(2)}) collective-permute-start(bf16[4,24,384]{2,1,0:T(8,128)(2,1)} %get-tuple-element.199), channel_id=1, source_target_pairs={{0,5},{1,4},{2,7},{3,6},{4,1},{5,0},{6,3},{7,2},{8,13},{9,12},{10,... | collective-permute-start | bytes 221192 | tf_op jit(solution)/shard_map/ppermute | solution.py:513
  260.2 9.6 %collective-permute-start.23 = (bf16[4,24,384]{2,1,0:T(8,128)(2,1)}, bf16[4,24,384]{2,1,0:T(8,128)(2,1)S(1)}, u32[]{:S(2)}, u32[]{:S(2)}) collective-permute-start(bf16[4,24,384]{2,1,0:T(8,128)(2,1)} %get-tuple-element.206), channel_id=1, source_target_pairs={{0,24},{1,25},{2,26},{3,27},{4,28},{5,29},{6,30},{7,31},{8,16},{9,... | collective-permute-start | bytes 221192 | tf_op jit(solution)/shard_map/ppermute | solution.py:513
  265.0 9.3 %collective-permute-start.21 = (bf16[8,24,384]{2,1,0:T(8,128)(2,1)}, bf16[8,24,384]{2,1,0:T(8,128)(2,1)S(1)}, u32[]{:S(2)}, u32[]{:S(2)}) collective-permute-start(bf16[8,24,384]{2,1,0:T(8,128)(2,1)} %get-tuple-element.204), channel_id=1, source_target_pairs={{0,16},{1,17},{2,18},{3,19},{4,20},{5,21},{6,22},{7,23},{8,24},{9,... | collective-permute-start | bytes 442376 | tf_op jit(solution)/shard_map/ppermute | solution.py:513
  (31 other events, 138.7 us)

commit v4 on v3

--- a/solution.py
+++ b/solution.py
@@ -52,7 +52,7 @@
             e = jnp.exp2(s - top)
             row = jnp.sum(e, axis=-1, keepdims=True)
             out = mm(e.astype(jnp.bfloat16), v_ref[pl.ds(begin, width), :])
-            total[...] = jnp.where(lane == h, out / row, total[...])
+            total[...] = jnp.where(lane == h, out * (1.0 / row), total[...])
             place = jnp.where(h < GROUP // 2, h, h + GROUP // 2)
             return jnp.where(lane_head == place, top + jnp.log2(row), logs)
 
@@ -108,11 +108,10 @@
         gq_t[...] = jnp.zeros_like(gq_t)
         q_t[...] = jnp.transpose(q_ref[...])
         up_t[...] = jnp.transpose(up_ref[...])
-        pick = (lax.div(lax.broadcasted_iota(jnp.int32, (8, lanes), 1), HEAD_DIM)
-                == lax.broadcasted_iota(jnp.int32, (8, lanes), 0)).astype(jnp.float32)
-        product = up_ref[...].astype(jnp.float32) * o_ref[...].astype(jnp.float32)
-        inner[...] = lax.dot_general(pick, product, NT, precision=lax.Precision.HIGHEST,
-                                     preferred_element_type=jnp.float32)
+        product = up_t[...].astype(jnp.float32) * jnp.transpose(o_ref[...]).astype(jnp.float32)
+        for h in range(heads):
+            rows = slice(h * HEAD_DIM, (h + 1) * HEAD_DIM)
+            inner[h:h + 1, :] = jnp.sum(product[rows], axis=0, keepdims=True)
 
     key_t[...] = jnp.transpose(k_ref[...])
     value_t[...] = jnp.transpose(v_ref[...])
@@ -120,15 +119,19 @@
     def span(width):
         begin = pl.multiple_of(j * bk, bk)
         here = pl.ds(begin, width)
-        seg_k = jnp.transpose(jnp.broadcast_to(seg_ref[0:1, pl.ds(begin, bk)], (128, bk)))[:, 0:1]
-        place_k = lax.broadcasted_iota(jnp.int32, (bk, width), 0)
-        place_q = lax.broadcasted_iota(jnp.int32, (bk, width), 1)
-        allowed = (place_k <= place_q) & (seg_k == seg_ref[0:1, here])
-        bias[:, :width] = jnp.where(allowed, 0.0, masked_score)
+
+        @pl.when(g == 0)
+        def _():
+            seg_k = jnp.transpose(jnp.broadcast_to(seg_ref[0:1, pl.ds(begin, bk)], (128, bk)))[:, 0:1]
+            place_k = lax.broadcasted_iota(jnp.int32, (bk, width), 0)
+            place_q = lax.broadcasted_iota(jnp.int32, (bk, width), 1)
+            allowed = (place_k <= place_q) & (seg_k == seg_ref[0:1, here])
+            bias[j, :, :width] = jnp.where(allowed, 0.0, masked_score)
+
         for h in range(heads):
             rows = slice(h * HEAD_DIM, (h + 1) * HEAD_DIM)
             key, value = jnp.transpose(key_t[rows, :]), jnp.transpose(value_t[rows, :])
-            s = mm(key, q_t[rows, here]) * SCALE2 + (bias[:, :width] - lse_ref[h:h + 1, here])
+            s = mm(key, q_t[rows, here]) * SCALE2 + (bias[j, :, :width] - lse_ref[h:h + 1, here])
             p = jnp.exp2(s)
             dp = mm(value, up_t[rows, here])
             ds = (p * (dp - inner[h:h + 1, here])).astype(jnp.bfloat16)
@@ -190,7 +193,7 @@
         ],
         out_specs=[out, out, out, split, split],
         scratch_shapes=[
-            pltpu.VMEM((bk, length), jnp.float32),
+            pltpu.VMEM((length // bk, bk, length), jnp.float32),
             pltpu.VMEM((8, length), jnp.float32),
             pltpu.VMEM((SMALL, bk), jnp.bfloat16),
             pltpu.VMEM((SMALL, bk), jnp.bfloat16),
@@ -387,8 +390,8 @@
         out_other[...] = total[other, :].astype(jnp.bfloat16)
         for at in pieces:
             grad = gy[at, :].astype(jnp.float32) + norm_back(x1[at, :], gain_ref[...], back[at, :])
+            grad = grad.astype(jnp.bfloat16)
             gx_ref[at, :] = grad
-            grad = grad.astype(jnp.bfloat16)
             branch.append(grad)
             go_ref[at, :] = mm(grad, w_out_ref[...], NT).astype(jnp.bfloat16)
             flat[:, at] = jnp.transpose(o_ref[at, :].astype(jnp.float32))
@@ -446,7 +449,7 @@
         grid_spec=grid_spec,
         out_shape=[
             shape((window, width), bf16), shape((window, width), bf16),
-            shape((length, width), jnp.float32), shape((length, width), bf16),
+            shape((length, width), bf16), shape((length, width), bf16),
             *[shape(size, bf16) for size in (up_shape, up_shape, down_shape, down_shape, out_shape, out_shape)],
         ],
         compiler_params=pltpu.CompilerParams(vmem_limit_bytes=60 << 20),
@@ -457,17 +460,10 @@
 
 def after_kernel(place, x_ref, gain_ref, gx_ref, w_ref, *refs):
     out_ref = refs[-1]
-    width = x_ref.shape[1]
-    back = jnp.zeros(gx_ref.shape, jnp.float32)
-    at = 0
-    for names in zip(*[iter(refs[:-1])] * 3):
-        columns = names[0].shape[1]
-        for third, ref in enumerate(names):
-            begin = third * width + at
-            back += mm(ref[...], w_ref[:, begin:begin + columns], NT)
-        at += columns
+    grads = jnp.concatenate([ref[...] for third in range(3) for ref in refs[third:-1:3]], axis=1)
+    back = mm(grads, w_ref[...], NT)
     values = x_ref[...].astype(jnp.float32)
-    out_ref[...] = (gx_ref[...] + norm_back(values, gain_ref[...], back)).astype(out_ref.dtype)
+    out_ref[...] = (gx_ref[...].astype(jnp.float32) + norm_back(values, gain_ref[...], back)).astype(out_ref.dtype)
 
 
 def after(place, x, gain, gx, w, pieces, block=256):
@@ -530,14 +526,23 @@
                     refs[target][offset + index * count + at] = total.astype(refs[target].dtype)
             return carry
 
+        count = lead // steps if cut_up else lead
+
+        def all_of(count=count, one=one):
+            if sum(len(sources) for _, _, _, sources in targets) > 32:
+                lax.fori_loop(0, count, one, 0)
+            else:
+                for index in range(count):
+                    one(index, 0)
+
         if cut_up:
-            lax.fori_loop(0, lead // steps, one, 0)
+            all_of()
         elif steps > 1:
             @pl.when(pl.program_id(0) == 0)
             def _():
-                lax.fori_loop(0, lead, one, 0)
+                all_of()
         else:
-            lax.fori_loop(0, lead, one, 0)
+            all_of()
 
 
 class Flow:
@@ -660,7 +665,7 @@
     return value
 
 
-def finish_kernel(*refs, work, count):
+def finish_kernel(*refs, work, gains, count):
     inputs, outputs = refs[:count], refs[count:]
     for terms, targets in work:
         for lead, (target, row, column, width, parts) in enumerate(targets):
@@ -673,36 +678,26 @@
                 piece = slice(part * width, (part + 1) * width)
                 begin = column + part * (outputs[target].shape[1] // parts if parts > 1 else 0)
                 outputs[target][row:row + total.shape[0], begin:begin + width] = total[:, piece]
-    for number, source in enumerate((0, 2)):
-        weight, gain = inputs[count - 4 + 2 * number], inputs[count - 3 + 2 * number]
-        ones = jnp.ones((8, weight.shape[1]), jnp.float32)
-        sums = lax.dot_general(ones, weight[...] * outputs[source][...], NT, precision=lax.Precision.HIGHEST,
-                               preferred_element_type=jnp.float32)
-        outputs[4 + number][...] = sums[:1] / gain[...]
-
-
-def finish(up, down, out_and_one, others, out_lead, weights):
-    operands, work = Operands(), []
-    rows = up.rows
-    heads = iter(range(64))
-    third = lambda: (0, 0, next(heads) * SMALL, SMALL, 3)
-    plans = [
-        (up, [(2, 0, lead * PART, PART, 1) for lead in range(up.lead)]),
-        (down, [(3, (lead % 4) * rows, (lead // 4) * PART, PART, 1) for lead in range(down.lead)]),
-        (out_and_one, [third() for _ in range(out_and_one.lead - out_lead)]
-         + [(1, 0, lead * PART, PART, 1) for lead in range(out_lead)]),
-    ]
-    plans += [(flow, [third() for _ in range(flow.lead)]) for flow in others]
+    for source, weight, gain, target in gains:
+        product = inputs[weight][...] * outputs[source][...]
+        sums = lax.dot_general(jnp.ones((8, product.shape[1]), jnp.float32), product, NT,
+                               precision=lax.Precision.HIGHEST, preferred_element_type=jnp.float32)
+        outputs[target][...] = sums[:1] / inputs[gain][...]
+
+
+def finish(plans, sizes, gained):
+    operands, work, gains = Operands(), [], []
     gone = {bit: 0 for bit in range(64)}
     for flow, targets in plans:
         finders = [operands.finder(flow, term, gone, False) for term in flow.terms]
         work.append(([find(gone) for find in finders], targets))
-    for weight in weights:
-        operands.add(weight, pl.BlockSpec(weight.shape, lambda i: (0, 0), pipeline_mode=pl.Buffered(1)))
-    width = out_lead * PART
-    sizes = [(rows, 3 * width), (rows, width), (rows, up.lead * PART), (4 * rows, width), (1, rows), (1, rows)]
+    sizes = list(sizes)
+    for source, *arrays in gained:
+        at = [operands.add(array, pl.BlockSpec(array.shape, lambda i: (0, 0), pipeline_mode=pl.Buffered(1))) for array in arrays]
+        gains.append((source, *at, len(sizes)))
+        sizes.append((1, sizes[source][0]))
     return pl.pallas_call(
-        functools.partial(finish_kernel, work=work, count=len(operands.arrays)),
+        functools.partial(finish_kernel, work=work, gains=gains, count=len(operands.arrays)),
         grid=(1,),
         in_specs=operands.specs,
         out_specs=[pl.BlockSpec(size, lambda i: (0, 0), pipeline_mode=pl.Buffered(1)) for size in sizes],
@@ -720,7 +715,7 @@
     here = jnp.stack([dp & 1, (dp >> 1) * 2 + seq, seq]).astype(jnp.int32)
     there = jnp.stack([dp & 1, (dp >> 1) * 2 + seq, 1 - seq]).astype(jnp.int32)
     far = tuple(range(2, chips.bit_length() - 1))
-    wide = [far[at:at + 2] for at in range(0, len(far), 2)]
+    rest = [far[at:at + 2] for at in range(2, len(far), 2)]
 
     x_kept, x_sent = split_window(tokens)
     segments, cotangent, x_sent = lax.optimization_barrier((segments, cotangent, x_sent))
@@ -756,10 +751,10 @@
     one = heads_back(0, 2, [*near[:1], (0,), (1,), *near[1:]], (keep_out, send_out))
     out_other = arrive(moving, out_other)
     (go, out_other), moving = leave([up, down, one], (go, out_other), 2)
-    two = heads_back(2, 3, [(1,), (0,), *wide])
+    two = heads_back(2, 3, [(1,), *near[:1], (0, *far[1:2]), *rest])
     arrive(moving)
     go, moving = leave([up, down, one, two], go, 2)
-    three = heads_back(5, 1, [(0, 1), *wide])
+    three = heads_back(5, 1, [(1, *far[:1]), (0, *far[1:2]), *rest])
     arrive(moving)
     flows = [up, down, one, two, three]
     gx, moving = leave(flows, gx)
@@ -769,17 +764,36 @@
     rows_back = swapped(other_rows)
     gx, moving = leave(flows, gx)
     kept_rows = after(here, x_kept, gain_one, gx, w_qkv, pieces)
+    kept_rows, rows_back = arrive(moving, (kept_rows, rows_back))
+    rows, width = up.rows, w_out.shape[1]
+    w_qkv_rows, gain_one_rows, w_up_rows, gain_two_rows = weights
+
+    def finish_ffn(w_rows):
+        return finish([
+            (up, [(0, 0, lead * PART, PART, 1) for lead in range(up.lead)]),
+            (down, [(1, (lead % 4) * rows, (lead // 4) * PART, PART, 1) for lead in range(down.lead)]),
+        ], [(rows, up.lead * PART), (4 * rows, width)], [(0, w_rows, gain_two_rows)])
+
+    soon = not (up.plan or down.plan)
+    (kept_rows, rows_back, w_up_rows), moving = leave(flows, (kept_rows, rows_back, w_up_rows))
+    ffn_grads = finish_ffn(w_up_rows) if soon else None
+    grad_tokens = joined(kept_rows, rows_back)
     while True:
-        kept_rows = arrive(moving, kept_rows)
+        ffn_grads, grad_tokens = arrive(moving, (ffn_grads, grad_tokens))
         if not any(flow.plan for flow in flows):
             break
         _, moving = leave(flows)
-    grad_qkv, grad_out, grad_up, grad_down, grad_gain_attn, grad_gain_ffn = finish(
-        up, down, one, [two, three], w_out.shape[1] // PART, weights
-    )
+    grad_up, grad_down, grad_gain_ffn = ffn_grads or finish_ffn(w_up_rows)
+    out_lead, group = width // PART, iter(range(64))
+    of_group = lambda flow, extra=0: [(0, 0, next(group) * SMALL, SMALL, 3) for _ in range(flow.lead - extra)]
+    grad_qkv, grad_out, grad_gain_attn = finish([
+        (one, of_group(one, out_lead) + [(1, 0, lead * PART, PART, 1) for lead in range(out_lead)]),
+        (two, of_group(two)),
+        (three, of_group(three)),
+    ], [(rows, 3 * width), (rows, width)], [(0, w_qkv_rows, gain_one_rows)])
     return (
         joined(out_kept, out_other),
-        joined(kept_rows, rows_back),
+        grad_tokens,
         grad_qkv,
         grad_out,
         grad_up,

time: 285 us -> 275 us (0.965)
  waiting for transfers between devices: 23.8 us -> 17.3 us
    ppermute x20, waiting for transfers between devices: 21.1 us -> 14.5 us  [crossed(): lax.ppermute(block, ('dp', 'seq'), [(i, i ^ step) for i in range(count)])]
    unnamed x60 -> x62, local copies, waits for them, and re-layouts: 7.74 us -> 7.72 us
  transfers between devices with their start and end apart: 25 -> 25, of which waited for: 10 -> 9; matrix products, arithmetic and copies ran while one was open for 4% -> 4% of each run, Pallas kernels for 51% -> 51%
where the time goes in v4:
time: 275 us; the launch traced here: 271 us
  Pallas kernels  202 us (73%)
  starting transfers between devices  28.6 us (10%)
  waiting for transfers between devices  17.3 us (6%)
  local copies, waits for them, and re-layouts  13.2 us (5%)
  other arithmetic  8.56 us (3%)
    pallas_call x3, Pallas kernels, attend_back(): pl.pallas_call(functools.partial(attend_back_kernel, bk=bk), grid_spec=gr...  68.5 us
    pallas_call x1, Pallas kernels, middle(): pl.pallas_call(functools.partial(middle_kernel, shards=shards, block=bloc...  49.2 us
    pallas_call x1, Pallas kernels, attend(): pl.pallas_call(functools.partial(attend_kernel, bq=bq, unroll=unroll), gr...  33.3 us
    ppermute x20, starting transfers between devices, crossed(): lax.ppermute(block, ('dp', 'seq'), [(i, i ^ step) for i in range(count)])  21.8 us
    pallas_call x5, Pallas kernels, combine(): pl.pallas_call(functools.partial(combine_kernel, work=work, steps=steps),...  16.3 us
    pallas_call x2, Pallas kernels, before(): pl.pallas_call(functools.partial(before_kernel, shards=shards, block=bloc...  14.7 us
    ppermute x20, waiting for transfers between devices, crossed(): lax.ppermute(block, ('dp', 'seq'), [(i, i ^ step) for i in range(count)])  14.5 us
    pallas_call x2, Pallas kernels, after(): pl.pallas_call(after_kernel, grid_spec=grid_spec, out_shape=jax.ShapeDtyp...  14.3 us
  transfers between devices with their start and end apart: 25, of which 9 were waited for; matrix products, arithmetic and copies ran while one was open for 4% of the time, Pallas kernels for 51%

profile of v4, /device:TPU:0, one launch (start us, length us, event | category | flops | bytes accessed | tf_op | source)
XLA Modules:
  0.0 270.6 jit_solution(6987458958895245936)
XLA Ops:
  0.7 2.5 dynamic-slice_bitcast_fusion.2
  3.2 3.0 %collective-permute-start.1 = (s32[512]{0:T(512)S(1)}, s32[512]{0:T(512)S(1)}, u32[]{:S(2)}, u32[]{:S(2)}) collective-permute-start(s32[512]{0:T(512)S(1)} %bitcast.118), channel_id=1, source_target_pairs={{0,1},{1,0},{2,3},{3,2},{4,5},{5,4},{6,7},{7,6},{8,9},{9,8},{10,11... | collective-permute-start | bytes 6152 | tf_op jit(solution)/shard_map/ppermute | solution.py:492
  13.7 7.4 %before.2 = (bf16[1024,2304]{1,0:T(8,128)(2,1)}, bf16[768,1024]{1,0:T(8,128)(2,1)}) custom-call(s32[3]{0:T(128)} %get-tuple-element.252.place, bf16[512,768]{1,0:T(8,128)(2,1)} %get-tuple-element.249.x_ref.x_kept, f32[1,768]{1,0:T(1,128)} %broadcast_in_dim.17.gain_ref, bf16[768,2304]{1,0:T(8,128)(2,1)} %w_ref.7), custom_call_target="tpu_custom_call" | custom-call | flops 1811939328 | bytes 12582912 | tf_op jit(solution)/shard_map/before/pallas_call | solution.py:315
  23.9 2.8 %collective-permute-done.x_ref.x_other = bf16[512,768]{1,0:T(8,128)(2,1)S(1)} collective-permute-done((bf16[512,768]{1,0:T(8,128)(2,1)S(1)}, bf16[512,768]{1,0:T(8,128)(2,1)S(1)}, u32[]{:S(2)}, u32[]{:S(2)}) %collective-permute-start) | collective-permute-done | bytes 786464 | tf_op jit(solution)/shard_map/ppermute | solution.py:492
  27.6 7.3 %before.3 = (bf16[1024,2304]{1,0:T(8,128)(2,1)}, bf16[768,1024]{1,0:T(8,128)(2,1)}) custom-call(s32[3]{0:T(128)} %get-tuple-element.253.place, bf16[512,768]{1,0:T(8,128)(2,1)} %copy-done.10, f32[1,768]{1,0:T(1,128)} %broadcast_in_dim.17.gain_ref, bf16[768,2304]{1,0:T(8,128)(2,1)} %w_ref.7, ...), custom_call_target="tpu_custom_call", output_to_operand_aliasing={{0}: (4, {}), {1}: (5, {})} | custom-call | flops 1811939328 | bytes 12582912 | tf_op jit(solution)/shard_map/before/pallas_call | solution.py:315
  34.9 33.3 %attend.1 = (bf16[1024,768]{1,0:T(8,128)(2,1)}, f32[48,1024]{1,0:T(8,128)}) custom-call(s32[4]{0:T(128)} %and_select_fusion.1.first, s32[1,1024]{1,0:T(1,128)} %broadcast_select_fusion.seg_ref, bf16[1024,2304]{1,0:T(8,128)(2,1)} %get-tuple-element.131.q_ref.k_ref.v_ref, bf16[1024,2304]{1,0:T(8,128)(2,1)} %get-tuple-element.131.q_ref.k_ref.v_ref, ...), custom_call_target="tpu_custom_call" | custom-call | flops 30064771072 | bytes 8388608 | tf_op jit(solution)/shard_map/attend/pallas_call | solution.py:86
  69.1 49.2 %middle.1 = (bf16[512,768]{1,0:T(8,128)(2,1)}, bf16[512,768]{1,0:T(8,128)(2,1)}, bf16[1024,768]{1,0:T(8,128)(2,1)}, bf16[1024,768]{1,0:T(8,128)(2,1)}, bf16[8,16...) custom-call(s32[3]{0:T(128)} %get-tuple-element.252.place, ...), custom_call_target="tpu_custom_call" | custom-call | flops 28991029248 | bytes 41943040 | tf_op jit(solution)/shard_map/middle/pallas_call | solution.py:447
  119.4 23.8 %attend_back.3 = (bf16[1024,256]{1,0:T(8,128)(2,1)}, bf16[1024,256]{1,0:T(8,128)(2,1)}, bf16[1024,256]{1,0:T(8,128)(2,1)}, bf16[4,16,24,384]{3,2,1,0:T(8,128)(2,1)}, bf16[4,16,24,384]{3,2,1,0:T(8,128)(2,1)}) custom-call(s32[4]{0:T(128)} %and_select_fusion.last, s32[1,1024]{1,0:T(1,128)} %broadcast_select_fusion.seg_ref, ...), custom_call_target="tpu_custom_call" | custom-call | flops 21474836480 | bytes 8388608 | tf_op jit(solution)/shard_map/attend_back/pallas_call | solution.py:209
  144.7 3.5 %combine.5 = (bf16[64,24,384]{2,1,0:T(8,128)(2,1)}, bf16[64,24,384]{2,1,0:T(8,128)(2,1)}) custom-call(bf16[8,2,2,2,2,24,384]{6,5,4,3,2,1,0:T(8,128)(2,1)} %bitcast.48, bf16[8,2,2,2,2,24,384]{6,5,4,3,2,1,0:T(8,128)(2,1)} %bitcast.58, bf16[8,2,2,2,2,24,384]{6,5,4,3,2,1,0:T(8,128)(2,1)} %bitcast.53, ...), custom_call_target="tpu_custom_call" | custom-call | flops 1048576 | bytes 8388608 | tf_op jit(solution)/shard_map/combine/pallas_call | solution.py:629
  150.2 2.2 collective-permute-start.7
  152.9 32.0 %attend_back.4 = (bf16[1024,384]{1,0:T(8,128)(2,1)}, bf16[1024,384]{1,0:T(8,128)(2,1)}, bf16[1024,384]{1,0:T(8,128)(2,1)}, bf16[3,16,24,384]{3,2,1,0:T(8,128)(2,1)}, bf16[3,16,24,384]{3,2,1,0:T(8,128)(2,1)}) custom-call(s32[4]{0:T(128)} %and_select_fusion.last, s32[1,1024]{1,0:T(1,128)} %broadcast_select_fusion.seg_ref, ...), custom_call_target="tpu_custom_call" | custom-call | flops 32212254720 | bytes 8388608 | tf_op jit(solution)/shard_map/attend_back/pallas_call | solution.py:209
  186.7 3.5 %combine.6 = (bf16[32,24,384]{2,1,0:T(8,128)(2,1)}, bf16[32,24,384]{2,1,0:T(8,128)(2,1)}, bf16[32,24,384]{2,1,0:T(8,128)(2,1)}) custom-call(bf16[8,2,2,2,2,24,384]{6,5,4,3,2,1,0:T(8,128)(2,1)} %bitcast.49, bf16[8,2,2,2,2,24,384]{6,5,4,3,2,1,0:T(8,128)(2,1)} %bitcast.59, bf16[8,2,2,2,24,384]{5,4,3,2,1,0:T(8,128)(2,1)} %bitcast.73, ...), custom_call_target="tpu_custom_call" | custom-call | flops 1048576 | bytes 8388608 | tf_op jit(solution)/shard_map/combine/pallas_call | solution.py:629
  194.5 12.8 %attend_back.5 = (bf16[1024,128]{1,0:T(8,128)(2,1)}, bf16[1024,128]{1,0:T(8,128)(2,1)}, bf16[1024,128]{1,0:T(8,128)(2,1)}, bf16[1,16,24,384]{3,2,1,0:T(8,128)(2,1)}, bf16[1,16,24,384]{3,2,1,0:T(8,128)(2,1)}) custom-call(s32[4]{0:T(128)} %and_select_fusion.last, s32[1,1024]{1,0:T(1,128)} %broadcast_select_fusion.seg_ref, ...), custom_call_target="tpu_custom_call" | custom-call | flops 10737418240 | bytes 8388608 | tf_op jit(solution)/shard_map/attend_back/pallas_call | solution.py:209
  210.2 3.5 %combine.7 = (bf16[16,24,384]{2,1,0:T(8,128)(2,1)}, bf16[32,24,384]{2,1,0:T(8,128)(2,1)}, bf16[24,24,384]{2,1,0:T(8,128)(2,1)}) custom-call(bf16[8,2,2,2,2,24,384]{6,5,4,3,2,1,0:T(8,128)(2,1)} %bitcast.50, bf16[8,2,2,2,2,24,384]{6,5,4,3,2,1,0:T(8,128)(2,1)} %bitcast.60, bf16[8,2,2,2,24,384]{5,4,3,2,1,0:T(8,128)(2,1)} %bitcast.74, ...), custom_call_target="tpu_custom_call" | custom-call | flops 1048576 | bytes 8388608 | tf_op jit(solution)/shard_map/combine/pallas_call | solution.py:629
  216.1 7.1 %after.2 = bf16[512,768]{1,0:T(8,128)(2,1)} custom-call(s32[3]{0:T(128)} %get-tuple-element.253.place, bf16[512,768]{1,0:T(8,128)(2,1)} %copy-done.10, f32[1,768]{1,0:T(1,128)} %broadcast_in_dim.17.gain_ref, bf16[1024,768]{1,0:T(8,128)(2,1)} %get-tuple-element.210.gx_ref, bf16[768,2304]{1,0:T(8,128)(2,1)} %w_ref.7, ...), custom_call_target="tpu_custom_call" | custom-call | flops 1811939328 | bytes 16777216 | tf_op jit(solution)/shard_map/after/pallas_call | solution.py:481
  223.8 3.1 %collective-permute-done.15 = bf16[24,24,384]{2,1,0:T(8,128)(2,1)S(1)} collective-permute-done((bf16[24,24,384]{2,1,0:T(8,128)(2,1)}, bf16[24,24,384]{2,1,0:T(8,128)(2,1)S(1)}, u32[]{:S(2)}, u32[]{:S(2)}) %collective-permute-start.15) | collective-permute-done | bytes 442400 | tf_op jit(solution)/shard_map/ppermute | solution.py:509
  230.4 3.3 %combine.8 = (bf16[16,24,384]{2,1,0:T(8,128)(2,1)}, bf16[12,24,384]{2,1,0:T(8,128)(2,1)}, bf16[16,24,384]{2,1,0:T(8,128)(2,1)}, bf16[4,24,384]{2,1,0:T(8,128)(2,1)}) custom-call(bf16[8,2,2,2,2,24,384]{6,5,4,3,2,1,0:T(8,128)(2,1)} %bitcast.51, bf16[8,2,2,2,2,24,384]{6,5,4,3,2,1,0:T(8,128)(2,1)} %bitcast.61, bf16[8,2,2,2,24,384]{5,4,3,2,1,0:T(8,128)(2,1)} %bitcast.75, ...), custom_call_target="tpu_custom_call" | custom-call | flops 1048576 | bytes 8388608 | tf_op jit(solution)/shard_map/combine/pallas_call | solution.py:629
  234.4 2.1 collective-permute-start.17
  240.7 7.2 %after.3 = bf16[512,768]{1,0:T(8,128)(2,1)} custom-call(s32[3]{0:T(128)} %get-tuple-element.252.place, bf16[512,768]{1,0:T(8,128)(2,1)} %get-tuple-element.249.x_ref.x_kept, f32[1,768]{1,0:T(1,128)} %broadcast_in_dim.17.gain_ref, bf16[1024,768]{1,0:T(8,128)(2,1)} %get-tuple-element.210.gx_ref, bf16[768,2304]{1,0:T(8,128)(2,1)} %w_ref.7, ...), custom_call_target="tpu_custom_call" | custom-call | flops 1811939328 | bytes 16777216 | tf_op jit(solution)/shard_map/after/pallas_call | solution.py:481
  247.9 4.5 %collective-permute-done.20 = bf16[4,24,384]{2,1,0:T(8,128)(2,1)S(1)} collective-permute-done((bf16[4,24,384]{2,1,0:T(8,128)(2,1)S(1)}, bf16[4,24,384]{2,1,0:T(8,128)(2,1)S(1)}, u32[]{:S(2)}, u32[]{:S(2)}) %collective-permute-start.20) | collective-permute-done | bytes 73760 | tf_op jit(solution)/shard_map/ppermute | solution.py:509
  253.3 2.5 combine.9
  257.7 2.5 collective-permute-start.22
  261.6 2.9 %finish.2 = (f32[24,3072]{1,0:T(8,128)}, f32[96,768]{1,0:T(8,128)}, f32[1,24]{1,0:T(1,128)}) custom-call(bf16[8,2,2,2,2,24,384]{6,5,4,3,2,1,0:T(8,128)(2,1)} %bitcast.52, bf16[8,2,2,2,2,24,384]{6,5,4,3,2,1,0:T(8,128)(2,1)} %bitcast.62, bf16[8,2,2,2,24,384]{5,4,3,2,1,0:T(8,128)(2,1)} %bitcast.76, bf16[8,2,2,24,384]{4,3,2,1,0:T(8,128)(2,1)} %bitcast.95, ...), custom_call_target="tpu_custom_call" | custom-call | flops 1048576 | bytes 4194304 | tf_op jit(solution)/shard_map/finish/pallas_call | solution.py:699
  267.9 2.5 finish.3
  (122 shorter events, 44.9 us)
Async XLA Ops:
  3.2 19.2 %collective-permute-start.1 = (s32[512]{0:T(512)S(1)}, s32[512]{0:T(512)S(1)}, u32[]{:S(2)}, u32[]{:S(2)}) collective-permute-start(s32[512]{0:T(512)S(1)} %bitcast.118), channel_id=1, source_target_pairs={{0,1},{1,0},{2,3},{3,2},{4,5},{5,4},{6,7},{7,6},{8,9},{9,8},{10,11... | collective-permute-start | bytes 6152 | tf_op jit(solution)/shard_map/ppermute | solution.py:492
  6.2 20.5 %collective-permute-start = (bf16[512,768]{1,0:T(8,128)(2,1)S(1)}, bf16[512,768]{1,0:T(8,128)(2,1)S(1)}, u32[]{:S(2)}, u32[]{:S(2)}) collective-permute-start(bf16[512,768]{1,0:T(8,128)(2,1)S(1)} %get-tuple-element.126), channel_id=1, source_target_pairs={{0,1},{1,0},{2,3},{3,2},{4,5},{5,4},{6,7},{7,6},{8,9},{9,8},{10,11... | collective-permute-start | bytes 2359304 | tf_op jit(solution)/shard_map/ppermute | solution.py:492
  7.3 60.9 %collective-permute-start.2 = (bf16[512,768]{1,0:T(8,128)(2,1)S(1)}, bf16[512,768]{1,0:T(8,128)(2,1)S(1)}, u32[]{:S(2)}, u32[]{:S(2)}) collective-permute-start(bf16[512,768]{1,0:T(8,128)(2,1)S(1)} %get-tuple-element.246), channel_id=1, source_target_pairs={{0,1},{1,0},{2,3},{3,2},{4,5},{5,4},{6,7},{7,6},{8,9},{9,8},{10,11... | collective-permute-start | bytes 2359304 | tf_op jit(solution)/shard_map/ppermute | solution.py:492
  118.3 25.0 %collective-permute-start.3 = (bf16[128,24,384]{2,1,0:T(8,128)(2,1)}, bf16[128,24,384]{2,1,0:T(8,128)(2,1)S(1)}, u32[]{:S(2)}, u32[]{:S(2)}) collective-permute-start(bf16[128,24,384]{2,1,0:T(8,128)(2,1)} %bitcast.120), channel_id=1, source_target_pairs={{0,2},{1,3},{2,0},{3,1},{4,6},{5,7},{6,4},{7,5},{8,10},{9,11},{10,... | collective-permute-start | bytes 7077896 | tf_op jit(solution)/shard_map/ppermute | solution.py:509
  118.4 24.9 %collective-permute-start.4 = (bf16[128,24,384]{2,1,0:T(8,128)(2,1)}, bf16[128,24,384]{2,1,0:T(8,128)(2,1)}, u32[]{:S(2)}, u32[]{:S(2)}) collective-permute-start(bf16[128,24,384]{2,1,0:T(8,128)(2,1)} %bitcast.119), channel_id=1, source_target_pairs={{0,2},{1,3},{2,0},{3,1},{4,6},{5,7},{6,4},{7,5},{8,10},{9,11},{10,... | collective-permute-start | bytes 7077896 | tf_op jit(solution)/shard_map/ppermute | solution.py:509
  119.4 23.8 %collective-permute-start.5 = (bf16[512,768]{1,0:T(8,128)(2,1)}, bf16[512,768]{1,0:T(8,128)(2,1)S(1)}, u32[]{:S(2)}, u32[]{:S(2)}) collective-permute-start(bf16[512,768]{1,0:T(8,128)(2,1)} %get-tuple-element.142), channel_id=1, source_target_pairs={{0,1},{1,0},{2,3},{3,2},{4,5},{5,4},{6,7},{7,6},{8,9},{9,8},{10,11... | collective-permute-start | bytes 2359304 | tf_op jit(solution)/shard_map/ppermute | solution.py:492
  148.2 36.6 %collective-permute-start.6 = (bf16[64,24,384]{2,1,0:T(8,128)(2,1)}, bf16[64,24,384]{2,1,0:T(8,128)(2,1)S(1)}, u32[]{:S(2)}, u32[]{:S(2)}) collective-permute-start(bf16[64,24,384]{2,1,0:T(8,128)(2,1)} %get-tuple-element.157), channel_id=1, source_target_pairs={{0,4},{1,5},{2,6},{3,7},{4,0},{5,1},{6,2},{7,3},{8,12},{9,13},{10,... | collective-permute-start | bytes 3538952 | tf_op jit(solution)/shard_map/ppermute | solution.py:509
  150.2 34.7 %collective-permute-start.7 = (bf16[64,24,384]{2,1,0:T(8,128)(2,1)}, bf16[64,24,384]{2,1,0:T(8,128)(2,1)S(1)}, u32[]{:S(2)}, u32[]{:S(2)}) collective-permute-start(bf16[64,24,384]{2,1,0:T(8,128)(2,1)} %get-tuple-element.158), channel_id=1, source_target_pairs={{0,8},{1,9},{2,10},{3,11},{4,12},{5,13},{6,14},{7,15},{8,0},{9,1},... | collective-permute-start | bytes 3538952 | tf_op jit(solution)/shard_map/ppermute | solution.py:509
  152.4 32.5 %collective-permute-start.8 = (bf16[64,24,384]{2,1,0:T(8,128)(2,1)}, bf16[64,24,384]{2,1,0:T(8,128)(2,1)S(1)}, u32[]{:S(2)}, u32[]{:S(2)}) collective-permute-start(bf16[64,24,384]{2,1,0:T(8,128)(2,1)} %bitcast.121), channel_id=1, source_target_pairs={{0,2},{1,3},{2,0},{3,1},{4,6},{5,7},{6,4},{7,5},{8,10},{9,11},{10,... | collective-permute-start | bytes 3538952 | tf_op jit(solution)/shard_map/ppermute | solution.py:509
  190.2 17.1 %collective-permute-start.9 = (bf16[32,24,384]{2,1,0:T(8,128)(2,1)}, bf16[32,24,384]{2,1,0:T(8,128)(2,1)S(1)}, u32[]{:S(2)}, u32[]{:S(2)}) collective-permute-start(bf16[32,24,384]{2,1,0:T(8,128)(2,1)} %get-tuple-element.169), channel_id=1, source_target_pairs={{0,1},{1,0},{2,3},{3,2},{4,5},{5,4},{6,7},{7,6},{8,9},{9,8},{10,11... | collective-permute-start | bytes 1769480 | tf_op jit(solution)/shard_map/ppermute | solution.py:509
  191.8 16.1 %collective-permute-start.10 = (bf16[32,24,384]{2,1,0:T(8,128)(2,1)}, bf16[32,24,384]{2,1,0:T(8,128)(2,1)S(1)}, u32[]{:S(2)}, u32[]{:S(2)}) collective-permute-start(bf16[32,24,384]{2,1,0:T(8,128)(2,1)} %get-tuple-element.170), channel_id=1, source_target_pairs={{0,4},{1,5},{2,6},{3,7},{4,0},{5,1},{6,2},{7,3},{8,12},{9,13},{10,... | collective-permute-start | bytes 1769480 | tf_op jit(solution)/shard_map/ppermute | solution.py:509
  193.7 15.4 %collective-permute-start.11 = (bf16[32,24,384]{2,1,0:T(8,128)(2,1)}, bf16[32,24,384]{2,1,0:T(8,128)(2,1)S(1)}, u32[]{:S(2)}, u32[]{:S(2)}) collective-permute-start(bf16[32,24,384]{2,1,0:T(8,128)(2,1)} %get-tuple-element.171), channel_id=1, source_target_pairs={{0,8},{1,9},{2,10},{3,11},{4,12},{5,13},{6,14},{7,15},{8,0},{9,1},... | collective-permute-start | bytes 1769480 | tf_op jit(solution)/shard_map/ppermute | solution.py:509
  193.7 15.4 %collective-permute-start.12 = (bf16[48,24,384]{2,1,0:T(8,128)(2,1)}, bf16[48,24,384]{2,1,0:T(8,128)(2,1)S(1)}, u32[]{:S(2)}, u32[]{:S(2)}) collective-permute-start(bf16[48,24,384]{2,1,0:T(8,128)(2,1)} %bitcast.122), channel_id=1, source_target_pairs={{0,2},{1,3},{2,0},{3,1},{4,6},{5,7},{6,4},{7,5},{8,10},{9,11},{10,... | collective-permute-start | bytes 2654216 | tf_op jit(solution)/shard_map/ppermute | solution.py:509
  213.8 14.9 %collective-permute-start.14 = (bf16[32,24,384]{2,1,0:T(8,128)(2,1)}, bf16[32,24,384]{2,1,0:T(8,128)(2,1)S(1)}, u32[]{:S(2)}, u32[]{:S(2)}) collective-permute-start(bf16[32,24,384]{2,1,0:T(8,128)(2,1)} %get-tuple-element.185), channel_id=1, source_target_pairs={{0,1},{1,0},{2,3},{3,2},{4,5},{5,4},{6,7},{7,6},{8,9},{9,8},{10,11... | collective-permute-start | bytes 1769480 | tf_op jit(solution)/shard_map/ppermute | solution.py:509
  214.8 12.1 %collective-permute-start.15 = (bf16[24,24,384]{2,1,0:T(8,128)(2,1)}, bf16[24,24,384]{2,1,0:T(8,128)(2,1)S(1)}, u32[]{:S(2)}, u32[]{:S(2)}) collective-permute-start(bf16[24,24,384]{2,1,0:T(8,128)(2,1)} %get-tuple-element.186), channel_id=1, source_target_pairs={{0,4},{1,5},{2,6},{3,7},{4,0},{5,1},{6,2},{7,3},{8,12},{9,13},{10,... | collective-permute-start | bytes 1327112 | tf_op jit(solution)/shard_map/ppermute | solution.py:509
  214.8 9.0 %collective-permute-start.13 = (bf16[16,24,384]{2,1,0:T(8,128)(2,1)}, bf16[16,24,384]{2,1,0:T(8,128)(2,1)S(1)}, u32[]{:S(2)}, u32[]{:S(2)}) collective-permute-start(bf16[16,24,384]{2,1,0:T(8,128)(2,1)} %get-tuple-element.184), channel_id=1, source_target_pairs={{0,8},{1,9},{2,10},{3,11},{4,12},{5,13},{6,14},{7,15},{8,0},{9,1},... | collective-permute-start | bytes 884744 | tf_op jit(solution)/shard_map/ppermute | solution.py:509
  228.6 23.8 %collective-permute-start.21 = (bf16[512,768]{1,0:T(8,128)(2,1)}, bf16[512,768]{1,0:T(8,128)(2,1)S(1)}, u32[]{:S(2)}, u32[]{:S(2)}) collective-permute-start(bf16[512,768]{1,0:T(8,128)(2,1)} %after.2), channel_id=1, source_target_pairs={{0,1},{1,0},{2,3},{3,2},{4,5},{5,4},{6,7},{7,6},{8,9},{9,8},{10,11... | collective-permute-start | bytes 2359304 | tf_op jit(solution)/shard_map/ppermute | solution.py:492
  233.7 18.7 %collective-permute-start.18 = (bf16[12,24,384]{2,1,0:T(8,128)(2,1)}, bf16[12,24,384]{2,1,0:T(8,128)(2,1)S(1)}, u32[]{:S(2)}, u32[]{:S(2)}) collective-permute-start(bf16[12,24,384]{2,1,0:T(8,128)(2,1)} %get-tuple-element.207), channel_id=1, source_target_pairs={{0,4},{1,5},{2,6},{3,7},{4,0},{5,1},{6,2},{7,3},{8,12},{9,13},{10,... | collective-permute-start | bytes 663560 | tf_op jit(solution)/shard_map/ppermute | solution.py:509
  234.4 18.0 %collective-permute-start.17 = (bf16[16,24,384]{2,1,0:T(8,128)(2,1)}, bf16[16,24,384]{2,1,0:T(8,128)(2,1)S(1)}, u32[]{:S(2)}, u32[]{:S(2)}) collective-permute-start(bf16[16,24,384]{2,1,0:T(8,128)(2,1)} %get-tuple-element.206), channel_id=1, source_target_pairs={{0,16},{1,17},{2,18},{3,19},{4,20},{5,21},{6,22},{7,23},{8,24},{9,... | collective-permute-start | bytes 884744 | tf_op jit(solution)/shard_map/ppermute | solution.py:509
  236.5 15.9 %collective-permute-start.19 = (bf16[16,24,384]{2,1,0:T(8,128)(2,1)}, bf16[16,24,384]{2,1,0:T(8,128)(2,1)S(1)}, u32[]{:S(2)}, u32[]{:S(2)}) collective-permute-start(bf16[16,24,384]{2,1,0:T(8,128)(2,1)} %get-tuple-element.208), channel_id=1, source_target_pairs={{0,8},{1,9},{2,10},{3,11},{4,12},{5,13},{6,14},{7,15},{8,0},{9,1},... | collective-permute-start | bytes 884744 | tf_op jit(solution)/shard_map/ppermute | solution.py:509
  239.2 13.2 %collective-permute-start.20 = (bf16[4,24,384]{2,1,0:T(8,128)(2,1)S(1)}, bf16[4,24,384]{2,1,0:T(8,128)(2,1)S(1)}, u32[]{:S(2)}, u32[]{:S(2)}) collective-permute-start(bf16[4,24,384]{2,1,0:T(8,128)(2,1)S(1)} %copy-done.30), channel_id=1, source_target_pairs={{0,12},{1,13},{2,14},{3,15},{4,8},{5,9},{6,10},{7,11},{8,4},{9,5},... | collective-permute-start | bytes 221192 | tf_op jit(solution)/shard_map/ppermute | solution.py:509
  255.8 8.7 %collective-permute-start.23 = (bf16[4,24,384]{2,1,0:T(8,128)(2,1)}, bf16[4,24,384]{2,1,0:T(8,128)(2,1)S(1)}, u32[]{:S(2)}, u32[]{:S(2)}) collective-permute-start(bf16[4,24,384]{2,1,0:T(8,128)(2,1)} %get-tuple-element.222), channel_id=1, source_target_pairs={{0,1},{1,0},{2,3},{3,2},{4,5},{5,4},{6,7},{7,6},{8,9},{9,8},{10,11... | collective-permute-start | bytes 221192 | tf_op jit(solution)/shard_map/ppermute | solution.py:509
  256.9 9.0 %collective-permute-start.24 = (bf16[4,24,384]{2,1,0:T(8,128)(2,1)}, bf16[4,24,384]{2,1,0:T(8,128)(2,1)S(1)}, u32[]{:S(2)}, u32[]{:S(2)}) collective-permute-start(bf16[4,24,384]{2,1,0:T(8,128)(2,1)} %get-tuple-element.223), channel_id=1, source_target_pairs={{0,17},{1,16},{2,19},{3,18},{4,21},{5,20},{6,23},{7,22},{8,25},{9,... | collective-permute-start | bytes 221192 | tf_op jit(solution)/shard_map/ppermute | solution.py:509
  257.7 9.6 %collective-permute-start.22 = (bf16[8,24,384]{2,1,0:T(8,128)(2,1)}, bf16[8,24,384]{2,1,0:T(8,128)(2,1)S(1)}, u32[]{:S(2)}, u32[]{:S(2)}) collective-permute-start(bf16[8,24,384]{2,1,0:T(8,128)(2,1)} %get-tuple-element.221), channel_id=1, source_target_pairs={{0,16},{1,17},{2,18},{3,19},{4,20},{5,21},{6,22},{7,23},{8,24},{9,... | collective-permute-start | bytes 442376 | tf_op jit(solution)/shard_map/ppermute | solution.py:509
  (32 other events, 102.2 us)

commit v5 on v4

--- a/solution.py
+++ b/solution.py
@@ -90,14 +90,14 @@
             jax.ShapeDtypeStruct((length, width // 3), jnp.bfloat16),
             jax.ShapeDtypeStruct((groups * 2 * GROUP, length), jnp.float32),
         ],
-        compiler_params=pltpu.CompilerParams(vmem_limit_bytes=60 << 20),
+        compiler_params=pltpu.CompilerParams(vmem_limit_bytes=48 << 20),
         cost_estimate=pl.CostEstimate(flops=28 << 30, bytes_accessed=8 << 20, transcendentals=24 * length * length),
         name="attend",
     )(first, seg, proj, proj, proj)
 
 
-def attend_back_kernel(last, seg_ref, q_ref, k_ref, v_ref, up_ref, o_ref, lse_ref, low_t_ref, *refs, bk):
-    *riders, gq_ref, gk_ref, gv_ref, keep_ref, send_ref, bias, inner, key_t, value_t, q_t, up_t, gq_t, gk, gv = refs
+def attend_back_kernel(last, place, seg_ref, q_ref, k_ref, v_ref, up_ref, o_ref, lse_ref, low_t_ref, *refs, bk):
+    *riders, gq_ref, gk_ref, gv_ref, keep_ref, send_ref, bias, inner, key_t, value_t, q_t, up_t, gq_t, gk, gv, grad = refs
     g, j = pl.program_id(0), pl.program_id(1)
     length, lanes = q_ref.shape
     heads = lanes // HEAD_DIM
@@ -153,7 +153,8 @@
     def _():
         gq_ref[...] = jnp.transpose((gq_t[...] * SCALE).astype(gq_ref.dtype))
         joined = jnp.concatenate([gq_ref[...], gk_ref[...], gv_ref[...]], axis=1)
-        cut(mm(low_t_ref[...], joined), keep_ref, send_ref, g)
+        grad[...] = mm(low_t_ref[...], joined)
+        cut(place, grad, keep_ref, send_ref, g)
 
     if riders:
         @pl.when((g == 0) & (j == 0))
@@ -163,7 +164,7 @@
                 target[-extra:] = rider[...]
 
 
-def attend_back(begin, count, last, seg, proj, up, o, lse, low_t, shards, riders=(), bk=256):
+def attend_back(begin, count, last, place, seg, proj, up, o, lse, low_t, shards, riders=(), bk=256):
     length, width = proj.shape
     groups = width // 3 // SMALL
     half = width // 6
@@ -178,7 +179,7 @@
     all_of = lambda *size: pl.BlockSpec(size, lambda g, j, *_: (0,) * len(size), pipeline_mode=pl.Buffered(1))
     split = all_of(lead, *piece)
     grid_spec = pltpu.PrefetchScalarGridSpec(
-        num_scalar_prefetch=1,
+        num_scalar_prefetch=2,
         grid=(count, length // bk),
         in_specs=[
             fixed(1, length),
@@ -202,6 +203,7 @@
             pltpu.VMEM((SMALL, length), jnp.float32),
             pltpu.VMEM((bk, SMALL), jnp.float32),
             pltpu.VMEM((bk, SMALL), jnp.float32),
+            pltpu.VMEM((2 * half, PART), jnp.float32),
         ],
     )
     heads = jax.ShapeDtypeStruct((length, count * SMALL), jnp.bfloat16)
@@ -213,7 +215,7 @@
         compiler_params=pltpu.CompilerParams(vmem_limit_bytes=60 << 20),
         cost_estimate=pl.CostEstimate(flops=(count * 10) << 30, bytes_accessed=8 << 20, transcendentals=count * 4 * length * length),
         name="attend_back",
-    )(last, seg, proj, proj, proj, up, o, lse, low_t, *riders)
+    )(last, place, seg, proj, proj, proj, up, o, lse, low_t, *riders)
 
 
 def bounds(seg, bq, bk):
@@ -252,35 +254,23 @@
     return ((q >> 1) * 2 + core) * 2 + (q & 1)
 
 
-def arranged(place, rows, source, target, shards):
-    if rows % 8:
-        target[...] = source[...].astype(target.dtype)
-        return
-    chips = shards // 2
-    for at in range(0, shards, 2):
-        pair = [
-            source[pl.ds(pl.multiple_of(shard_at(place, b // chips, b % chips) * rows, 8), rows), :]
-            for b in (at, at + 1)
-        ]
-        target[at * rows:(at + 2) * rows, :] = jnp.concatenate(pair).astype(target.dtype)
-
-
-def cut(grad, keep, send, first):
+def cut(place, grad, keep, send, first):
     half = grad.shape[0] // 2
     for at in range(grad.shape[1] // PART):
-        block = grad[:, at * PART:(at + 1) * PART]
+        columns = slice(at * PART, (at + 1) * PART)
         if len(keep.shape) == 3:
-            keep[first + at] = block[:half].astype(keep.dtype)
-            send[first + at] = block[half:].astype(send.dtype)
+            keep[first + at] = grad[:half, columns].astype(keep.dtype)
+            send[first + at] = grad[half:, columns].astype(send.dtype)
         else:
             chips, rows = keep.shape[1:3]
-            for q in range(chips):
-                keep[first + at, q] = block[q * rows:(q + 1) * rows].astype(keep.dtype)
-                send[first + at, q] = block[half + q * rows:half + (q + 1) * rows].astype(send.dtype)
+            for rel, target in enumerate((keep, send)):
+                for q in range(chips):
+                    source = pl.ds(pl.multiple_of(shard_at(place, rel, q) * rows, 8), rows)
+                    target[first + at, q] = grad[source, columns].astype(target.dtype)
 
 
 def before_kernel(place, x_ref, gain_ref, w_ref, *refs, shards, block):
-    proj_ref, low_t_ref, low, flat = refs[-4:]
+    proj_ref, low_t_ref, low = refs[-3:]
     length, width = x_ref.shape
 
     @pl.when(pl.program_id(0) == 0)
@@ -289,10 +279,9 @@
             at = slice(at, at + block)
             values = x_ref[at, :].astype(jnp.float32)
             mean, rate = row_stats(values)
-            normed = (values - mean) * rate * gain_ref[...]
-            low[at, :] = normed.astype(jnp.bfloat16)
-            flat[:, at] = jnp.transpose(normed)
-        arranged(place, width // shards, flat, low_t_ref, shards)
+            normed = ((values - mean) * rate * gain_ref[...]).astype(jnp.bfloat16)
+            low[at, :] = normed
+            low_t_ref[:, at] = jnp.transpose(normed)
 
     proj_ref[...] = mm(low[...], w_ref[...]).astype(jnp.bfloat16)
 
@@ -310,7 +299,7 @@
             pl.BlockSpec((length, chunk), lambda c, place: (place[2], c)),
             pl.BlockSpec((width, length), lambda c, place: (0, place[2])),
         ],
-        scratch_shapes=[pltpu.VMEM((length, width), jnp.bfloat16), pltpu.VMEM((width, length), jnp.float32)],
+        scratch_shapes=[pltpu.VMEM((length, width), jnp.bfloat16)],
     )
     return pl.pallas_call(
         functools.partial(before_kernel, shards=shards, block=block),
@@ -328,7 +317,7 @@
 
 def middle_kernel(place, x_kept, x_other, o_ref, gy_kept, gy_other, w_out_ref, gain_ref, w_up_ref, w_down_ref,
                   out_kept, out_other, gx_ref, go_ref, keep_up, send_up, keep_down, send_down, keep_out, send_out,
-                  gy, x1, low, low_t, total, back, flat, part, *, shards, block):
+                  gy, x1, low, low_t, total, back, whole, part, *, shards, block):
     c = pl.program_id(0)
     length, width = o_ref.shape
     chunk = w_down_ref.shape[0]
@@ -348,12 +337,11 @@
             values = x1[at, :] + mm(o_ref[at, :], w_out_ref[...])
             x1[at, :] = values
             mean, rate = row_stats(values)
-            normed = (values - mean) * rate * gain_ref[...]
-            low[at, :] = normed.astype(jnp.bfloat16)
-            flat[:, at] = jnp.transpose(normed)
+            normed = ((values - mean) * rate * gain_ref[...]).astype(jnp.bfloat16)
+            low[at, :] = normed
+            low_t[:, at] = jnp.transpose(normed)
             total[at, :] = values
             back[at, :] = jnp.zeros_like(values)
-        arranged(place, rows, flat, low_t, shards)
 
     lifted, slopes = [], []
     for at in pieces:
@@ -364,7 +352,8 @@
         back[at, :] += mm(gu, w_up_ref[...], NT)
         lifted.append(jnp.transpose(a))
         slopes.append(gu)
-    cut(mm(low_t[...], jnp.concatenate(slopes, axis=0)), keep_up, send_up, 0)
+    whole[...] = mm(low_t[...], jnp.concatenate(slopes, axis=0))
+    cut(place, whole, keep_up, send_up, 0)
     grad_down = mm(jnp.concatenate(lifted, axis=1), gy[...])
     if rows % 8:
         for at in range(width // PART):
@@ -394,12 +383,12 @@
             gx_ref[at, :] = grad
             branch.append(grad)
             go_ref[at, :] = mm(grad, w_out_ref[...], NT).astype(jnp.bfloat16)
-            flat[:, at] = jnp.transpose(o_ref[at, :].astype(jnp.float32))
-        arranged(place, rows, flat, low_t, shards)
-        cut(mm(low_t[...], jnp.concatenate(branch, axis=0)), keep_out, send_out, 0)
-
-
-def middle(place, x, o, gy, w_out, gain, w_up, w_down, shards, block=256):
+            low_t[:, at] = jnp.transpose(o_ref[at, :])
+        whole[...] = mm(low_t[...], jnp.concatenate(branch, axis=0))
+        cut(place, whole, keep_out, send_out, 0)
+
+
+def middle(place, x, o, gy, w_out, gain, w_up, w_down, shards, block=512):
     length, width = o.shape
     lift = w_up.shape[1]
     steps = 4
@@ -440,7 +429,7 @@
             pltpu.VMEM((width, length), bf16),
             pltpu.VMEM((length, width), jnp.float32),
             pltpu.VMEM((length, width), jnp.float32),
-            pltpu.VMEM((width, length), jnp.float32),
+            pltpu.VMEM((width, width), jnp.float32),
             pltpu.VMEM((chunk, width), jnp.float32),
         ],
     )
@@ -742,7 +731,7 @@
     heads = []
 
     def heads_back(begin, count, plan, riders=()):
-        *grads, keep, send = attend_back(begin, count, last, seg, proj, go, mixture, lse, low_t, shards, riders)
+        *grads, keep, send = attend_back(begin, count, last, here, seg, proj, go, mixture, lse, low_t, shards, riders)
         heads.append(grads)
         return Flow(here, keep, send, chips, [core, *plan])
 
@@ -775,11 +764,11 @@
         ], [(rows, up.lead * PART), (4 * rows, width)], [(0, w_rows, gain_two_rows)])
 
     soon = not (up.plan or down.plan)
-    (kept_rows, rows_back, w_up_rows), moving = leave(flows, (kept_rows, rows_back, w_up_rows))
+    (kept_rows, rows_back, out_other, w_up_rows), moving = leave(flows, (kept_rows, rows_back, out_other, w_up_rows))
     ffn_grads = finish_ffn(w_up_rows) if soon else None
-    grad_tokens = joined(kept_rows, rows_back)
+    grad_tokens, outputs = joined(kept_rows, rows_back), joined(out_kept, out_other)
     while True:
-        ffn_grads, grad_tokens = arrive(moving, (ffn_grads, grad_tokens))
+        ffn_grads, grad_tokens, outputs = arrive(moving, (ffn_grads, grad_tokens, outputs))
         if not any(flow.plan for flow in flows):
             break
         _, moving = leave(flows)
@@ -792,7 +781,7 @@
         (three, of_group(three)),
     ], [(rows, 3 * width), (rows, width)], [(0, w_qkv_rows, gain_one_rows)])
     return (
-        joined(out_kept, out_other),
+        outputs,
         grad_tokens,
         grad_qkv,
         grad_out,

time: 275 us -> 270 us (0.982)
  Pallas kernels: 202 us -> 197 us
    unnamed x62 -> x66, local copies, waits for them, and re-layouts: 7.72 us -> 9.73 us
  transfers between devices with their start and end apart: 25 -> 25, of which waited for: 9 -> 6; matrix products, arithmetic and copies ran while one was open for 4% -> 4% of each run, Pallas kernels for 51% -> 50%
where the time goes in v5:
time: 270 us; the launch traced here: 268 us
  Pallas kernels  197 us (73%)
  starting transfers between devices  29.1 us (11%)
  waiting for transfers between devices  17.8 us (7%)
  local copies, waits for them, and re-layouts  15.2 us (6%)
  other arithmetic  7.42 us (3%)
    pallas_call x3, Pallas kernels, attend_back(): pl.pallas_call(functools.partial(attend_back_kernel, bk=bk), grid_spec=gr...  69.2 us
    pallas_call x1, Pallas kernels, middle(): pl.pallas_call(functools.partial(middle_kernel, shards=shards, block=bloc...  47.3 us
    pallas_call x1, Pallas kernels, attend(): pl.pallas_call(functools.partial(attend_kernel, bq=bq, unroll=unroll), gr...  30.6 us
    ppermute x20, starting transfers between devices, crossed(): lax.ppermute(block, ('dp', 'seq'), [(i, i ^ step) for i in range(count)])  23.4 us
    pallas_call x5, Pallas kernels, combine(): pl.pallas_call(functools.partial(combine_kernel, work=work, steps=steps),...  16.2 us
    pallas_call x2, Pallas kernels, after(): pl.pallas_call(after_kernel, grid_spec=grid_spec, out_shape=jax.ShapeDtyp...  14.3 us
    pallas_call x2, Pallas kernels, before(): pl.pallas_call(functools.partial(before_kernel, shards=shards, block=bloc...  13.9 us
    ppermute x20, waiting for transfers between devices, crossed(): lax.ppermute(block, ('dp', 'seq'), [(i, i ^ step) for i in range(count)])  13.6 us
  transfers between devices with their start and end apart: 25, of which 6 were waited for; matrix products, arithmetic and copies ran while one was open for 4% of the time, Pallas kernels for 50%

profile of v5, /device:TPU:0, one launch (start us, length us, event | category | flops | bytes accessed | tf_op | source)
XLA Modules:
  0.0 267.6 jit_solution(17380512334032067668)
XLA Ops:
  3.2 3.0 %collective-permute-start.1 = (s32[512]{0:T(512)S(1)}, s32[512]{0:T(512)S(1)}, u32[]{:S(2)}, u32[]{:S(2)}) collective-permute-start(s32[512]{0:T(512)S(1)} %bitcast.118), channel_id=1, source_target_pairs={{0,1},{1,0},{2,3},{3,2},{4,5},{5,4},{6,7},{7,6},{8,9},{9,8},{10,11... | collective-permute-start | bytes 6152 | tf_op jit(solution)/shard_map/ppermute | solution.py:481
  13.7 7.0 %before.2 = (bf16[1024,2304]{1,0:T(8,128)(2,1)}, bf16[768,1024]{1,0:T(8,128)(2,1)}) custom-call(s32[3]{0:T(128)} %get-tuple-element.256.place, bf16[512,768]{1,0:T(8,128)(2,1)} %get-tuple-element.253.x_ref.x_kept, f32[1,768]{1,0:T(1,128)} %broadcast_in_dim.17.gain_ref, bf16[768,2304]{1,0:T(8,128)(2,1)} %w_ref.7), custom_call_target="tpu_custom_call" | custom-call | flops 1811939328 | bytes 12582912 | tf_op jit(solution)/shard_map/before/pallas_call | solution.py:304
  22.4 4.2 %collective-permute-done.x_ref.x_other = bf16[512,768]{1,0:T(8,128)(2,1)S(1)} collective-permute-done((bf16[512,768]{1,0:T(8,128)(2,1)S(1)}, bf16[512,768]{1,0:T(8,128)(2,1)S(1)}, u32[]{:S(2)}, u32[]{:S(2)}) %collective-permute-start) | collective-permute-done | bytes 786464 | tf_op jit(solution)/shard_map/ppermute | solution.py:481
  27.6 6.9 %before.3 = (bf16[1024,2304]{1,0:T(8,128)(2,1)}, bf16[768,1024]{1,0:T(8,128)(2,1)}) custom-call(s32[3]{0:T(128)} %get-tuple-element.257.place, bf16[512,768]{1,0:T(8,128)(2,1)} %copy-done.13, f32[1,768]{1,0:T(1,128)} %broadcast_in_dim.17.gain_ref, bf16[768,2304]{1,0:T(8,128)(2,1)} %w_ref.7, ...), custom_call_target="tpu_custom_call", output_to_operand_aliasing={{0}: (4, {}), {1}: (5, {})} | custom-call | flops 1811939328 | bytes 12582912 | tf_op jit(solution)/shard_map/before/pallas_call | solution.py:304
  34.4 30.6 %attend.1 = (bf16[1024,768]{1,0:T(8,128)(2,1)S(1)}, f32[48,1024]{1,0:T(8,128)S(1)}) custom-call(s32[4]{0:T(128)S(1)} %and_select_fusion.1.first, s32[1,1024]{1,0:T(1,128)S(1)} %broadcast_select_fusion.seg_ref, bf16[1024,2304]{1,0:T(8,128)(2,1)} %get-tuple-element.133.q_ref.k_ref.v_ref, bf16[1024,2304]{1,0:T(8,128)(2,1)} %get-tuple-element.133.q_ref.k_ref.v_ref, ...), custom_call_target="tpu_custom_call" | custom-call | flops 30064771072 | bytes 8388608 | tf_op jit(solution)/shard_map/attend/pallas_call | solution.py:86
  67.7 47.3 %middle.1 = (bf16[512,768]{1,0:T(8,128)(2,1)}, bf16[512,768]{1,0:T(8,128)(2,1)}, bf16[1024,768]{1,0:T(8,128)(2,1)}, bf16[1024,768]{1,0:T(8,128)(2,1)}, bf16[8,16...) custom-call(s32[3]{0:T(128)} %get-tuple-element.256.place, ...), custom_call_target="tpu_custom_call" | custom-call | flops 28991029248 | bytes 41943040 | tf_op jit(solution)/shard_map/middle/pallas_call | solution.py:436
  116.1 24.1 %attend_back.3 = (bf16[1024,256]{1,0:T(8,128)(2,1)}, bf16[1024,256]{1,0:T(8,128)(2,1)}, bf16[1024,256]{1,0:T(8,128)(2,1)}, bf16[4,16,24,384]{3,2,1,0:T(8,128)(2,1)}, bf16[4,16,24,384]{3,2,1,0:T(8,128)(2,1)}) custom-call(s32[4]{0:T(128)} %and_select_fusion.last, s32[3]{0:T(128)} %get-tuple-element.256.place, s32[1,1024]{1,0:T(1,128)} %copy-done, ...), custom_call_target="tpu_custom_call" | custom-call | flops 21474836480 | bytes 8388608 | tf_op jit(solution)/shard_map/attend_back/pallas_call | solution.py:211
  141.8 3.5 %combine.5 = (bf16[64,24,384]{2,1,0:T(8,128)(2,1)}, bf16[64,24,384]{2,1,0:T(8,128)(2,1)}) custom-call(bf16[8,2,2,2,2,24,384]{6,5,4,3,2,1,0:T(8,128)(2,1)} %bitcast.48, bf16[8,2,2,2,2,24,384]{6,5,4,3,2,1,0:T(8,128)(2,1)} %bitcast.58, bf16[8,2,2,2,2,24,384]{6,5,4,3,2,1,0:T(8,128)(2,1)} %bitcast.53, ...), custom_call_target="tpu_custom_call" | custom-call | flops 1048576 | bytes 8388608 | tf_op jit(solution)/shard_map/combine/pallas_call | solution.py:618
  148.8 32.2 %attend_back.4 = (bf16[1024,384]{1,0:T(8,128)(2,1)}, bf16[1024,384]{1,0:T(8,128)(2,1)}, bf16[1024,384]{1,0:T(8,128)(2,1)}, bf16[3,16,24,384]{3,2,1,0:T(8,128)(2,1)}, bf16[3,16,24,384]{3,2,1,0:T(8,128)(2,1)}) custom-call(s32[4]{0:T(128)} %and_select_fusion.last, s32[3]{0:T(128)} %get-tuple-element.256.place, s32[1,1024]{1,0:T(1,128)} %copy-done, ...), custom_call_target="tpu_custom_call" | custom-call | flops 32212254720 | bytes 8388608 | tf_op jit(solution)/shard_map/attend_back/pallas_call | solution.py:211
  182.8 3.5 %combine.6 = (bf16[32,24,384]{2,1,0:T(8,128)(2,1)}, bf16[32,24,384]{2,1,0:T(8,128)(2,1)}, bf16[32,24,384]{2,1,0:T(8,128)(2,1)}) custom-call(bf16[8,2,2,2,2,24,384]{6,5,4,3,2,1,0:T(8,128)(2,1)} %bitcast.49, bf16[8,2,2,2,2,24,384]{6,5,4,3,2,1,0:T(8,128)(2,1)} %bitcast.59, bf16[8,2,2,2,24,384]{5,4,3,2,1,0:T(8,128)(2,1)} %bitcast.73, ...), custom_call_target="tpu_custom_call" | custom-call | flops 1048576 | bytes 8388608 | tf_op jit(solution)/shard_map/combine/pallas_call | solution.py:618
  186.3 3.4 %collective-permute-start.9 = (bf16[32,24,384]{2,1,0:T(8,128)(2,1)}, bf16[32,24,384]{2,1,0:T(8,128)(2,1)S(1)}, u32[]{:S(2)}, u32[]{:S(2)}) collective-permute-start(bf16[32,24,384]{2,1,0:T(8,128)(2,1)} %get-tuple-element.169), channel_id=1, source_target_pairs={{0,1},{1,0},{2,3},{3,2},{4,5},{5,4},{6,7},{7,6},{8,9},{9,8},{10,11... | collective-permute-start | bytes 1769480 | tf_op jit(solution)/shard_map/ppermute | solution.py:498
  189.8 2.9 %collective-permute-start.11 = (bf16[32,24,384]{2,1,0:T(8,128)(2,1)}, bf16[32,24,384]{2,1,0:T(8,128)(2,1)S(1)}, u32[]{:S(2)}, u32[]{:S(2)}) collective-permute-start(bf16[32,24,384]{2,1,0:T(8,128)(2,1)} %get-tuple-element.171), channel_id=1, source_target_pairs={{0,8},{1,9},{2,10},{3,11},{4,12},{5,13},{6,14},{7,15},{8,0},{9,1},... | collective-permute-start | bytes 1769480 | tf_op jit(solution)/shard_map/ppermute | solution.py:498
  192.8 12.9 %attend_back.5 = (bf16[1024,128]{1,0:T(8,128)(2,1)}, bf16[1024,128]{1,0:T(8,128)(2,1)}, bf16[1024,128]{1,0:T(8,128)(2,1)}, bf16[1,16,24,384]{3,2,1,0:T(8,128)(2,1)}, bf16[1,16,24,384]{3,2,1,0:T(8,128)(2,1)}) custom-call(s32[4]{0:T(128)} %and_select_fusion.last, s32[3]{0:T(128)} %get-tuple-element.256.place, s32[1,1024]{1,0:T(1,128)} %copy-done, ...), custom_call_target="tpu_custom_call" | custom-call | flops 10737418240 | bytes 8388608 | tf_op jit(solution)/shard_map/attend_back/pallas_call | solution.py:211
  207.2 3.5 %combine.7 = (bf16[16,24,384]{2,1,0:T(8,128)(2,1)}, bf16[32,24,384]{2,1,0:T(8,128)(2,1)}, bf16[24,24,384]{2,1,0:T(8,128)(2,1)}) custom-call(bf16[8,2,2,2,2,24,384]{6,5,4,3,2,1,0:T(8,128)(2,1)} %bitcast.50, bf16[8,2,2,2,2,24,384]{6,5,4,3,2,1,0:T(8,128)(2,1)} %bitcast.60, bf16[8,2,2,2,24,384]{5,4,3,2,1,0:T(8,128)(2,1)} %bitcast.74, ...), custom_call_target="tpu_custom_call" | custom-call | flops 1048576 | bytes 8388608 | tf_op jit(solution)/shard_map/combine/pallas_call | solution.py:618
  212.7 2.7 collective-permute-start.13
  215.4 7.1 %after.2 = bf16[512,768]{1,0:T(8,128)(2,1)} custom-call(s32[3]{0:T(128)} %get-tuple-element.257.place, bf16[512,768]{1,0:T(8,128)(2,1)} %copy-done.13, f32[1,768]{1,0:T(1,128)} %broadcast_in_dim.17.gain_ref, bf16[1024,768]{1,0:T(8,128)(2,1)} %get-tuple-element.210.gx_ref, bf16[768,2304]{1,0:T(8,128)(2,1)} %w_ref.7, ...), custom_call_target="tpu_custom_call" | custom-call | flops 1811939328 | bytes 16777216 | tf_op jit(solution)/shard_map/after/pallas_call | solution.py:470
  224.1 2.9 %collective-permute-done.14.refs_9_.refs_3_.refs_10_ = bf16[32,24,384]{2,1,0:T(8,128)(2,1)S(1)} collective-permute-done((bf16[32,24,384]{2,1,0:T(8,128)(2,1)}, bf16[32,24,384]{2,1,0:T(8,128)(2,1)S(1)}, u32[]{:S(2)}, u32[]{:S(2)}) %collective-permute-start.14) | collective-permute-done | bytes 589856 | tf_op jit(solution)/shard_map/ppermute | solution.py:498
  227.9 3.2 %combine.8 = (bf16[16,24,384]{2,1,0:T(8,128)(2,1)}, bf16[12,24,384]{2,1,0:T(8,128)(2,1)}, bf16[16,24,384]{2,1,0:T(8,128)(2,1)}, bf16[4,24,384]{2,1,0:T(8,128)(2,1)}) custom-call(bf16[8,2,2,2,2,24,384]{6,5,4,3,2,1,0:T(8,128)(2,1)} %bitcast.51, bf16[8,2,2,2,2,24,384]{6,5,4,3,2,1,0:T(8,128)(2,1)} %bitcast.61, bf16[8,2,2,2,24,384]{5,4,3,2,1,0:T(8,128)(2,1)} %bitcast.75, ...), custom_call_target="tpu_custom_call" | custom-call | flops 1048576 | bytes 8388608 | tf_op jit(solution)/shard_map/combine/pallas_call | solution.py:618
  234.9 7.2 %after.3 = bf16[512,768]{1,0:T(8,128)(2,1)} custom-call(s32[3]{0:T(128)} %get-tuple-element.256.place, bf16[512,768]{1,0:T(8,128)(2,1)} %get-tuple-element.253.x_ref.x_kept, f32[1,768]{1,0:T(1,128)} %broadcast_in_dim.17.gain_ref, bf16[1024,768]{1,0:T(8,128)(2,1)} %get-tuple-element.210.gx_ref, bf16[768,2304]{1,0:T(8,128)(2,1)} %w_ref.7, ...), custom_call_target="tpu_custom_call" | custom-call | flops 1811939328 | bytes 16777216 | tf_op jit(solution)/shard_map/after/pallas_call | solution.py:470
  242.1 6.1 %collective-permute-done.20 = bf16[4,24,384]{2,1,0:T(8,128)(2,1)S(1)} collective-permute-done((bf16[4,24,384]{2,1,0:T(8,128)(2,1)}, bf16[4,24,384]{2,1,0:T(8,128)(2,1)S(1)}, u32[]{:S(2)}, u32[]{:S(2)}) %collective-permute-start.20) | collective-permute-done | bytes 73760 | tf_op jit(solution)/shard_map/ppermute | solution.py:498
  249.0 2.5 combine.9
  252.5 2.7 collective-permute-start.24
  258.7 2.9 %finish.2 = (f32[24,3072]{1,0:T(8,128)}, f32[96,768]{1,0:T(8,128)}, f32[1,24]{1,0:T(1,128)}) custom-call(bf16[8,2,2,2,2,24,384]{6,5,4,3,2,1,0:T(8,128)(2,1)} %bitcast.52, bf16[8,2,2,2,2,24,384]{6,5,4,3,2,1,0:T(8,128)(2,1)} %bitcast.62, bf16[8,2,2,2,24,384]{5,4,3,2,1,0:T(8,128)(2,1)} %bitcast.76, bf16[8,2,2,24,384]{4,3,2,1,0:T(8,128)(2,1)} %bitcast.95, ...), custom_call_target="tpu_custom_call" | custom-call | flops 1048576 | bytes 4194304 | tf_op jit(solution)/shard_map/finish/pallas_call | solution.py:688
  261.7 2.5 collective-permute-done.22.refs_5_
  (126 shorter events, 41.5 us)
Async XLA Ops:
  3.2 18.8 %collective-permute-start.1 = (s32[512]{0:T(512)S(1)}, s32[512]{0:T(512)S(1)}, u32[]{:S(2)}, u32[]{:S(2)}) collective-permute-start(s32[512]{0:T(512)S(1)} %bitcast.118), channel_id=1, source_target_pairs={{0,1},{1,0},{2,3},{3,2},{4,5},{5,4},{6,7},{7,6},{8,9},{9,8},{10,11... | collective-permute-start | bytes 6152 | tf_op jit(solution)/shard_map/ppermute | solution.py:481
  6.2 20.5 %collective-permute-start = (bf16[512,768]{1,0:T(8,128)(2,1)S(1)}, bf16[512,768]{1,0:T(8,128)(2,1)S(1)}, u32[]{:S(2)}, u32[]{:S(2)}) collective-permute-start(bf16[512,768]{1,0:T(8,128)(2,1)S(1)} %get-tuple-element.128), channel_id=1, source_target_pairs={{0,1},{1,0},{2,3},{3,2},{4,5},{5,4},{6,7},{7,6},{8,9},{9,8},{10,11... | collective-permute-start | bytes 2359304 | tf_op jit(solution)/shard_map/ppermute | solution.py:481
  7.3 59.5 %collective-permute-start.2 = (bf16[512,768]{1,0:T(8,128)(2,1)S(1)}, bf16[512,768]{1,0:T(8,128)(2,1)S(1)}, u32[]{:S(2)}, u32[]{:S(2)}) collective-permute-start(bf16[512,768]{1,0:T(8,128)(2,1)S(1)} %get-tuple-element.250), channel_id=1, source_target_pairs={{0,1},{1,0},{2,3},{3,2},{4,5},{5,4},{6,7},{7,6},{8,9},{9,8},{10,11... | collective-permute-start | bytes 2359304 | tf_op jit(solution)/shard_map/ppermute | solution.py:481
  115.0 25.3 %collective-permute-start.3 = (bf16[128,24,384]{2,1,0:T(8,128)(2,1)}, bf16[128,24,384]{2,1,0:T(8,128)(2,1)S(1)}, u32[]{:S(2)}, u32[]{:S(2)}) collective-permute-start(bf16[128,24,384]{2,1,0:T(8,128)(2,1)} %bitcast.120), channel_id=1, source_target_pairs={{0,2},{1,3},{2,0},{3,1},{4,6},{5,7},{6,4},{7,5},{8,10},{9,11},{10,... | collective-permute-start | bytes 7077896 | tf_op jit(solution)/shard_map/ppermute | solution.py:498
  115.1 25.3 %collective-permute-start.4 = (bf16[128,24,384]{2,1,0:T(8,128)(2,1)}, bf16[128,24,384]{2,1,0:T(8,128)(2,1)}, u32[]{:S(2)}, u32[]{:S(2)}) collective-permute-start(bf16[128,24,384]{2,1,0:T(8,128)(2,1)} %bitcast.119), channel_id=1, source_target_pairs={{0,2},{1,3},{2,0},{3,1},{4,6},{5,7},{6,4},{7,5},{8,10},{9,11},{10,... | collective-permute-start | bytes 7077896 | tf_op jit(solution)/shard_map/ppermute | solution.py:498
  116.1 24.2 %collective-permute-start.5 = (bf16[512,768]{1,0:T(8,128)(2,1)}, bf16[512,768]{1,0:T(8,128)(2,1)S(1)}, u32[]{:S(2)}, u32[]{:S(2)}) collective-permute-start(bf16[512,768]{1,0:T(8,128)(2,1)} %get-tuple-element.144), channel_id=1, source_target_pairs={{0,1},{1,0},{2,3},{3,2},{4,5},{5,4},{6,7},{7,6},{8,9},{9,8},{10,11... | collective-permute-start | bytes 2359304 | tf_op jit(solution)/shard_map/ppermute | solution.py:481
  145.2 35.8 %collective-permute-start.6 = (bf16[64,24,384]{2,1,0:T(8,128)(2,1)}, bf16[64,24,384]{2,1,0:T(8,128)(2,1)S(1)}, u32[]{:S(2)}, u32[]{:S(2)}) collective-permute-start(bf16[64,24,384]{2,1,0:T(8,128)(2,1)} %get-tuple-element.157), channel_id=1, source_target_pairs={{0,4},{1,5},{2,6},{3,7},{4,0},{5,1},{6,2},{7,3},{8,12},{9,13},{10,... | collective-permute-start | bytes 3538952 | tf_op jit(solution)/shard_map/ppermute | solution.py:498
  147.2 33.8 %collective-permute-start.7 = (bf16[64,24,384]{2,1,0:T(8,128)(2,1)}, bf16[64,24,384]{2,1,0:T(8,128)(2,1)S(1)}, u32[]{:S(2)}, u32[]{:S(2)}) collective-permute-start(bf16[64,24,384]{2,1,0:T(8,128)(2,1)} %get-tuple-element.158), channel_id=1, source_target_pairs={{0,8},{1,9},{2,10},{3,11},{4,12},{5,13},{6,14},{7,15},{8,0},{9,1},... | collective-permute-start | bytes 3538952 | tf_op jit(solution)/shard_map/ppermute | solution.py:498
  148.8 32.3 %collective-permute-start.8 = (bf16[64,24,384]{2,1,0:T(8,128)(2,1)}, bf16[64,24,384]{2,1,0:T(8,128)(2,1)S(1)}, u32[]{:S(2)}, u32[]{:S(2)}) collective-permute-start(bf16[64,24,384]{2,1,0:T(8,128)(2,1)} %bitcast.121), channel_id=1, source_target_pairs={{0,2},{1,3},{2,0},{3,1},{4,6},{5,7},{6,4},{7,5},{8,10},{9,11},{10,... | collective-permute-start | bytes 3538952 | tf_op jit(solution)/shard_map/ppermute | solution.py:498
  186.3 19.3 %collective-permute-start.9 = (bf16[32,24,384]{2,1,0:T(8,128)(2,1)}, bf16[32,24,384]{2,1,0:T(8,128)(2,1)S(1)}, u32[]{:S(2)}, u32[]{:S(2)}) collective-permute-start(bf16[32,24,384]{2,1,0:T(8,128)(2,1)} %get-tuple-element.169), channel_id=1, source_target_pairs={{0,1},{1,0},{2,3},{3,2},{4,5},{5,4},{6,7},{7,6},{8,9},{9,8},{10,11... | collective-permute-start | bytes 1769480 | tf_op jit(solution)/shard_map/ppermute | solution.py:498
  189.7 15.9 %collective-permute-start.10 = (bf16[32,24,384]{2,1,0:T(8,128)(2,1)}, bf16[32,24,384]{2,1,0:T(8,128)(2,1)S(1)}, u32[]{:S(2)}, u32[]{:S(2)}) collective-permute-start(bf16[32,24,384]{2,1,0:T(8,128)(2,1)} %get-tuple-element.170), channel_id=1, source_target_pairs={{0,4},{1,5},{2,6},{3,7},{4,0},{5,1},{6,2},{7,3},{8,12},{9,13},{10,... | collective-permute-start | bytes 1769480 | tf_op jit(solution)/shard_map/ppermute | solution.py:498
  189.8 16.3 %collective-permute-start.11 = (bf16[32,24,384]{2,1,0:T(8,128)(2,1)}, bf16[32,24,384]{2,1,0:T(8,128)(2,1)S(1)}, u32[]{:S(2)}, u32[]{:S(2)}) collective-permute-start(bf16[32,24,384]{2,1,0:T(8,128)(2,1)} %get-tuple-element.171), channel_id=1, source_target_pairs={{0,8},{1,9},{2,10},{3,11},{4,12},{5,13},{6,14},{7,15},{8,0},{9,1},... | collective-permute-start | bytes 1769480 | tf_op jit(solution)/shard_map/ppermute | solution.py:498
  192.7 13.4 %collective-permute-start.12 = (bf16[48,24,384]{2,1,0:T(8,128)(2,1)}, bf16[48,24,384]{2,1,0:T(8,128)(2,1)S(1)}, u32[]{:S(2)}, u32[]{:S(2)}) collective-permute-start(bf16[48,24,384]{2,1,0:T(8,128)(2,1)} %bitcast.122), channel_id=1, source_target_pairs={{0,2},{1,3},{2,0},{3,1},{4,6},{5,7},{6,4},{7,5},{8,10},{9,11},{10,... | collective-permute-start | bytes 2654216 | tf_op jit(solution)/shard_map/ppermute | solution.py:498
  210.7 16.3 %collective-permute-start.14 = (bf16[32,24,384]{2,1,0:T(8,128)(2,1)}, bf16[32,24,384]{2,1,0:T(8,128)(2,1)S(1)}, u32[]{:S(2)}, u32[]{:S(2)}) collective-permute-start(bf16[32,24,384]{2,1,0:T(8,128)(2,1)} %get-tuple-element.185), channel_id=1, source_target_pairs={{0,1},{1,0},{2,3},{3,2},{4,5},{5,4},{6,7},{7,6},{8,9},{9,8},{10,11... | collective-permute-start | bytes 1769480 | tf_op jit(solution)/shard_map/ppermute | solution.py:498
  211.2 12.9 %collective-permute-start.15 = (bf16[24,24,384]{2,1,0:T(8,128)(2,1)}, bf16[24,24,384]{2,1,0:T(8,128)(2,1)S(1)}, u32[]{:S(2)}, u32[]{:S(2)}) collective-permute-start(bf16[24,24,384]{2,1,0:T(8,128)(2,1)} %get-tuple-element.186), channel_id=1, source_target_pairs={{0,4},{1,5},{2,6},{3,7},{4,0},{5,1},{6,2},{7,3},{8,12},{9,13},{10,... | collective-permute-start | bytes 1327112 | tf_op jit(solution)/shard_map/ppermute | solution.py:498
  212.7 9.8 %collective-permute-start.13 = (bf16[16,24,384]{2,1,0:T(8,128)(2,1)}, bf16[16,24,384]{2,1,0:T(8,128)(2,1)S(1)}, u32[]{:S(2)}, u32[]{:S(2)}) collective-permute-start(bf16[16,24,384]{2,1,0:T(8,128)(2,1)} %get-tuple-element.184), channel_id=1, source_target_pairs={{0,8},{1,9},{2,10},{3,11},{4,12},{5,13},{6,14},{7,15},{8,0},{9,1},... | collective-permute-start | bytes 884744 | tf_op jit(solution)/shard_map/ppermute | solution.py:498
  227.0 21.2 %collective-permute-start.21 = (bf16[512,768]{1,0:T(8,128)(2,1)}, bf16[512,768]{1,0:T(8,128)(2,1)S(1)}, u32[]{:S(2)}, u32[]{:S(2)}) collective-permute-start(bf16[512,768]{1,0:T(8,128)(2,1)} %after.2), channel_id=1, source_target_pairs={{0,1},{1,0},{2,3},{3,2},{4,5},{5,4},{6,7},{7,6},{8,9},{9,8},{10,11... | collective-permute-start | bytes 2359304 | tf_op jit(solution)/shard_map/ppermute | solution.py:481
  231.1 17.1 %collective-permute-start.17 = (bf16[16,24,384]{2,1,0:T(8,128)(2,1)}, bf16[16,24,384]{2,1,0:T(8,128)(2,1)S(1)}, u32[]{:S(2)}, u32[]{:S(2)}) collective-permute-start(bf16[16,24,384]{2,1,0:T(8,128)(2,1)} %get-tuple-element.206), channel_id=1, source_target_pairs={{0,16},{1,17},{2,18},{3,19},{4,20},{5,21},{6,22},{7,23},{8,24},{9,... | collective-permute-start | bytes 884744 | tf_op jit(solution)/shard_map/ppermute | solution.py:498
  231.4 16.8 %collective-permute-start.19 = (bf16[16,24,384]{2,1,0:T(8,128)(2,1)}, bf16[16,24,384]{2,1,0:T(8,128)(2,1)S(1)}, u32[]{:S(2)}, u32[]{:S(2)}) collective-permute-start(bf16[16,24,384]{2,1,0:T(8,128)(2,1)} %get-tuple-element.208), channel_id=1, source_target_pairs={{0,8},{1,9},{2,10},{3,11},{4,12},{5,13},{6,14},{7,15},{8,0},{9,1},... | collective-permute-start | bytes 884744 | tf_op jit(solution)/shard_map/ppermute | solution.py:498
  232.6 15.6 %collective-permute-start.18 = (bf16[12,24,384]{2,1,0:T(8,128)(2,1)}, bf16[12,24,384]{2,1,0:T(8,128)(2,1)S(1)}, u32[]{:S(2)}, u32[]{:S(2)}) collective-permute-start(bf16[12,24,384]{2,1,0:T(8,128)(2,1)} %get-tuple-element.207), channel_id=1, source_target_pairs={{0,4},{1,5},{2,6},{3,7},{4,0},{5,1},{6,2},{7,3},{8,12},{9,13},{10,... | collective-permute-start | bytes 663560 | tf_op jit(solution)/shard_map/ppermute | solution.py:498
  233.8 14.4 %collective-permute-start.20 = (bf16[4,24,384]{2,1,0:T(8,128)(2,1)}, bf16[4,24,384]{2,1,0:T(8,128)(2,1)S(1)}, u32[]{:S(2)}, u32[]{:S(2)}) collective-permute-start(bf16[4,24,384]{2,1,0:T(8,128)(2,1)} %get-tuple-element.209), channel_id=1, source_target_pairs={{0,12},{1,13},{2,14},{3,15},{4,8},{5,9},{6,10},{7,11},{8,4},{9,5},... | collective-permute-start | bytes 221192 | tf_op jit(solution)/shard_map/ppermute | solution.py:498
  251.6 10.1 %collective-permute-start.23 = (bf16[4,24,384]{2,1,0:T(8,128)(2,1)}, bf16[4,24,384]{2,1,0:T(8,128)(2,1)S(1)}, u32[]{:S(2)}, u32[]{:S(2)}) collective-permute-start(bf16[4,24,384]{2,1,0:T(8,128)(2,1)} %get-tuple-element.223), channel_id=1, source_target_pairs={{0,1},{1,0},{2,3},{3,2},{4,5},{5,4},{6,7},{7,6},{8,9},{9,8},{10,11... | collective-permute-start | bytes 221192 | tf_op jit(solution)/shard_map/ppermute | solution.py:498
  252.5 9.2 %collective-permute-start.24 = (bf16[4,24,384]{2,1,0:T(8,128)(2,1)}, bf16[4,24,384]{2,1,0:T(8,128)(2,1)S(1)}, u32[]{:S(2)}, u32[]{:S(2)}) collective-permute-start(bf16[4,24,384]{2,1,0:T(8,128)(2,1)} %get-tuple-element.224), channel_id=1, source_target_pairs={{0,17},{1,16},{2,19},{3,18},{4,21},{5,20},{6,23},{7,22},{8,25},{9,... | collective-permute-start | bytes 221192 | tf_op jit(solution)/shard_map/ppermute | solution.py:498
  255.1 9.1 %collective-permute-start.22 = (bf16[8,24,384]{2,1,0:T(8,128)(2,1)}, bf16[8,24,384]{2,1,0:T(8,128)(2,1)S(1)}, u32[]{:S(2)}, u32[]{:S(2)}) collective-permute-start(bf16[8,24,384]{2,1,0:T(8,128)(2,1)} %get-tuple-element.222), channel_id=1, source_target_pairs={{0,16},{1,17},{2,18},{3,19},{4,20},{5,21},{6,22},{7,23},{8,24},{9,... | collective-permute-start | bytes 442376 | tf_op jit(solution)/shard_map/ppermute | solution.py:498
  (34 other events, 113.6 us)

commit v6 on v5

--- a/solution.py
+++ b/solution.py
@@ -727,7 +727,7 @@
 
     core, near = (-1,), [(bit,) for bit in far]
     up = Flow(here, keep_up, send_up, chips, [core, (1,), (0,), *near])
-    down = Flow(here, keep_down, send_down, chips, [core, *near[:1], (1,), (0,), *near[1:]], 4)
+    down = Flow(here, keep_down, send_down, chips, [core, *near[:1], (1,), *near[1:2], (), (0,), *near[2:]], 4)
     heads = []
 
     def heads_back(begin, count, plan, riders=()):
@@ -753,33 +753,32 @@
     rows_back = swapped(other_rows)
     gx, moving = leave(flows, gx)
     kept_rows = after(here, x_kept, gain_one, gx, w_qkv, pieces)
-    kept_rows, rows_back = arrive(moving, (kept_rows, rows_back))
+    kept_rows = arrive(moving, kept_rows)
     rows, width = up.rows, w_out.shape[1]
     w_qkv_rows, gain_one_rows, w_up_rows, gain_two_rows = weights
 
-    def finish_ffn(w_rows):
-        return finish([
-            (up, [(0, 0, lead * PART, PART, 1) for lead in range(up.lead)]),
-            (down, [(1, (lead % 4) * rows, (lead // 4) * PART, PART, 1) for lead in range(down.lead)]),
-        ], [(rows, up.lead * PART), (4 * rows, width)], [(0, w_rows, gain_two_rows)])
-
-    soon = not (up.plan or down.plan)
-    (kept_rows, rows_back, out_other, w_up_rows), moving = leave(flows, (kept_rows, rows_back, out_other, w_up_rows))
-    ffn_grads = finish_ffn(w_up_rows) if soon else None
+    def finish_up(w_rows):
+        whole = [(0, 0, lead * PART, PART, 1) for lead in range(up.lead)]
+        return finish([(up, whole)], [(rows, up.lead * PART)], [(0, w_rows, gain_two_rows)])
+
+    soon = not up.plan
+    (kept_rows, out_other, w_up_rows), moving = leave(flows, (kept_rows, out_other, w_up_rows))
+    up_grads = finish_up(w_up_rows) if soon else None
     grad_tokens, outputs = joined(kept_rows, rows_back), joined(out_kept, out_other)
     while True:
-        ffn_grads, grad_tokens, outputs = arrive(moving, (ffn_grads, grad_tokens, outputs))
+        up_grads, grad_tokens, outputs = arrive(moving, (up_grads, grad_tokens, outputs))
         if not any(flow.plan for flow in flows):
             break
         _, moving = leave(flows)
-    grad_up, grad_down, grad_gain_ffn = ffn_grads or finish_ffn(w_up_rows)
+    grad_up, grad_gain_ffn = up_grads or finish_up(w_up_rows)
     out_lead, group = width // PART, iter(range(64))
     of_group = lambda flow, extra=0: [(0, 0, next(group) * SMALL, SMALL, 3) for _ in range(flow.lead - extra)]
-    grad_qkv, grad_out, grad_gain_attn = finish([
+    grad_qkv, grad_out, grad_down, grad_gain_attn = finish([
         (one, of_group(one, out_lead) + [(1, 0, lead * PART, PART, 1) for lead in range(out_lead)]),
         (two, of_group(two)),
         (three, of_group(three)),
-    ], [(rows, 3 * width), (rows, width)], [(0, w_qkv_rows, gain_one_rows)])
+        (down, [(2, (lead % 4) * rows, (lead // 4) * PART, PART, 1) for lead in range(down.lead)]),
+    ], [(rows, 3 * width), (rows, width), (4 * rows, width)], [(0, w_qkv_rows, gain_one_rows)])
     return (
         outputs,
         grad_tokens,

time: 270 us -> 271 us (level)
  waiting for transfers between devices: 17.8 us -> 8.62 us
  starting transfers between devices: 29.1 us -> 38.2 us
    ppermute x20 -> x21, waiting for transfers between devices: 13.6 us -> 4.38 us  [crossed(): lax.ppermute(block, ('dp', 'seq'), [(i, i ^ step) for i in range(count)])]
    ppermute x5, starting transfers between devices: 5.63 us -> 13.2 us  [swapped(): return lax.ppermute(block, 'seq', [(0, 1), (1, 0)])]
    ppermute x20 -> x21, starting transfers between devices: 23.4 us -> 25 us  [crossed(): lax.ppermute(block, ('dp', 'seq'), [(i, i ^ step) for i in range(count)])]
    unnamed x66 -> x68, local copies, waits for them, and re-layouts: 9.73 us -> 9.53 us
  transfers between devices with their start and end apart: 25 -> 26, of which waited for: 6 -> 7; matrix products, arithmetic and copies ran while one was open for 4% -> 4% of each run, Pallas kernels for 50% -> 51%
where the time goes in v6:
time: 271 us; the launch traced here: 267 us
  Pallas kernels  197 us (73%)
  starting transfers between devices  38.2 us (14%)
  local copies, waits for them, and re-layouts  15 us (6%)
  waiting for transfers between devices  8.62 us (3%)
  other arithmetic  7.43 us (3%)
    pallas_call x3, Pallas kernels, attend_back(): pl.pallas_call(functools.partial(attend_back_kernel, bk=bk), grid_spec=gr...  69.3 us
    pallas_call x1, Pallas kernels, middle(): pl.pallas_call(functools.partial(middle_kernel, shards=shards, block=bloc...  47.3 us
    pallas_call x1, Pallas kernels, attend(): pl.pallas_call(functools.partial(attend_kernel, bq=bq, unroll=unroll), gr...  30.6 us
    ppermute x21, starting transfers between devices, crossed(): lax.ppermute(block, ('dp', 'seq'), [(i, i ^ step) for i in range(count)])  25 us
    pallas_call x5, Pallas kernels, combine(): pl.pallas_call(functools.partial(combine_kernel, work=work, steps=steps),...  16 us
    pallas_call x2, Pallas kernels, after(): pl.pallas_call(after_kernel, grid_spec=grid_spec, out_shape=jax.ShapeDtyp...  14.3 us
    pallas_call x2, Pallas kernels, before(): pl.pallas_call(functools.partial(before_kernel, shards=shards, block=bloc...  13.9 us
    ppermute x5, starting transfers between devices, swapped(): return lax.ppermute(block, 'seq', [(0, 1), (1, 0)])  13.2 us
  transfers between devices with their start and end apart: 26, of which 7 were waited for; matrix products, arithmetic and copies ran while one was open for 4% of the time, Pallas kernels for 51%

profile of v6, /device:TPU:0, one launch (start us, length us, event | category | flops | bytes accessed | tf_op | source)
XLA Modules:
  0.0 267.2 jit_solution(1660942358072872760)
XLA Ops:
  0.7 2.5 dynamic-slice_bitcast_fusion.2
  3.2 3.0 %collective-permute-start.1 = (s32[512]{0:T(512)S(1)}, s32[512]{0:T(512)S(1)}, u32[]{:S(2)}, u32[]{:S(2)}) collective-permute-start(s32[512]{0:T(512)S(1)} %bitcast.125), channel_id=1, source_target_pairs={{0,1},{1,0},{2,3},{3,2},{4,5},{5,4},{6,7},{7,6},{8,9},{9,8},{10,11... | collective-permute-start | bytes 6152 | tf_op jit(solution)/shard_map/ppermute | solution.py:481
  13.7 7.0 %before.2 = (bf16[1024,2304]{1,0:T(8,128)(2,1)}, bf16[768,1024]{1,0:T(8,128)(2,1)}) custom-call(s32[3]{0:T(128)} %get-tuple-element.256.place, bf16[512,768]{1,0:T(8,128)(2,1)} %get-tuple-element.253.x_ref.x_kept, f32[1,768]{1,0:T(1,128)} %broadcast_in_dim.17.gain_ref, bf16[768,2304]{1,0:T(8,128)(2,1)} %w_ref.7), custom_call_target="tpu_custom_call" | custom-call | flops 1811939328 | bytes 12582912 | tf_op jit(solution)/shard_map/before/pallas_call | solution.py:304
  22.4 4.2 %collective-permute-done.x_ref.x_other = bf16[512,768]{1,0:T(8,128)(2,1)S(1)} collective-permute-done((bf16[512,768]{1,0:T(8,128)(2,1)S(1)}, bf16[512,768]{1,0:T(8,128)(2,1)S(1)}, u32[]{:S(2)}, u32[]{:S(2)}) %collective-permute-start) | collective-permute-done | bytes 786464 | tf_op jit(solution)/shard_map/ppermute | solution.py:481
  27.6 6.9 %before.3 = (bf16[1024,2304]{1,0:T(8,128)(2,1)}, bf16[768,1024]{1,0:T(8,128)(2,1)}) custom-call(s32[3]{0:T(128)} %get-tuple-element.257.place, bf16[512,768]{1,0:T(8,128)(2,1)} %copy-done.12, f32[1,768]{1,0:T(1,128)} %broadcast_in_dim.17.gain_ref, bf16[768,2304]{1,0:T(8,128)(2,1)} %w_ref.7, ...), custom_call_target="tpu_custom_call", output_to_operand_aliasing={{0}: (4, {}), {1}: (5, {})} | custom-call | flops 1811939328 | bytes 12582912 | tf_op jit(solution)/shard_map/before/pallas_call | solution.py:304
  34.5 30.6 %attend.1 = (bf16[1024,768]{1,0:T(8,128)(2,1)S(1)}, f32[48,1024]{1,0:T(8,128)S(1)}) custom-call(s32[4]{0:T(128)S(1)} %and_select_fusion.1.first, s32[1,1024]{1,0:T(1,128)S(1)} %broadcast_select_fusion.seg_ref, bf16[1024,2304]{1,0:T(8,128)(2,1)} %get-tuple-element.133.q_ref.k_ref.v_ref, bf16[1024,2304]{1,0:T(8,128)(2,1)} %get-tuple-element.133.q_ref.k_ref.v_ref, ...), custom_call_target="tpu_custom_call" | custom-call | flops 30064771072 | bytes 8388608 | tf_op jit(solution)/shard_map/attend/pallas_call | solution.py:86
  67.8 47.3 %middle.1 = (bf16[512,768]{1,0:T(8,128)(2,1)}, bf16[512,768]{1,0:T(8,128)(2,1)}, bf16[1024,768]{1,0:T(8,128)(2,1)}, bf16[1024,768]{1,0:T(8,128)(2,1)}, bf16[8,16...) custom-call(s32[3]{0:T(128)} %get-tuple-element.256.place, ...), custom_call_target="tpu_custom_call" | custom-call | flops 28991029248 | bytes 41943040 | tf_op jit(solution)/shard_map/middle/pallas_call | solution.py:436
  118.3 24.1 %attend_back.3 = (bf16[1024,256]{1,0:T(8,128)(2,1)}, bf16[1024,256]{1,0:T(8,128)(2,1)}, bf16[1024,256]{1,0:T(8,128)(2,1)}, bf16[4,16,24,384]{3,2,1,0:T(8,128)(2,1)}, bf16[4,16,24,384]{3,2,1,0:T(8,128)(2,1)}) custom-call(s32[4]{0:T(128)} %and_select_fusion.last, s32[3]{0:T(128)} %get-tuple-element.256.place, s32[1,1024]{1,0:T(1,128)} %copy-done, ...), custom_call_target="tpu_custom_call" | custom-call | flops 21474836480 | bytes 8388608 | tf_op jit(solution)/shard_map/attend_back/pallas_call | solution.py:211
  144.0 3.5 %combine.5 = (bf16[64,24,384]{2,1,0:T(8,128)(2,1)}, bf16[64,24,384]{2,1,0:T(8,128)(2,1)}) custom-call(bf16[8,2,2,2,2,24,384]{6,5,4,3,2,1,0:T(8,128)(2,1)} %bitcast.60, bf16[8,2,2,2,2,24,384]{6,5,4,3,2,1,0:T(8,128)(2,1)} %bitcast.16.refs_1_, bf16[8,2,2,2,2,24,384]{6,5,4,3,2,1,0:T(8,128)(2,1)} %bitcast.50, bf16[8,2,2,2,2,24,384]{6,5,4,3,2,1,0:T(8,128)(2,1)} %bitcast.55), custom_call_target="tpu_custom_call" | custom-call | flops 1048576 | bytes 8388608 | tf_op jit(solution)/shard_map/combine/pallas_call | solution.py:618
  149.3 32.3 %attend_back.4 = (bf16[1024,384]{1,0:T(8,128)(2,1)}, bf16[1024,384]{1,0:T(8,128)(2,1)}, bf16[1024,384]{1,0:T(8,128)(2,1)}, bf16[3,16,24,384]{3,2,1,0:T(8,128)(2,1)}, bf16[3,16,24,384]{3,2,1,0:T(8,128)(2,1)}) custom-call(s32[4]{0:T(128)} %and_select_fusion.last, s32[3]{0:T(128)} %get-tuple-element.256.place, s32[1,1024]{1,0:T(1,128)} %copy-done, ...), custom_call_target="tpu_custom_call" | custom-call | flops 32212254720 | bytes 8388608 | tf_op jit(solution)/shard_map/attend_back/pallas_call | solution.py:211
  183.4 3.5 %combine.6 = (bf16[32,24,384]{2,1,0:T(8,128)(2,1)}, bf16[32,24,384]{2,1,0:T(8,128)(2,1)}, bf16[32,24,384]{2,1,0:T(8,128)(2,1)}) custom-call(bf16[8,2,2,2,2,24,384]{6,5,4,3,2,1,0:T(8,128)(2,1)} %bitcast.61, bf16[8,2,2,2,2,24,384]{6,5,4,3,2,1,0:T(8,128)(2,1)} %bitcast.16.refs_1_, bf16[8,2,2,2,24,384]{5,4,3,2,1,0:T(8,128)(2,1)} %bitcast.79, ...), custom_call_target="tpu_custom_call" | custom-call | flops 1048576 | bytes 8388608 | tf_op jit(solution)/shard_map/combine/pallas_call | solution.py:618
  186.8 2.3 collective-permute-start.9
  191.8 12.8 %attend_back.5 = (bf16[1024,128]{1,0:T(8,128)(2,1)}, bf16[1024,128]{1,0:T(8,128)(2,1)}, bf16[1024,128]{1,0:T(8,128)(2,1)}, bf16[1,16,24,384]{3,2,1,0:T(8,128)(2,1)}, bf16[1,16,24,384]{3,2,1,0:T(8,128)(2,1)}) custom-call(s32[4]{0:T(128)} %and_select_fusion.last, s32[3]{0:T(128)} %get-tuple-element.256.place, s32[1,1024]{1,0:T(1,128)} %copy-done, ...), custom_call_target="tpu_custom_call" | custom-call | flops 10737418240 | bytes 8388608 | tf_op jit(solution)/shard_map/attend_back/pallas_call | solution.py:211
  206.9 3.5 %combine.7 = (bf16[16,24,384]{2,1,0:T(8,128)(2,1)}, bf16[16,24,384]{2,1,0:T(8,128)(2,1)}, bf16[16,24,384]{2,1,0:T(8,128)(2,1)}, bf16[24,24,384]{2,1,0:T(8,128)(2,1)}) custom-call(bf16[8,2,2,2,2,24,384]{6,5,4,3,2,1,0:T(8,128)(2,1)} %bitcast.62, bf16[8,2,2,2,2,24,384]{6,5,4,3,2,1,0:T(8,128)(2,1)} %bitcast.16.refs_1_, bf16[8,2,2,2,24,384]{5,4,3,2,1,0:T(8,128)(2,1)} %bitcast.80, ...), custom_call_target="tpu_custom_call" | custom-call | flops 1048576 | bytes 8388608 | tf_op jit(solution)/shard_map/combine/pallas_call | solution.py:618
  212.4 4.6 %collective-permute-start.14 = (bf16[16,24,384]{2,1,0:T(8,128)(2,1)}, bf16[16,24,384]{2,1,0:T(8,128)(2,1)S(1)}, u32[]{:S(2)}, u32[]{:S(2)}) collective-permute-start(bf16[16,24,384]{2,1,0:T(8,128)(2,1)} %get-tuple-element.186), channel_id=1, source_target_pairs={{0,16},{1,17},{2,18},{3,19},{4,20},{5,21},{6,22},{7,23},{8,24},{9,... | collective-permute-start | bytes 884744 | tf_op jit(solution)/shard_map/ppermute | solution.py:498
  219.1 7.1 %after.2 = bf16[512,768]{1,0:T(8,128)(2,1)} custom-call(s32[3]{0:T(128)} %get-tuple-element.257.place, bf16[512,768]{1,0:T(8,128)(2,1)} %copy-done.12, f32[1,768]{1,0:T(1,128)} %broadcast_in_dim.17.gain_ref, bf16[1024,768]{1,0:T(8,128)(2,1)} %get-tuple-element.212.gx_ref, bf16[768,2304]{1,0:T(8,128)(2,1)} %w_ref.7, ...), custom_call_target="tpu_custom_call" | custom-call | flops 1811939328 | bytes 16777216 | tf_op jit(solution)/shard_map/after/pallas_call | solution.py:470
  226.4 6.0 %collective-permute-start.25 = (bf16[512,768]{1,0:T(8,128)(2,1)}, bf16[512,768]{1,0:T(8,128)(2,1)S(1)}, u32[]{:S(2)}, u32[]{:S(2)}) collective-permute-start(bf16[512,768]{1,0:T(8,128)(2,1)} %after.2), channel_id=1, source_target_pairs={{0,1},{1,0},{2,3},{3,2},{4,5},{5,4},{6,7},{7,6},{8,9},{9,8},{10,11... | collective-permute-start | bytes 2359304 | tf_op jit(solution)/shard_map/ppermute | solution.py:481
  232.4 2.8 %combine.8 = (bf16[8,24,384]{2,1,0:T(8,128)(2,1)}, bf16[12,24,384]{2,1,0:T(8,128)(2,1)}, bf16[16,24,384]{2,1,0:T(8,128)(2,1)}, bf16[4,24,384]{2,1,0:T(8,128)(2,1)}) custom-call(bf16[8,2,2,2,2,24,384]{6,5,4,3,2,1,0:T(8,128)(2,1)} %bitcast.63, bf16[8,2,2,2,2,24,384]{6,5,4,3,2,1,0:T(8,128)(2,1)} %bitcast.16.refs_1_, bf16[8,2,2,2,24,384]{5,4,3,2,1,0:T(8,128)(2,1)} %bitcast.81, ...), custom_call_target="tpu_custom_call" | custom-call | flops 1048576 | bytes 8388608 | tf_op jit(solution)/shard_map/combine/pallas_call | solution.py:618
  236.5 2.3 collective-permute-start.21
  239.8 7.2 %after.3 = bf16[512,768]{1,0:T(8,128)(2,1)} custom-call(s32[3]{0:T(128)} %get-tuple-element.256.place, bf16[512,768]{1,0:T(8,128)(2,1)} %get-tuple-element.253.x_ref.x_kept, f32[1,768]{1,0:T(1,128)} %broadcast_in_dim.17.gain_ref, bf16[1024,768]{1,0:T(8,128)(2,1)} %get-tuple-element.212.gx_ref, bf16[768,2304]{1,0:T(8,128)(2,1)} %w_ref.7, ...), custom_call_target="tpu_custom_call" | custom-call | flops 1811939328 | bytes 16777216 | tf_op jit(solution)/shard_map/after/pallas_call | solution.py:470
  248.2 2.8 %combine.9 = (bf16[12,24,384]{2,1,0:T(8,128)(2,1)}, bf16[8,24,384]{2,1,0:T(8,128)(2,1)}, bf16[4,24,384]{2,1,0:T(8,128)(2,1)}) custom-call(bf16[8,2,2,2,2,24,384]{6,5,4,3,2,1,0:T(8,128)(2,1)} %bitcast.53, bf16[8,2,2,2,2,24,384]{6,5,4,3,2,1,0:T(8,128)(2,1)} %bitcast.58, bf16[8,2,2,2,24,384]{5,4,3,2,1,0:T(8,128)(2,1)} %bitcast.77, ...), custom_call_target="tpu_custom_call" | custom-call | flops 1048576 | bytes 8388608 | tf_op jit(solution)/shard_map/combine/pallas_call | solution.py:618
  251.0 2.5 collective-permute-start.24
  256.9 2.4 finish.2
  264.0 2.9 %finish.3 = (f32[24,2304]{1,0:T(8,128)}, f32[24,768]{1,0:T(8,128)}, f32[96,768]{1,0:T(8,128)}, f32[1,24]{1,0:T(1,128)}) custom-call(bf16[4,2,2,2,2,24,384]{6,5,4,3,2,1,0:T(8,128)(2,1)} %bitcast.69, bf16[4,2,2,2,2,24,384]{6,5,4,3,2,1,0:T(8,128)(2,1)} %bitcast.74, bf16[4,2,2,2,24,384]{5,4,3,2,1,0:T(8,128)(2,1)} %bitcast.94, ...), custom_call_target="tpu_custom_call" | custom-call | flops 1048576 | bytes 4194304 | tf_op jit(solution)/shard_map/finish/pallas_call | solution.py:688
  (130 shorter events, 41.9 us)
Async XLA Ops:
  3.2 18.8 %collective-permute-start.1 = (s32[512]{0:T(512)S(1)}, s32[512]{0:T(512)S(1)}, u32[]{:S(2)}, u32[]{:S(2)}) collective-permute-start(s32[512]{0:T(512)S(1)} %bitcast.125), channel_id=1, source_target_pairs={{0,1},{1,0},{2,3},{3,2},{4,5},{5,4},{6,7},{7,6},{8,9},{9,8},{10,11... | collective-permute-start | bytes 6152 | tf_op jit(solution)/shard_map/ppermute | solution.py:481
  6.2 20.5 %collective-permute-start = (bf16[512,768]{1,0:T(8,128)(2,1)S(1)}, bf16[512,768]{1,0:T(8,128)(2,1)S(1)}, u32[]{:S(2)}, u32[]{:S(2)}) collective-permute-start(bf16[512,768]{1,0:T(8,128)(2,1)S(1)} %get-tuple-element.128), channel_id=1, source_target_pairs={{0,1},{1,0},{2,3},{3,2},{4,5},{5,4},{6,7},{7,6},{8,9},{9,8},{10,11... | collective-permute-start | bytes 2359304 | tf_op jit(solution)/shard_map/ppermute | solution.py:481
  7.3 59.6 %collective-permute-start.2 = (bf16[512,768]{1,0:T(8,128)(2,1)S(1)}, bf16[512,768]{1,0:T(8,128)(2,1)S(1)}, u32[]{:S(2)}, u32[]{:S(2)}) collective-permute-start(bf16[512,768]{1,0:T(8,128)(2,1)S(1)} %get-tuple-element.250), channel_id=1, source_target_pairs={{0,1},{1,0},{2,3},{3,2},{4,5},{5,4},{6,7},{7,6},{8,9},{9,8},{10,11... | collective-permute-start | bytes 2359304 | tf_op jit(solution)/shard_map/ppermute | solution.py:481
  115.1 27.4 %collective-permute-start.3 = (bf16[128,24,384]{2,1,0:T(8,128)(2,1)}, bf16[128,24,384]{2,1,0:T(8,128)(2,1)}, u32[]{:S(2)}, u32[]{:S(2)}) collective-permute-start(bf16[128,24,384]{2,1,0:T(8,128)(2,1)} %bitcast.127), channel_id=1, source_target_pairs={{0,2},{1,3},{2,0},{3,1},{4,6},{5,7},{6,4},{7,5},{8,10},{9,11},{10,... | collective-permute-start | bytes 7077896 | tf_op jit(solution)/shard_map/ppermute | solution.py:498
  115.2 27.3 %collective-permute-start.4 = (bf16[128,24,384]{2,1,0:T(8,128)(2,1)}, bf16[128,24,384]{2,1,0:T(8,128)(2,1)S(1)}, u32[]{:S(2)}, u32[]{:S(2)}) collective-permute-start(bf16[128,24,384]{2,1,0:T(8,128)(2,1)} %bitcast.126), channel_id=1, source_target_pairs={{0,2},{1,3},{2,0},{3,1},{4,6},{5,7},{6,4},{7,5},{8,10},{9,11},{10,... | collective-permute-start | bytes 7077896 | tf_op jit(solution)/shard_map/ppermute | solution.py:498
  116.2 26.3 %collective-permute-start.5 = (bf16[512,768]{1,0:T(8,128)(2,1)}, bf16[512,768]{1,0:T(8,128)(2,1)S(1)}, u32[]{:S(2)}, u32[]{:S(2)}) collective-permute-start(bf16[512,768]{1,0:T(8,128)(2,1)} %get-tuple-element.144), channel_id=1, source_target_pairs={{0,1},{1,0},{2,3},{3,2},{4,5},{5,4},{6,7},{7,6},{8,9},{9,8},{10,11... | collective-permute-start | bytes 2359304 | tf_op jit(solution)/shard_map/ppermute | solution.py:481
  147.4 34.1 %collective-permute-start.6 = (bf16[64,24,384]{2,1,0:T(8,128)(2,1)}, bf16[64,24,384]{2,1,0:T(8,128)(2,1)S(1)}, u32[]{:S(2)}, u32[]{:S(2)}) collective-permute-start(bf16[64,24,384]{2,1,0:T(8,128)(2,1)} %get-tuple-element.157), channel_id=1, source_target_pairs={{0,4},{1,5},{2,6},{3,7},{4,0},{5,1},{6,2},{7,3},{8,12},{9,13},{10,... | collective-permute-start | bytes 3538952 | tf_op jit(solution)/shard_map/ppermute | solution.py:498
  147.5 34.1 %collective-permute-start.7 = (bf16[64,24,384]{2,1,0:T(8,128)(2,1)}, bf16[64,24,384]{2,1,0:T(8,128)(2,1)S(1)}, u32[]{:S(2)}, u32[]{:S(2)}) collective-permute-start(bf16[64,24,384]{2,1,0:T(8,128)(2,1)} %get-tuple-element.158), channel_id=1, source_target_pairs={{0,8},{1,9},{2,10},{3,11},{4,12},{5,13},{6,14},{7,15},{8,0},{9,1},... | collective-permute-start | bytes 3538952 | tf_op jit(solution)/shard_map/ppermute | solution.py:498
  148.9 32.8 %collective-permute-start.8 = (bf16[64,24,384]{2,1,0:T(8,128)(2,1)}, bf16[64,24,384]{2,1,0:T(8,128)(2,1)S(1)}, u32[]{:S(2)}, u32[]{:S(2)}) collective-permute-start(bf16[64,24,384]{2,1,0:T(8,128)(2,1)} %bitcast.128), channel_id=1, source_target_pairs={{0,2},{1,3},{2,0},{3,1},{4,6},{5,7},{6,4},{7,5},{8,10},{9,11},{10,... | collective-permute-start | bytes 3538952 | tf_op jit(solution)/shard_map/ppermute | solution.py:498
  186.8 17.8 %collective-permute-start.9 = (bf16[32,24,384]{2,1,0:T(8,128)(2,1)}, bf16[32,24,384]{2,1,0:T(8,128)(2,1)S(1)}, u32[]{:S(2)}, u32[]{:S(2)}) collective-permute-start(bf16[32,24,384]{2,1,0:T(8,128)(2,1)} %get-tuple-element.169), channel_id=1, source_target_pairs={{0,1},{1,0},{2,3},{3,2},{4,5},{5,4},{6,7},{7,6},{8,9},{9,8},{10,11... | collective-permute-start | bytes 1769480 | tf_op jit(solution)/shard_map/ppermute | solution.py:498
  189.1 16.1 %collective-permute-start.10 = (bf16[32,24,384]{2,1,0:T(8,128)(2,1)}, bf16[32,24,384]{2,1,0:T(8,128)(2,1)S(1)}, u32[]{:S(2)}, u32[]{:S(2)}) collective-permute-start(bf16[32,24,384]{2,1,0:T(8,128)(2,1)} %get-tuple-element.170), channel_id=1, source_target_pairs={{0,4},{1,5},{2,6},{3,7},{4,0},{5,1},{6,2},{7,3},{8,12},{9,13},{10,... | collective-permute-start | bytes 1769480 | tf_op jit(solution)/shard_map/ppermute | solution.py:498
  189.5 16.3 %collective-permute-start.11 = (bf16[32,24,384]{2,1,0:T(8,128)(2,1)}, bf16[32,24,384]{2,1,0:T(8,128)(2,1)S(1)}, u32[]{:S(2)}, u32[]{:S(2)}) collective-permute-start(bf16[32,24,384]{2,1,0:T(8,128)(2,1)} %get-tuple-element.171), channel_id=1, source_target_pairs={{0,8},{1,9},{2,10},{3,11},{4,12},{5,13},{6,14},{7,15},{8,0},{9,1},... | collective-permute-start | bytes 1769480 | tf_op jit(solution)/shard_map/ppermute | solution.py:498
  190.3 15.5 %collective-permute-start.12 = (bf16[48,24,384]{2,1,0:T(8,128)(2,1)}, bf16[48,24,384]{2,1,0:T(8,128)(2,1)S(1)}, u32[]{:S(2)}, u32[]{:S(2)}) collective-permute-start(bf16[48,24,384]{2,1,0:T(8,128)(2,1)} %bitcast.129), channel_id=1, source_target_pairs={{0,2},{1,3},{2,0},{3,1},{4,6},{5,7},{6,4},{7,5},{8,10},{9,11},{10,... | collective-permute-start | bytes 2654216 | tf_op jit(solution)/shard_map/ppermute | solution.py:498
  210.4 16.0 %collective-permute-start.16 = (bf16[24,24,384]{2,1,0:T(8,128)(2,1)}, bf16[24,24,384]{2,1,0:T(8,128)(2,1)S(1)}, u32[]{:S(2)}, u32[]{:S(2)}) collective-permute-start(bf16[24,24,384]{2,1,0:T(8,128)(2,1)} %get-tuple-element.188), channel_id=1, source_target_pairs={{0,4},{1,5},{2,6},{3,7},{4,0},{5,1},{6,2},{7,3},{8,12},{9,13},{10,... | collective-permute-start | bytes 1327112 | tf_op jit(solution)/shard_map/ppermute | solution.py:498
  211.6 14.7 %collective-permute-start.13 = (bf16[16,24,384]{2,1,0:T(8,128)(2,1)}, bf16[16,24,384]{2,1,0:T(8,128)(2,1)S(1)}, u32[]{:S(2)}, u32[]{:S(2)}) collective-permute-start(bf16[16,24,384]{2,1,0:T(8,128)(2,1)} %get-tuple-element.185), channel_id=1, source_target_pairs={{0,8},{1,9},{2,10},{3,11},{4,12},{5,13},{6,14},{7,15},{8,0},{9,1},... | collective-permute-start | bytes 884744 | tf_op jit(solution)/shard_map/ppermute | solution.py:498
  212.4 13.9 %collective-permute-start.14 = (bf16[16,24,384]{2,1,0:T(8,128)(2,1)}, bf16[16,24,384]{2,1,0:T(8,128)(2,1)S(1)}, u32[]{:S(2)}, u32[]{:S(2)}) collective-permute-start(bf16[16,24,384]{2,1,0:T(8,128)(2,1)} %get-tuple-element.186), channel_id=1, source_target_pairs={{0,16},{1,17},{2,18},{3,19},{4,20},{5,21},{6,22},{7,23},{8,24},{9,... | collective-permute-start | bytes 884744 | tf_op jit(solution)/shard_map/ppermute | solution.py:498
  217.0 9.3 %collective-permute-start.15 = (bf16[16,24,384]{2,1,0:T(8,128)(2,1)}, bf16[16,24,384]{2,1,0:T(8,128)(2,1)S(1)}, u32[]{:S(2)}, u32[]{:S(2)}) collective-permute-start(bf16[16,24,384]{2,1,0:T(8,128)(2,1)} %get-tuple-element.187), channel_id=1, source_target_pairs={{0,1},{1,0},{2,3},{3,2},{4,5},{5,4},{6,7},{7,6},{8,9},{9,8},{10,11... | collective-permute-start | bytes 884744 | tf_op jit(solution)/shard_map/ppermute | solution.py:498
  226.4 32.9 %collective-permute-start.25 = (bf16[512,768]{1,0:T(8,128)(2,1)}, bf16[512,768]{1,0:T(8,128)(2,1)S(1)}, u32[]{:S(2)}, u32[]{:S(2)}) collective-permute-start(bf16[512,768]{1,0:T(8,128)(2,1)} %after.2), channel_id=1, source_target_pairs={{0,1},{1,0},{2,3},{3,2},{4,5},{5,4},{6,7},{7,6},{8,9},{9,8},{10,11... | collective-permute-start | bytes 2359304 | tf_op jit(solution)/shard_map/ppermute | solution.py:481
  235.2 12.2 %collective-permute-start.20 = (bf16[16,24,384]{2,1,0:T(8,128)(2,1)}, bf16[16,24,384]{2,1,0:T(8,128)(2,1)S(1)}, u32[]{:S(2)}, u32[]{:S(2)}) collective-permute-start(bf16[16,24,384]{2,1,0:T(8,128)(2,1)} %get-tuple-element.210), channel_id=1, source_target_pairs={{0,8},{1,9},{2,10},{3,11},{4,12},{5,13},{6,14},{7,15},{8,0},{9,1},... | collective-permute-start | bytes 884744 | tf_op jit(solution)/shard_map/ppermute | solution.py:498
  235.6 11.8 %collective-permute-start.19 = (bf16[12,24,384]{2,1,0:T(8,128)(2,1)}, bf16[12,24,384]{2,1,0:T(8,128)(2,1)S(1)}, u32[]{:S(2)}, u32[]{:S(2)}) collective-permute-start(bf16[12,24,384]{2,1,0:T(8,128)(2,1)} %get-tuple-element.209), channel_id=1, source_target_pairs={{0,4},{1,5},{2,6},{3,7},{4,0},{5,1},{6,2},{7,3},{8,12},{9,13},{10,... | collective-permute-start | bytes 663560 | tf_op jit(solution)/shard_map/ppermute | solution.py:498
  236.5 10.9 %collective-permute-start.21 = (bf16[4,24,384]{2,1,0:T(8,128)(2,1)}, bf16[4,24,384]{2,1,0:T(8,128)(2,1)S(1)}, u32[]{:S(2)}, u32[]{:S(2)}) collective-permute-start(bf16[4,24,384]{2,1,0:T(8,128)(2,1)} %get-tuple-element.211), channel_id=1, source_target_pairs={{0,12},{1,13},{2,14},{3,15},{4,8},{5,9},{6,10},{7,11},{8,4},{9,5},... | collective-permute-start | bytes 221192 | tf_op jit(solution)/shard_map/ppermute | solution.py:498
  251.0 11.0 %collective-permute-start.24 = (bf16[4,24,384]{2,1,0:T(8,128)(2,1)}, bf16[4,24,384]{2,1,0:T(8,128)(2,1)S(1)}, u32[]{:S(2)}, u32[]{:S(2)}) collective-permute-start(bf16[4,24,384]{2,1,0:T(8,128)(2,1)} %get-tuple-element.225), channel_id=1, source_target_pairs={{0,17},{1,16},{2,19},{3,18},{4,21},{5,20},{6,23},{7,22},{8,25},{9,... | collective-permute-start | bytes 221192 | tf_op jit(solution)/shard_map/ppermute | solution.py:498
  253.5 9.8 %collective-permute-start.23 = (bf16[8,24,384]{2,1,0:T(8,128)(2,1)}, bf16[8,24,384]{2,1,0:T(8,128)(2,1)S(1)}, u32[]{:S(2)}, u32[]{:S(2)}) collective-permute-start(bf16[8,24,384]{2,1,0:T(8,128)(2,1)} %get-tuple-element.224), channel_id=1, source_target_pairs={{0,16},{1,17},{2,18},{3,19},{4,20},{5,21},{6,22},{7,23},{8,24},{9,... | collective-permute-start | bytes 442376 | tf_op jit(solution)/shard_map/ppermute | solution.py:498
  254.3 9.0 %collective-permute-start.22 = (bf16[12,24,384]{2,1,0:T(8,128)(2,1)}, bf16[12,24,384]{2,1,0:T(8,128)(2,1)S(1)}, u32[]{:S(2)}, u32[]{:S(2)}) collective-permute-start(bf16[12,24,384]{2,1,0:T(8,128)(2,1)} %get-tuple-element.223), channel_id=1, source_target_pairs={{0,1},{1,0},{2,3},{3,2},{4,5},{5,4},{6,7},{7,6},{8,9},{9,8},{10,11... | collective-permute-start | bytes 663560 | tf_op jit(solution)/shard_map/ppermute | solution.py:498
  (36 other events, 138.2 us)

commit v7 on v6

--- a/solution.py
+++ b/solution.py
@@ -90,7 +90,7 @@
             jax.ShapeDtypeStruct((length, width // 3), jnp.bfloat16),
             jax.ShapeDtypeStruct((groups * 2 * GROUP, length), jnp.float32),
         ],
-        compiler_params=pltpu.CompilerParams(vmem_limit_bytes=48 << 20),
+        compiler_params=pltpu.CompilerParams(vmem_limit_bytes=54 << 20),
         cost_estimate=pl.CostEstimate(flops=28 << 30, bytes_accessed=8 << 20, transcendentals=24 * length * length),
         name="attend",
     )(first, seg, proj, proj, proj)

time: 271 us -> 270 us (level)
  starting transfers between devices: 38.2 us -> 31.2 us
  waiting for transfers between devices: 8.62 us -> 12.9 us
    ppermute x21, waiting for transfers between devices: 4.38 us -> 9.81 us  [crossed(): lax.ppermute(block, ('dp', 'seq'), [(i, i ^ step) for i in range(count)])]
    ppermute x5, starting transfers between devices: 13.2 us -> 9.23 us  [swapped(): return lax.ppermute(block, 'seq', [(0, 1), (1, 0)])]
    ppermute x21, starting transfers between devices: 25 us -> 22 us  [crossed(): lax.ppermute(block, ('dp', 'seq'), [(i, i ^ step) for i in range(count)])]
    unnamed x68 -> x62, local copies, waits for them, and re-layouts: 9.53 us -> 7.74 us
  transfers between devices with their start and end apart: 26 -> 26, of which waited for: 7 -> 7; matrix products, arithmetic and copies ran while one was open for 4% -> 4% of each run, Pallas kernels for 51% -> 52%
where the time goes in v7:
time: 270 us; the launch traced here: 266 us
  Pallas kernels  199 us (74%)
  starting transfers between devices  31.2 us (12%)
  local copies, waits for them, and re-layouts  13.2 us (5%)
  waiting for transfers between devices  12.9 us (5%)
  other arithmetic  8.54 us (3%)
    pallas_call x3, Pallas kernels, attend_back(): pl.pallas_call(functools.partial(attend_back_kernel, bk=bk), grid_spec=gr...  69.3 us
    pallas_call x1, Pallas kernels, middle(): pl.pallas_call(functools.partial(middle_kernel, shards=shards, block=bloc...  47.2 us
    pallas_call x1, Pallas kernels, attend(): pl.pallas_call(functools.partial(attend_kernel, bq=bq, unroll=unroll), gr...  33.2 us
    ppermute x21, starting transfers between devices, crossed(): lax.ppermute(block, ('dp', 'seq'), [(i, i ^ step) for i in range(count)])  22 us
    pallas_call x5, Pallas kernels, combine(): pl.pallas_call(functools.partial(combine_kernel, work=work, steps=steps),...  16 us
    pallas_call x2, Pallas kernels, after(): pl.pallas_call(after_kernel, grid_spec=grid_spec, out_shape=jax.ShapeDtyp...  14.3 us
    pallas_call x2, Pallas kernels, before(): pl.pallas_call(functools.partial(before_kernel, shards=shards, block=bloc...  14 us
    ppermute x21, waiting for transfers between devices, crossed(): lax.ppermute(block, ('dp', 'seq'), [(i, i ^ step) for i in range(count)])  9.81 us
  transfers between devices with their start and end apart: 26, of which 7 were waited for; matrix products, arithmetic and copies ran while one was open for 4% of the time, Pallas kernels for 52%

profile of v7, /device:TPU:0, one launch (start us, length us, event | category | flops | bytes accessed | tf_op | source)
XLA Modules:
  0.0 266.5 jit_solution(11489733122576054790)
XLA Ops:
  0.7 2.5 dynamic-slice_bitcast_fusion.2
  3.2 3.0 %collective-permute-start.1 = (s32[512]{0:T(512)S(1)}, s32[512]{0:T(512)S(1)}, u32[]{:S(2)}, u32[]{:S(2)}) collective-permute-start(s32[512]{0:T(512)S(1)} %bitcast.125), channel_id=1, source_target_pairs={{0,1},{1,0},{2,3},{3,2},{4,5},{5,4},{6,7},{7,6},{8,9},{9,8},{10,11... | collective-permute-start | bytes 6152 | tf_op jit(solution)/shard_map/ppermute | solution.py:481
  13.7 7.1 %before.2 = (bf16[1024,2304]{1,0:T(8,128)(2,1)}, bf16[768,1024]{1,0:T(8,128)(2,1)}) custom-call(s32[3]{0:T(128)} %get-tuple-element.256.place, bf16[512,768]{1,0:T(8,128)(2,1)} %get-tuple-element.253.x_ref.x_kept, f32[1,768]{1,0:T(1,128)} %broadcast_in_dim.17.gain_ref, bf16[768,2304]{1,0:T(8,128)(2,1)} %w_ref.7), custom_call_target="tpu_custom_call" | custom-call | flops 1811939328 | bytes 12582912 | tf_op jit(solution)/shard_map/before/pallas_call | solution.py:304
  23.6 3.1 %collective-permute-done.x_ref.x_other = bf16[512,768]{1,0:T(8,128)(2,1)S(1)} collective-permute-done((bf16[512,768]{1,0:T(8,128)(2,1)S(1)}, bf16[512,768]{1,0:T(8,128)(2,1)S(1)}, u32[]{:S(2)}, u32[]{:S(2)}) %collective-permute-start) | collective-permute-done | bytes 786464 | tf_op jit(solution)/shard_map/ppermute | solution.py:481
  27.6 7.0 %before.3 = (bf16[1024,2304]{1,0:T(8,128)(2,1)}, bf16[768,1024]{1,0:T(8,128)(2,1)}) custom-call(s32[3]{0:T(128)} %get-tuple-element.257.place, bf16[512,768]{1,0:T(8,128)(2,1)} %copy-done.9, f32[1,768]{1,0:T(1,128)} %broadcast_in_dim.17.gain_ref, bf16[768,2304]{1,0:T(8,128)(2,1)} %w_ref.7, ...), custom_call_target="tpu_custom_call", output_to_operand_aliasing={{0}: (4, {}), {1}: (5, {})} | custom-call | flops 1811939328 | bytes 12582912 | tf_op jit(solution)/shard_map/before/pallas_call | solution.py:304
  34.5 33.2 %attend.1 = (bf16[1024,768]{1,0:T(8,128)(2,1)}, f32[48,1024]{1,0:T(8,128)}) custom-call(s32[4]{0:T(128)} %and_select_fusion.1.first, s32[1,1024]{1,0:T(1,128)} %broadcast_select_fusion.seg_ref, bf16[1024,2304]{1,0:T(8,128)(2,1)} %get-tuple-element.133.q_ref.k_ref.v_ref, bf16[1024,2304]{1,0:T(8,128)(2,1)} %get-tuple-element.133.q_ref.k_ref.v_ref, ...), custom_call_target="tpu_custom_call" | custom-call | flops 30064771072 | bytes 8388608 | tf_op jit(solution)/shard_map/attend/pallas_call | solution.py:86
  68.7 47.2 %middle.1 = (bf16[512,768]{1,0:T(8,128)(2,1)}, bf16[512,768]{1,0:T(8,128)(2,1)}, bf16[1024,768]{1,0:T(8,128)(2,1)}, bf16[1024,768]{1,0:T(8,128)(2,1)}, bf16[8,16...) custom-call(s32[3]{0:T(128)} %get-tuple-element.256.place, ...), custom_call_target="tpu_custom_call" | custom-call | flops 28991029248 | bytes 41943040 | tf_op jit(solution)/shard_map/middle/pallas_call | solution.py:436
  117.0 2.6 collective-permute-start.5
  119.7 24.1 %attend_back.3 = (bf16[1024,256]{1,0:T(8,128)(2,1)}, bf16[1024,256]{1,0:T(8,128)(2,1)}, bf16[1024,256]{1,0:T(8,128)(2,1)}, bf16[4,16,24,384]{3,2,1,0:T(8,128)(2,1)}, bf16[4,16,24,384]{3,2,1,0:T(8,128)(2,1)}) custom-call(s32[4]{0:T(128)} %and_select_fusion.last, s32[3]{0:T(128)} %get-tuple-element.256.place, s32[1,1024]{1,0:T(1,128)} %broadcast_select_fusion.seg_ref, ...), custom_call_target="tpu_custom_call" | custom-call | flops 21474836480 | bytes 8388608 | tf_op jit(solution)/shard_map/attend_back/pallas_call | solution.py:211
  145.3 3.5 %combine.5 = (bf16[64,24,384]{2,1,0:T(8,128)(2,1)}, bf16[64,24,384]{2,1,0:T(8,128)(2,1)}) custom-call(bf16[8,2,2,2,2,24,384]{6,5,4,3,2,1,0:T(8,128)(2,1)} %bitcast.60, bf16[8,2,2,2,2,24,384]{6,5,4,3,2,1,0:T(8,128)(2,1)} %bitcast.16.refs_1_, bf16[8,2,2,2,2,24,384]{6,5,4,3,2,1,0:T(8,128)(2,1)} %bitcast.50, bf16[8,2,2,2,2,24,384]{6,5,4,3,2,1,0:T(8,128)(2,1)} %bitcast.55), custom_call_target="tpu_custom_call" | custom-call | flops 1048576 | bytes 8388608 | tf_op jit(solution)/shard_map/combine/pallas_call | solution.py:618
  148.8 2.8 %collective-permute-start.7 = (bf16[64,24,384]{2,1,0:T(8,128)(2,1)}, bf16[64,24,384]{2,1,0:T(8,128)(2,1)S(1)}, u32[]{:S(2)}, u32[]{:S(2)}) collective-permute-start(bf16[64,24,384]{2,1,0:T(8,128)(2,1)} %get-tuple-element.158), channel_id=1, source_target_pairs={{0,8},{1,9},{2,10},{3,11},{4,12},{5,13},{6,14},{7,15},{8,0},{9,1},... | collective-permute-start | bytes 3538952 | tf_op jit(solution)/shard_map/ppermute | solution.py:498
  151.6 32.2 %attend_back.4 = (bf16[1024,384]{1,0:T(8,128)(2,1)}, bf16[1024,384]{1,0:T(8,128)(2,1)}, bf16[1024,384]{1,0:T(8,128)(2,1)}, bf16[3,16,24,384]{3,2,1,0:T(8,128)(2,1)}, bf16[3,16,24,384]{3,2,1,0:T(8,128)(2,1)}) custom-call(s32[4]{0:T(128)} %and_select_fusion.last, s32[3]{0:T(128)} %get-tuple-element.256.place, s32[1,1024]{1,0:T(1,128)} %broadcast_select_fusion.seg_ref, ...), custom_call_target="tpu_custom_call" | custom-call | flops 32212254720 | bytes 8388608 | tf_op jit(solution)/shard_map/attend_back/pallas_call | solution.py:211
  185.6 3.5 %combine.6 = (bf16[32,24,384]{2,1,0:T(8,128)(2,1)}, bf16[32,24,384]{2,1,0:T(8,128)(2,1)}, bf16[32,24,384]{2,1,0:T(8,128)(2,1)}) custom-call(bf16[8,2,2,2,2,24,384]{6,5,4,3,2,1,0:T(8,128)(2,1)} %bitcast.61, bf16[8,2,2,2,2,24,384]{6,5,4,3,2,1,0:T(8,128)(2,1)} %bitcast.16.refs_1_, bf16[8,2,2,2,24,384]{5,4,3,2,1,0:T(8,128)(2,1)} %bitcast.79, ...), custom_call_target="tpu_custom_call" | custom-call | flops 1048576 | bytes 8388608 | tf_op jit(solution)/shard_map/combine/pallas_call | solution.py:618
  190.0 3.2 %collective-permute-start.11 = (bf16[32,24,384]{2,1,0:T(8,128)(2,1)}, bf16[32,24,384]{2,1,0:T(8,128)(2,1)S(1)}, u32[]{:S(2)}, u32[]{:S(2)}) collective-permute-start(bf16[32,24,384]{2,1,0:T(8,128)(2,1)} %get-tuple-element.171), channel_id=1, source_target_pairs={{0,8},{1,9},{2,10},{3,11},{4,12},{5,13},{6,14},{7,15},{8,0},{9,1},... | collective-permute-start | bytes 1769480 | tf_op jit(solution)/shard_map/ppermute | solution.py:498
  193.2 12.9 %attend_back.5 = (bf16[1024,128]{1,0:T(8,128)(2,1)}, bf16[1024,128]{1,0:T(8,128)(2,1)}, bf16[1024,128]{1,0:T(8,128)(2,1)}, bf16[1,16,24,384]{3,2,1,0:T(8,128)(2,1)}, bf16[1,16,24,384]{3,2,1,0:T(8,128)(2,1)}) custom-call(s32[4]{0:T(128)} %and_select_fusion.last, s32[3]{0:T(128)} %get-tuple-element.256.place, s32[1,1024]{1,0:T(1,128)} %broadcast_select_fusion.seg_ref, ...), custom_call_target="tpu_custom_call" | custom-call | flops 10737418240 | bytes 8388608 | tf_op jit(solution)/shard_map/attend_back/pallas_call | solution.py:211
  208.7 3.5 %combine.7 = (bf16[16,24,384]{2,1,0:T(8,128)(2,1)}, bf16[16,24,384]{2,1,0:T(8,128)(2,1)}, bf16[16,24,384]{2,1,0:T(8,128)(2,1)}, bf16[24,24,384]{2,1,0:T(8,128)(2,1)}) custom-call(bf16[8,2,2,2,2,24,384]{6,5,4,3,2,1,0:T(8,128)(2,1)} %bitcast.62, bf16[8,2,2,2,2,24,384]{6,5,4,3,2,1,0:T(8,128)(2,1)} %bitcast.16.refs_1_, bf16[8,2,2,2,24,384]{5,4,3,2,1,0:T(8,128)(2,1)} %bitcast.80, ...), custom_call_target="tpu_custom_call" | custom-call | flops 1048576 | bytes 8388608 | tf_op jit(solution)/shard_map/combine/pallas_call | solution.py:618
  218.0 7.1 %after.2 = bf16[512,768]{1,0:T(8,128)(2,1)} custom-call(s32[3]{0:T(128)} %get-tuple-element.257.place, bf16[512,768]{1,0:T(8,128)(2,1)} %copy-done.9, f32[1,768]{1,0:T(1,128)} %broadcast_in_dim.17.gain_ref, bf16[1024,768]{1,0:T(8,128)(2,1)} %get-tuple-element.212.gx_ref, bf16[768,2304]{1,0:T(8,128)(2,1)} %w_ref.7, ...), custom_call_target="tpu_custom_call" | custom-call | flops 1811939328 | bytes 16777216 | tf_op jit(solution)/shard_map/after/pallas_call | solution.py:470
  225.1 2.5 collective-permute-done.13
  227.6 2.5 collective-permute-done.14
  231.7 2.8 %combine.8 = (bf16[8,24,384]{2,1,0:T(8,128)(2,1)}, bf16[12,24,384]{2,1,0:T(8,128)(2,1)}, bf16[16,24,384]{2,1,0:T(8,128)(2,1)}, bf16[4,24,384]{2,1,0:T(8,128)(2,1)}) custom-call(bf16[8,2,2,2,2,24,384]{6,5,4,3,2,1,0:T(8,128)(2,1)} %bitcast.63, bf16[8,2,2,2,2,24,384]{6,5,4,3,2,1,0:T(8,128)(2,1)} %bitcast.16.refs_1_, bf16[8,2,2,2,24,384]{5,4,3,2,1,0:T(8,128)(2,1)} %bitcast.81, ...), custom_call_target="tpu_custom_call" | custom-call | flops 1048576 | bytes 8388608 | tf_op jit(solution)/shard_map/combine/pallas_call | solution.py:618
  235.7 2.4 collective-permute-start.21
  238.7 7.1 %after.3 = bf16[512,768]{1,0:T(8,128)(2,1)} custom-call(s32[3]{0:T(128)} %get-tuple-element.256.place, bf16[512,768]{1,0:T(8,128)(2,1)} %get-tuple-element.253.x_ref.x_kept, f32[1,768]{1,0:T(1,128)} %broadcast_in_dim.17.gain_ref, bf16[1024,768]{1,0:T(8,128)(2,1)} %get-tuple-element.212.gx_ref, bf16[768,2304]{1,0:T(8,128)(2,1)} %w_ref.7, ...), custom_call_target="tpu_custom_call" | custom-call | flops 1811939328 | bytes 16777216 | tf_op jit(solution)/shard_map/after/pallas_call | solution.py:470
  248.5 2.8 %combine.9 = (bf16[12,24,384]{2,1,0:T(8,128)(2,1)}, bf16[8,24,384]{2,1,0:T(8,128)(2,1)}, bf16[4,24,384]{2,1,0:T(8,128)(2,1)}) custom-call(bf16[8,2,2,2,2,24,384]{6,5,4,3,2,1,0:T(8,128)(2,1)} %bitcast.53, bf16[8,2,2,2,2,24,384]{6,5,4,3,2,1,0:T(8,128)(2,1)} %bitcast.58, bf16[8,2,2,2,24,384]{5,4,3,2,1,0:T(8,128)(2,1)} %bitcast.77, ...), custom_call_target="tpu_custom_call" | custom-call | flops 1048576 | bytes 8388608 | tf_op jit(solution)/shard_map/combine/pallas_call | solution.py:618
  263.4 2.9 %finish.3 = (f32[24,2304]{1,0:T(8,128)}, f32[24,768]{1,0:T(8,128)}, f32[96,768]{1,0:T(8,128)}, f32[1,24]{1,0:T(1,128)}) custom-call(bf16[4,2,2,2,2,24,384]{6,5,4,3,2,1,0:T(8,128)(2,1)} %bitcast.69, bf16[4,2,2,2,2,24,384]{6,5,4,3,2,1,0:T(8,128)(2,1)} %bitcast.74, bf16[4,2,2,2,24,384]{5,4,3,2,1,0:T(8,128)(2,1)} %bitcast.94, ...), custom_call_target="tpu_custom_call" | custom-call | flops 1048576 | bytes 4194304 | tf_op jit(solution)/shard_map/finish/pallas_call | solution.py:688
  (124 shorter events, 43.7 us)
Async XLA Ops:
  3.2 18.9 %collective-permute-start.1 = (s32[512]{0:T(512)S(1)}, s32[512]{0:T(512)S(1)}, u32[]{:S(2)}, u32[]{:S(2)}) collective-permute-start(s32[512]{0:T(512)S(1)} %bitcast.125), channel_id=1, source_target_pairs={{0,1},{1,0},{2,3},{3,2},{4,5},{5,4},{6,7},{7,6},{8,9},{9,8},{10,11... | collective-permute-start | bytes 6152 | tf_op jit(solution)/shard_map/ppermute | solution.py:481
  6.2 20.5 %collective-permute-start = (bf16[512,768]{1,0:T(8,128)(2,1)S(1)}, bf16[512,768]{1,0:T(8,128)(2,1)S(1)}, u32[]{:S(2)}, u32[]{:S(2)}) collective-permute-start(bf16[512,768]{1,0:T(8,128)(2,1)S(1)} %get-tuple-element.128), channel_id=1, source_target_pairs={{0,1},{1,0},{2,3},{3,2},{4,5},{5,4},{6,7},{7,6},{8,9},{9,8},{10,11... | collective-permute-start | bytes 2359304 | tf_op jit(solution)/shard_map/ppermute | solution.py:481
  7.3 60.5 %collective-permute-start.2 = (bf16[512,768]{1,0:T(8,128)(2,1)S(1)}, bf16[512,768]{1,0:T(8,128)(2,1)S(1)}, u32[]{:S(2)}, u32[]{:S(2)}) collective-permute-start(bf16[512,768]{1,0:T(8,128)(2,1)S(1)} %get-tuple-element.250), channel_id=1, source_target_pairs={{0,1},{1,0},{2,3},{3,2},{4,5},{5,4},{6,7},{7,6},{8,9},{9,8},{10,11... | collective-permute-start | bytes 2359304 | tf_op jit(solution)/shard_map/ppermute | solution.py:481
  115.9 27.9 %collective-permute-start.3 = (bf16[128,24,384]{2,1,0:T(8,128)(2,1)}, bf16[128,24,384]{2,1,0:T(8,128)(2,1)}, u32[]{:S(2)}, u32[]{:S(2)}) collective-permute-start(bf16[128,24,384]{2,1,0:T(8,128)(2,1)} %bitcast.127), channel_id=1, source_target_pairs={{0,2},{1,3},{2,0},{3,1},{4,6},{5,7},{6,4},{7,5},{8,10},{9,11},{10,... | collective-permute-start | bytes 7077896 | tf_op jit(solution)/shard_map/ppermute | solution.py:498
  116.0 27.8 %collective-permute-start.4 = (bf16[128,24,384]{2,1,0:T(8,128)(2,1)}, bf16[128,24,384]{2,1,0:T(8,128)(2,1)S(1)}, u32[]{:S(2)}, u32[]{:S(2)}) collective-permute-start(bf16[128,24,384]{2,1,0:T(8,128)(2,1)} %bitcast.126), channel_id=1, source_target_pairs={{0,2},{1,3},{2,0},{3,1},{4,6},{5,7},{6,4},{7,5},{8,10},{9,11},{10,... | collective-permute-start | bytes 7077896 | tf_op jit(solution)/shard_map/ppermute | solution.py:498
  117.0 26.8 %collective-permute-start.5 = (bf16[512,768]{1,0:T(8,128)(2,1)}, bf16[512,768]{1,0:T(8,128)(2,1)S(1)}, u32[]{:S(2)}, u32[]{:S(2)}) collective-permute-start(bf16[512,768]{1,0:T(8,128)(2,1)} %get-tuple-element.144), channel_id=1, source_target_pairs={{0,1},{1,0},{2,3},{3,2},{4,5},{5,4},{6,7},{7,6},{8,9},{9,8},{10,11... | collective-permute-start | bytes 2359304 | tf_op jit(solution)/shard_map/ppermute | solution.py:481
  148.8 35.0 %collective-permute-start.6 = (bf16[64,24,384]{2,1,0:T(8,128)(2,1)}, bf16[64,24,384]{2,1,0:T(8,128)(2,1)S(1)}, u32[]{:S(2)}, u32[]{:S(2)}) collective-permute-start(bf16[64,24,384]{2,1,0:T(8,128)(2,1)} %get-tuple-element.157), channel_id=1, source_target_pairs={{0,4},{1,5},{2,6},{3,7},{4,0},{5,1},{6,2},{7,3},{8,12},{9,13},{10,... | collective-permute-start | bytes 3538952 | tf_op jit(solution)/shard_map/ppermute | solution.py:498
  148.8 35.0 %collective-permute-start.7 = (bf16[64,24,384]{2,1,0:T(8,128)(2,1)}, bf16[64,24,384]{2,1,0:T(8,128)(2,1)S(1)}, u32[]{:S(2)}, u32[]{:S(2)}) collective-permute-start(bf16[64,24,384]{2,1,0:T(8,128)(2,1)} %get-tuple-element.158), channel_id=1, source_target_pairs={{0,8},{1,9},{2,10},{3,11},{4,12},{5,13},{6,14},{7,15},{8,0},{9,1},... | collective-permute-start | bytes 3538952 | tf_op jit(solution)/shard_map/ppermute | solution.py:498
  151.6 32.3 %collective-permute-start.8 = (bf16[64,24,384]{2,1,0:T(8,128)(2,1)}, bf16[64,24,384]{2,1,0:T(8,128)(2,1)S(1)}, u32[]{:S(2)}, u32[]{:S(2)}) collective-permute-start(bf16[64,24,384]{2,1,0:T(8,128)(2,1)} %bitcast.128), channel_id=1, source_target_pairs={{0,2},{1,3},{2,0},{3,1},{4,6},{5,7},{6,4},{7,5},{8,10},{9,11},{10,... | collective-permute-start | bytes 3538952 | tf_op jit(solution)/shard_map/ppermute | solution.py:498
  189.1 17.0 %collective-permute-start.9 = (bf16[32,24,384]{2,1,0:T(8,128)(2,1)}, bf16[32,24,384]{2,1,0:T(8,128)(2,1)S(1)}, u32[]{:S(2)}, u32[]{:S(2)}) collective-permute-start(bf16[32,24,384]{2,1,0:T(8,128)(2,1)} %get-tuple-element.169), channel_id=1, source_target_pairs={{0,1},{1,0},{2,3},{3,2},{4,5},{5,4},{6,7},{7,6},{8,9},{9,8},{10,11... | collective-permute-start | bytes 1769480 | tf_op jit(solution)/shard_map/ppermute | solution.py:498
  189.1 17.0 %collective-permute-start.10 = (bf16[32,24,384]{2,1,0:T(8,128)(2,1)}, bf16[32,24,384]{2,1,0:T(8,128)(2,1)S(1)}, u32[]{:S(2)}, u32[]{:S(2)}) collective-permute-start(bf16[32,24,384]{2,1,0:T(8,128)(2,1)} %get-tuple-element.170), channel_id=1, source_target_pairs={{0,4},{1,5},{2,6},{3,7},{4,0},{5,1},{6,2},{7,3},{8,12},{9,13},{10,... | collective-permute-start | bytes 1769480 | tf_op jit(solution)/shard_map/ppermute | solution.py:498
  190.0 17.5 %collective-permute-start.11 = (bf16[32,24,384]{2,1,0:T(8,128)(2,1)}, bf16[32,24,384]{2,1,0:T(8,128)(2,1)S(1)}, u32[]{:S(2)}, u32[]{:S(2)}) collective-permute-start(bf16[32,24,384]{2,1,0:T(8,128)(2,1)} %get-tuple-element.171), channel_id=1, source_target_pairs={{0,8},{1,9},{2,10},{3,11},{4,12},{5,13},{6,14},{7,15},{8,0},{9,1},... | collective-permute-start | bytes 1769480 | tf_op jit(solution)/shard_map/ppermute | solution.py:498
  193.2 14.3 %collective-permute-start.12 = (bf16[48,24,384]{2,1,0:T(8,128)(2,1)}, bf16[48,24,384]{2,1,0:T(8,128)(2,1)S(1)}, u32[]{:S(2)}, u32[]{:S(2)}) collective-permute-start(bf16[48,24,384]{2,1,0:T(8,128)(2,1)} %bitcast.129), channel_id=1, source_target_pairs={{0,2},{1,3},{2,0},{3,1},{4,6},{5,7},{6,4},{7,5},{8,10},{9,11},{10,... | collective-permute-start | bytes 2654216 | tf_op jit(solution)/shard_map/ppermute | solution.py:498
  212.1 18.0 %collective-permute-start.16 = (bf16[24,24,384]{2,1,0:T(8,128)(2,1)}, bf16[24,24,384]{2,1,0:T(8,128)(2,1)S(1)}, u32[]{:S(2)}, u32[]{:S(2)}) collective-permute-start(bf16[24,24,384]{2,1,0:T(8,128)(2,1)} %get-tuple-element.188), channel_id=1, source_target_pairs={{0,4},{1,5},{2,6},{3,7},{4,0},{5,1},{6,2},{7,3},{8,12},{9,13},{10,... | collective-permute-start | bytes 1327112 | tf_op jit(solution)/shard_map/ppermute | solution.py:498
  212.1 15.5 %collective-permute-start.13 = (bf16[16,24,384]{2,1,0:T(8,128)(2,1)}, bf16[16,24,384]{2,1,0:T(8,128)(2,1)S(1)}, u32[]{:S(2)}, u32[]{:S(2)}) collective-permute-start(bf16[16,24,384]{2,1,0:T(8,128)(2,1)} %get-tuple-element.185), channel_id=1, source_target_pairs={{0,8},{1,9},{2,10},{3,11},{4,12},{5,13},{6,14},{7,15},{8,0},{9,1},... | collective-permute-start | bytes 884744 | tf_op jit(solution)/shard_map/ppermute | solution.py:498
  214.3 15.9 %collective-permute-start.14 = (bf16[16,24,384]{2,1,0:T(8,128)(2,1)}, bf16[16,24,384]{2,1,0:T(8,128)(2,1)S(1)}, u32[]{:S(2)}, u32[]{:S(2)}) collective-permute-start(bf16[16,24,384]{2,1,0:T(8,128)(2,1)} %get-tuple-element.186), channel_id=1, source_target_pairs={{0,16},{1,17},{2,18},{3,19},{4,20},{5,21},{6,22},{7,23},{8,24},{9,... | collective-permute-start | bytes 884744 | tf_op jit(solution)/shard_map/ppermute | solution.py:498
  216.5 13.6 %collective-permute-start.15 = (bf16[16,24,384]{2,1,0:T(8,128)(2,1)}, bf16[16,24,384]{2,1,0:T(8,128)(2,1)S(1)}, u32[]{:S(2)}, u32[]{:S(2)}) collective-permute-start(bf16[16,24,384]{2,1,0:T(8,128)(2,1)} %get-tuple-element.187), channel_id=1, source_target_pairs={{0,1},{1,0},{2,3},{3,2},{4,5},{5,4},{6,7},{7,6},{8,9},{9,8},{10,11... | collective-permute-start | bytes 884744 | tf_op jit(solution)/shard_map/ppermute | solution.py:498
  218.0 12.1 %collective-permute-start.17 = (bf16[16,24,384]{2,1,0:T(8,128)(2,1)S(1)}, bf16[16,24,384]{2,1,0:T(8,128)(2,1)S(1)}, u32[]{:S(2)}, u32[]{:S(2)}) collective-permute-start(bf16[16,24,384]{2,1,0:T(8,128)(2,1)S(1)} %bitcast.130), channel_id=1, source_target_pairs={{0,2},{1,3},{2,0},{3,1},{4,6},{5,7},{6,4},{7,5},{8,10},{9,11},{10,... | collective-permute-start | bytes 884744 | tf_op jit(solution)/shard_map/ppermute | solution.py:498
  230.2 29.3 %collective-permute-start.25 = (bf16[512,768]{1,0:T(8,128)(2,1)}, bf16[512,768]{1,0:T(8,128)(2,1)S(1)}, u32[]{:S(2)}, u32[]{:S(2)}) collective-permute-start(bf16[512,768]{1,0:T(8,128)(2,1)} %after.2), channel_id=1, source_target_pairs={{0,1},{1,0},{2,3},{3,2},{4,5},{5,4},{6,7},{7,6},{8,9},{9,8},{10,11... | collective-permute-start | bytes 2359304 | tf_op jit(solution)/shard_map/ppermute | solution.py:481
  234.5 13.1 %collective-permute-start.20 = (bf16[16,24,384]{2,1,0:T(8,128)(2,1)}, bf16[16,24,384]{2,1,0:T(8,128)(2,1)S(1)}, u32[]{:S(2)}, u32[]{:S(2)}) collective-permute-start(bf16[16,24,384]{2,1,0:T(8,128)(2,1)} %get-tuple-element.210), channel_id=1, source_target_pairs={{0,8},{1,9},{2,10},{3,11},{4,12},{5,13},{6,14},{7,15},{8,0},{9,1},... | collective-permute-start | bytes 884744 | tf_op jit(solution)/shard_map/ppermute | solution.py:498
  234.6 13.0 %collective-permute-start.19 = (bf16[12,24,384]{2,1,0:T(8,128)(2,1)}, bf16[12,24,384]{2,1,0:T(8,128)(2,1)S(1)}, u32[]{:S(2)}, u32[]{:S(2)}) collective-permute-start(bf16[12,24,384]{2,1,0:T(8,128)(2,1)} %get-tuple-element.209), channel_id=1, source_target_pairs={{0,4},{1,5},{2,6},{3,7},{4,0},{5,1},{6,2},{7,3},{8,12},{9,13},{10,... | collective-permute-start | bytes 663560 | tf_op jit(solution)/shard_map/ppermute | solution.py:498
  235.7 11.9 %collective-permute-start.21 = (bf16[4,24,384]{2,1,0:T(8,128)(2,1)}, bf16[4,24,384]{2,1,0:T(8,128)(2,1)S(1)}, u32[]{:S(2)}, u32[]{:S(2)}) collective-permute-start(bf16[4,24,384]{2,1,0:T(8,128)(2,1)} %get-tuple-element.211), channel_id=1, source_target_pairs={{0,12},{1,13},{2,14},{3,15},{4,8},{5,9},{6,10},{7,11},{8,4},{9,5},... | collective-permute-start | bytes 221192 | tf_op jit(solution)/shard_map/ppermute | solution.py:498
  251.3 9.8 %collective-permute-start.24 = (bf16[4,24,384]{2,1,0:T(8,128)(2,1)}, bf16[4,24,384]{2,1,0:T(8,128)(2,1)S(1)}, u32[]{:S(2)}, u32[]{:S(2)}) collective-permute-start(bf16[4,24,384]{2,1,0:T(8,128)(2,1)} %get-tuple-element.225), channel_id=1, source_target_pairs={{0,17},{1,16},{2,19},{3,18},{4,21},{5,20},{6,23},{7,22},{8,25},{9,... | collective-permute-start | bytes 221192 | tf_op jit(solution)/shard_map/ppermute | solution.py:498
  252.6 10.0 %collective-permute-start.23 = (bf16[8,24,384]{2,1,0:T(8,128)(2,1)}, bf16[8,24,384]{2,1,0:T(8,128)(2,1)S(1)}, u32[]{:S(2)}, u32[]{:S(2)}) collective-permute-start(bf16[8,24,384]{2,1,0:T(8,128)(2,1)} %get-tuple-element.224), channel_id=1, source_target_pairs={{0,16},{1,17},{2,18},{3,19},{4,20},{5,21},{6,22},{7,23},{8,24},{9,... | collective-permute-start | bytes 442376 | tf_op jit(solution)/shard_map/ppermute | solution.py:498
  (33 other events, 103.8 us)
